TPU v7x, 32 devices: a whole 2x2x4 slice. The times are simulated.
32 devices in a mesh: gx: 8 (over z, x), gy: 4 (over y, core).
Axes of the slice: x: 2, y: 2, z: 4, core: 2. Of those that a mesh axis runs over, the one named last changes fastest.
Arguments:
- order_params: float32 [24, 12, 64, 512], P(None, None, 'gx', 'gy'), may hold values from 0 to 1, as said below
- grain_ids: int32 [8, 4, 24], P('gx', 'gy'), may hold values from -1 to 1151, as said below
- channel_maps: int32 [8, 4, 4, 24], P('gx', 'gy'), may hold values from -1 to 23, as said below
- zplanes: int32 [2, 64, 512], P(None, 'gx', 'gy'), may hold values from 0 to 1151, as said below
Outputs:
- evolved: float32 [24, 12, 64, 512], P(None, None, 'gx', 'gy')
Inputs may be any that keep to these rules, and one draw needn't show every extreme that they name: `order_params`: zero in every slot whose grain id is -1. `grain_ids`: grain ids are distinct within a block; -1 marks an empty slot. `channel_maps`: A non-negative entry for face f of a block names the adjacent block's slot with the same grain; the entries for face f of a block and for the opposite face of the adjacent block are inverse one-to-one matchings. At most 6 slots of a block have an entry for any one face, and in every draw some face of some block has exactly 6. A slot has an entry for at most one face. `zplanes`: each cell names one of the non-negative grain ids of its block.
All inputs are finite; a program needn't handle non-finite values.
Results may differ from a plain program's by a relative error of at most 0.00018.
Values sent between devices are 32-bit elements; how exact they have to be, the bound alone decides.
No kernel may reach another device: no remote copies, remote signals or barrier semaphores. Data moves between devices by JAX's collectives and lax.ppermute only.
A program may use at most 64 MiB of HBM per device.

v0:
```python
import jax
import jax.numpy as jnp
from jax import lax
from jax.sharding import PartitionSpec as P

STEPS = 3


time_step = 0.05
mobility = 1.0
alpha_coef = 1.0
beta_coef = 1.0
gamma_coef = 1.5
kappa_coef = 2.0


def shifted(block, axis, distance):
    devices = range(lax.axis_size(axis))
    route = [((i - distance) % len(devices), i) for i in devices]
    return lax.ppermute(block, axis, route)


def reorder(rim, partner):
    count = rim.shape[0]
    select = (partner[:, None] == jnp.arange(count, dtype=jnp.int32)[None, :]).astype(jnp.float32)
    return jnp.einsum("st,tzc->szc", select, rim, precision=lax.Precision.HIGHEST)


def advance(field, lower_x, upper_x, lower_y, upper_y, frozen):
    depth, rows, cols = (field.shape[1], field.shape[2], field.shape[3])
    row_index = lax.broadcasted_iota(jnp.int32, (1, 1, rows, 1), 2)
    col_index = lax.broadcasted_iota(jnp.int32, (1, 1, 1, cols), 3)
    layer_index = lax.broadcasted_iota(jnp.int32, (1, depth, 1, 1), 1)
    above_x = jnp.where(row_index == rows - 1, upper_x[:, :, None, :], jnp.roll(field, -1, axis=2))
    below_x = jnp.where(row_index == 0, lower_x[:, :, None, :], jnp.roll(field, 1, axis=2))
    above_y = jnp.where(col_index == cols - 1, upper_y[..., None], jnp.roll(field, -1, axis=3))
    below_y = jnp.where(col_index == 0, lower_y[..., None], jnp.roll(field, 1, axis=3))
    above_z = jnp.where(layer_index == depth - 1, frozen[1][:, None], jnp.roll(field, -1, axis=1))
    below_z = jnp.where(layer_index == 0, frozen[0][:, None], jnp.roll(field, 1, axis=1))
    laplace = above_x + below_x + above_y + below_y + above_z + below_z - 6.0 * field
    total = jnp.sum(field * field, axis=0, keepdims=True)
    rate = (
        -alpha_coef * field
        + beta_coef * field**3
        + 2.0 * gamma_coef * field * (total - field * field)
        - kappa_coef * laplace
    )
    return field - time_step * mobility * rate


def on_device(order_params, grain_ids, channel_maps, zplanes):
    slot_grains = grain_ids[0, 0]
    face_maps = channel_maps[0, 0]
    matches = zplanes[:, None, :, :] == slot_grains[None, :, None, None]
    frozen = (matches & (slot_grains[None, :, None, None] >= 0)).astype(jnp.float32)
    field = order_params
    for repeat_index in range(STEPS):
        lower_x = reorder(shifted(field[:, :, -1, :], "gx", 1), face_maps[0])
        upper_x = reorder(shifted(field[:, :, 0, :], "gx", -1), face_maps[1])
        lower_y = reorder(shifted(field[:, :, :, -1], "gy", 1), face_maps[2])
        upper_y = reorder(shifted(field[:, :, :, 0], "gy", -1), face_maps[3])
        field = advance(field, lower_x, upper_x, lower_y, upper_y, frozen)
    return field


def solution(mesh):
    in_specs = (
        P(None, None, "gx", "gy"),
        P("gx", "gy", None),
        P("gx", "gy", None, None),
        P(None, "gx", "gy"),
    )
    out_specs = P(None, None, "gx", "gy")
    return jax.shard_map(
        on_device, mesh=mesh, in_specs=in_specs, out_specs=out_specs, check_vma=False
    )
```

profile of v0, /device:TPU:0, one launch (start us, length us, event | category | flops | bytes accessed | tf_op | source)
XLA Modules:
  0.0 84.1 jit_solution(9295400047081995666)
XLA Ops:
  0.0 2.1 %copy.45 = f32[24,12,8,128]{3,0,1,2:T(8,128)S(1)} copy(f32[24,12,8,128]{3,2,1,0:T(8,128)} %param.4) | data formatting | bytes 2359296 | tf_op args[0]
  2.1 0.9 %slice_bitcast_fusion.11 = (f32[24,12,128]{2,0,1:T(8,128)}, f32[24,12,1,128]{3,0,1,2:T(8,128)}, f32[24,12,1,128]{3,0,1,2:T(8,128)}, f32[24,12,128]{2,0,1:T(8,128)}) fusion(f32[24,12,8,128]{3,0,1,2:T(8,128)S(1)} %copy.45), kind=kLoop, calls=%fused_computation.117 | loop fusion | bytes 884736 | tf_op jit(solution)/shard_map/squeeze | solution.py:59
  2.9 6.0 %collective-permute-start = (f32[24,12,128]{2,0,1:T(8,128)}, f32[24,12,128]{2,0,1:T(8,128)}, u32[]{:S(2)}, u32[]{:S(2)}) collective-permute-start(f32[24,12,128]{2,0,1:T(8,128)} %get-tuple-element.33), channel_id=1, source_target_pairs={{4,0},{8,4},{12,8},{16,12},{20,16},{24,20},{28,24},{0,28},{5,1},{9... | collective-permute-start | bytes 442376 | tf_op jit(solution)/shard_map/ppermute | solution.py:20
  8.9 0.0 collective-permute-start.1
  8.9 1.4 %fusion.98 = (f32[24,12,8,1]{3,2,1,0:T(8,128)}, f32[24,12,8,1]{3,2,1,0:T(8,128)S(1)}) fusion(f32[24,12,8,128]{3,2,1,0:T(8,128)S(1)} %copy-done), kind=kLoop, calls=%fused_computation.131 | loop fusion | bytes 36864 | tf_op jit(solution)/shard_map/slice | solution.py:60
  10.3 1.5 %copy.59 = f32[24,12,8,1]{0,1,2,3:T(8,128)} copy(f32[24,12,8,1]{3,2,1,0:T(8,128)S(1)} %get-tuple-element.42) | data formatting | bytes 18432
  11.9 0.7 collective-permute-start.2
  12.6 2.7 %copy.60 = f32[24,12,8,1]{0,1,2,3:T(8,128)} copy(f32[24,12,8,1]{3,2,1,0:T(8,128)} %get-tuple-element.41) | data formatting | bytes 18432
  15.4 0.2 fusion.100
  15.6 0.1 fusion.97
  15.7 0.0 copy-start.9
  15.7 0.0 copy-start.8
  15.7 0.0 copy-start.7
  15.8 0.0 copy-start.1
  15.8 0.4 fusion.99
  16.2 0.2 copy-done.9
  16.4 0.0 copy-done.8
  16.4 0.0 copy-done.7
  16.5 0.1 and_convert_fusion
  16.6 0.4 copy-done.1
  17.0 0.7 copy.39
  17.8 0.7 copy.36
  18.5 1.1 %fusion.64 = f32[24,12,8]{0,1,2:T(8,128)S(1)} fusion(f32[24,12,8]{0,1,2:T(8,128)} %collective-permute-done.2, s32[24]{0:T(128)S(1)} %get-tuple-element.52), kind=kOutput, calls=%fused_computation.84 | convolution fusion | flops 664128 | bytes 18528 | tf_op jit(solution)/shard_map/st,tzc->szc/dot_general | solution.py:26
  19.5 0.2 fusion.71
  19.8 1.2 %fusion.50 = f32[24,12,128]{2,0,1:T(8,128)S(1)} fusion(f32[24,12,128]{2,0,1:T(8,128)} %collective-permute-done, s32[24]{0:T(128)S(1)} %get-tuple-element.49), kind=kOutput, calls=%fused_computation.76 | convolution fusion | flops 10617408 | bytes 295008 | tf_op jit(solution)/shard_map/st,tzc->szc/dot_general | solution.py:26
  21.0 1.2 %fusion.57 = f32[24,12,128]{2,0,1:T(8,128)S(1)} fusion(f32[24,12,128]{2,0,1:T(8,128)} %collective-permute-done.1, s32[24]{0:T(128)S(1)} %get-tuple-element.50), kind=kOutput, calls=%fused_computation.80 | convolution fusion | flops 10617408 | bytes 295008 | tf_op jit(solution)/shard_map/st,tzc->szc/dot_general | solution.py:26
  22.3 4.8 %fusion.20 = f32[24,12,8,128]{3,0,1,2:T(8,128)S(1)} fusion(f32[24,12,1,128]{3,0,1,2:T(8,128)S(1)} %copy-done.4, f32[24,12,7,128]{3,0,1,2:T(8,128)S(1)} %get-tuple-element.46, f32[24,12,7,128]{3,0,1,2:T(8,128)S(1)} %get-tuple-element.45, f32[24,12,1,128]{3,0,1,2:T(8,128)S(1)} %copy-done.3, f32[24,12,8,1]{3,0,1,2:T(8,128)S(1)} %copy.36, ...), kind=kOutput, calls=%fused_computation.20 | output fusion | flops 9154583 | bytes 9947432 | tf_op jit(solution)/shard_map/sub | solution.py:45
  27.1 0.8 slice_bitcast_fusion.9
  27.9 1.6 %fusion.95 = (f32[24,12,7,128]{3,0,1,2:T(8,128)}, f32[24,12,7,128]{3,0,1,2:T(8,128)}) fusion(f32[24,12,8,128]{3,0,1,2:T(8,128)S(1)} %fusion.20), kind=kLoop, calls=%fused_computation.128 | loop fusion | bytes 4128768 | tf_op jit(solution)/shard_map/jit(_roll_static)/slice | solution.py:35
  29.5 1.5 %fusion.92 = (f32[24,11,8,128]{3,0,1,2:T(8,128)}, f32[24,11,8,128]{3,0,1,2:T(8,128)}) fusion(f32[24,12,8,128]{3,0,1,2:T(8,128)S(1)} %fusion.20), kind=kLoop, calls=%fused_computation.125 | loop fusion | bytes 4325376 | tf_op jit(solution)/shard_map/jit(_roll_static)/slice | solution.py:39
  31.0 1.8 %fusion.94 = (f32[24,12,8,127]{3,0,1,2:T(8,128)}, f32[24,12,8,127]{3,0,1,2:T(8,128)}) fusion(f32[24,12,8,128]{3,0,1,2:T(8,128)S(1)} %fusion.20), kind=kLoop, calls=%fused_computation.127 | loop fusion | bytes 4681728 | tf_op jit(solution)/shard_map/jit(_roll_static)/slice | solution.py:37
  32.8 0.4 fusion.93
  33.2 0.0 copy-start.2
  33.2 1.4 %copy.55 = f32[24,12,8,1]{0,1,2,3:T(8,128)} copy(f32[24,12,8,1]{3,0,1,2:T(8,128)S(1)} %get-tuple-element.28) | data formatting | bytes 18432 | tf_op jit(solution)/shard_map/squeeze | solution.py:61
  34.7 1.7 %collective-permute-start.6 = (f32[24,12,8]{0,1,2:T(8,128)}, f32[24,12,8]{0,1,2:T(8,128)}, u32[]{:S(2)}, u32[]{:S(2)}) collective-permute-start(f32[24,12,8]{0,1,2:T(8,128)} %bitcast.70), channel_id=1, source_target_pairs={{1,0},{2,1},{3,2},{0,3},{5,4},{6,5},{7,6},{4,7},{9,8},{10,9},{11,1... | collective-permute-start | bytes 27656 | tf_op jit(solution)/shard_map/ppermute | solution.py:20
  36.4 0.7 fusion.91
  37.1 4.4 %collective-permute-start.4 = (f32[24,12,128]{2,0,1:T(8,128)}, f32[24,12,128]{2,0,1:T(8,128)}, u32[]{:S(2)}, u32[]{:S(2)}) collective-permute-start(f32[24,12,128]{2,0,1:T(8,128)} %get-tuple-element.19), channel_id=1, source_target_pairs={{4,0},{8,4},{12,8},{16,12},{20,16},{24,20},{28,24},{0,28},{5,1},{9... | collective-permute-start | bytes 442376 | tf_op jit(solution)/shard_map/ppermute | solution.py:20
  41.6 0.0 collective-permute-start.5
  41.6 1.4 %copy.56 = f32[24,12,8,1]{0,1,2,3:T(8,128)} copy(f32[24,12,8,1]{3,0,1,2:T(8,128)S(1)} %get-tuple-element.27) | data formatting | bytes 18432 | tf_op jit(solution)/shard_map/squeeze | solution.py:60
  43.0 1.1 %fusion.62 = f32[24,12,8]{0,1,2:T(8,128)S(1)} fusion(f32[24,12,8]{0,1,2:T(8,128)} %collective-permute-done.6, s32[24]{0:T(128)S(1)} %get-tuple-element.52), kind=kOutput, calls=%fused_computation.83 | convolution fusion | flops 664128 | bytes 18528 | tf_op jit(solution)/shard_map/st,tzc->szc/dot_general | solution.py:26
  44.1 2.8 %collective-permute-done.7 = f32[24,12,8]{0,1,2:T(8,128)S(1)} collective-permute-done((f32[24,12,8]{0,1,2:T(8,128)}, f32[24,12,8]{0,1,2:T(8,128)S(1)}, u32[]{:S(2)}, u32[]{:S(2)}) %collective-permute-start.7) | collective-permute-done | bytes 9248 | tf_op jit(solution)/shard_map/ppermute | solution.py:20
  46.9 0.2 fusion.69
  47.1 1.2 %fusion.48 = f32[24,12,128]{2,0,1:T(8,128)S(1)} fusion(f32[24,12,128]{2,0,1:T(8,128)} %collective-permute-done.4, s32[24]{0:T(128)S(1)} %get-tuple-element.49), kind=kOutput, calls=%fused_computation.75 | convolution fusion | flops 10617408 | bytes 295008 | tf_op jit(solution)/shard_map/st,tzc->szc/dot_general | solution.py:26
  48.3 1.4 %collective-permute-done.5 = f32[24,12,128]{2,0,1:T(8,128)} collective-permute-done((f32[24,12,128]{2,0,1:T(8,128)}, f32[24,12,128]{2,0,1:T(8,128)}, u32[]{:S(2)}, u32[]{:S(2)}) %collective-permute-start.5) | collective-permute-done | bytes 147488 | tf_op jit(solution)/shard_map/ppermute | solution.py:20
  49.7 1.2 %fusion.55 = f32[24,12,128]{2,0,1:T(8,128)S(1)} fusion(f32[24,12,128]{2,0,1:T(8,128)} %collective-permute-done.5, s32[24]{0:T(128)S(1)} %get-tuple-element.50), kind=kOutput, calls=%fused_computation.79 | convolution fusion | flops 10617408 | bytes 295008 | tf_op jit(solution)/shard_map/st,tzc->szc/dot_general | solution.py:26
  50.9 5.0 %fusion.15 = f32[24,12,8,128]{3,0,1,2:T(8,128)S(1)} fusion(f32[24,12,8,128]{3,0,1,2:T(8,128)S(1)} %fusion.20, f32[24,12,1,128]{3,0,1,2:T(8,128)} %get-tuple-element.22, f32[24,12,7,128]{3,0,1,2:T(8,128)} %get-tuple-element.32, f32[24,12,7,128]{3,0,1,2:T(8,128)} %get-tuple-element.31, f32[24,12,1,128]{3,0,1,2:T(8,128)} %get-tuple-element.21, ...), kind=kOutput, calls=%fused_computation.15 | output fusion | flops 9154583 | bytes 9947432 | tf_op jit(solution)/shard_map/sub | solution.py:45
  55.9 0.9 %slice_bitcast_fusion.7 = (f32[24,12,128]{2,0,1:T(8,128)}, f32[24,12,128]{2,0,1:T(8,128)}, f32[24,12,1,128]{3,0,1,2:T(8,128)}, f32[24,12,1,128]{3,0,1,2:T(8,128)}) fusion(f32[24,12,8,128]{3,0,1,2:T(8,128)S(1)} %fusion.15), kind=kLoop, calls=%fused_computation.113 | loop fusion | bytes 884736 | tf_op jit(solution)/shard_map/squeeze | solution.py:59
  56.8 1.5 %fusion.90 = (f32[24,12,7,128]{3,0,1,2:T(8,128)}, f32[24,12,7,128]{3,0,1,2:T(8,128)}) fusion(f32[24,12,8,128]{3,0,1,2:T(8,128)S(1)} %fusion.15), kind=kLoop, calls=%fused_computation.123 | loop fusion | bytes 4128768 | tf_op jit(solution)/shard_map/jit(_roll_static)/slice | solution.py:35
  58.3 1.5 %fusion.87 = (f32[24,11,8,128]{3,0,1,2:T(8,128)}, f32[24,11,8,128]{3,0,1,2:T(8,128)}) fusion(f32[24,12,8,128]{3,0,1,2:T(8,128)S(1)} %fusion.15), kind=kLoop, calls=%fused_computation.120 | loop fusion | bytes 4325376 | tf_op jit(solution)/shard_map/jit(_roll_static)/slice | solution.py:39
  59.8 1.8 %fusion.89 = (f32[24,12,8,127]{3,0,1,2:T(8,128)}, f32[24,12,8,127]{3,0,1,2:T(8,128)}) fusion(f32[24,12,8,128]{3,0,1,2:T(8,128)S(1)} %fusion.15), kind=kLoop, calls=%fused_computation.122 | loop fusion | bytes 4681728 | tf_op jit(solution)/shard_map/jit(_roll_static)/slice | solution.py:37
  61.6 0.4 fusion.88
  62.0 1.4 %copy.57 = f32[24,12,8,1]{0,1,2,3:T(8,128)} copy(f32[24,12,8,1]{3,0,1,2:T(8,128)S(1)} %get-tuple-element.14) | data formatting | bytes 18432 | tf_op jit(solution)/shard_map/squeeze | solution.py:61
  63.4 0.7 fusion.86
  64.1 3.3 %collective-permute-start.8 = (f32[24,12,128]{2,0,1:T(8,128)}, f32[24,12,128]{2,0,1:T(8,128)}, u32[]{:S(2)}, u32[]{:S(2)}) collective-permute-start(f32[24,12,128]{2,0,1:T(8,128)} %get-tuple-element.5), channel_id=1, source_target_pairs={{4,0},{8,4},{12,8},{16,12},{20,16},{24,20},{28,24},{0,28},{5,1},{9... | collective-permute-start | bytes 442376 | tf_op jit(solution)/shard_map/ppermute | solution.py:20
  67.4 1.4 %copy.58 = f32[24,12,8,1]{0,1,2,3:T(8,128)} copy(f32[24,12,8,1]{3,0,1,2:T(8,128)S(1)} %get-tuple-element.13) | data formatting | bytes 18432 | tf_op jit(solution)/shard_map/squeeze | solution.py:60
  68.9 0.2 collective-permute-start.11
  69.1 1.1 %fusion.60 = f32[24,12,8]{0,1,2:T(8,128)S(1)} fusion(f32[24,12,8]{0,1,2:T(8,128)} %collective-permute-done.10, s32[24]{0:T(128)S(1)} %get-tuple-element.52), kind=kOutput, calls=%fused_computation.82 | convolution fusion | flops 664128 | bytes 18528 | tf_op jit(solution)/shard_map/st,tzc->szc/dot_general | solution.py:26
  70.2 2.6 %collective-permute-done.11 = f32[24,12,8]{0,1,2:T(8,128)S(1)} collective-permute-done((f32[24,12,8]{0,1,2:T(8,128)}, f32[24,12,8]{0,1,2:T(8,128)S(1)}, u32[]{:S(2)}, u32[]{:S(2)}) %collective-permute-start.11) | collective-permute-done | bytes 9248 | tf_op jit(solution)/shard_map/ppermute | solution.py:20
  72.8 0.2 fusion.67
  73.0 1.2 %fusion.46 = f32[24,12,128]{2,0,1:T(8,128)S(1)} fusion(f32[24,12,128]{2,0,1:T(8,128)} %collective-permute-done.8, s32[24]{0:T(128)S(1)} %get-tuple-element.49), kind=kOutput, calls=%fused_computation.74 | convolution fusion | flops 10617408 | bytes 295008 | tf_op jit(solution)/shard_map/st,tzc->szc/dot_general | solution.py:26
  74.2 2.2 %collective-permute-done.9 = f32[24,12,128]{2,0,1:T(8,128)} collective-permute-done((f32[24,12,128]{2,0,1:T(8,128)}, f32[24,12,128]{2,0,1:T(8,128)}, u32[]{:S(2)}, u32[]{:S(2)}) %collective-permute-start.9) | collective-permute-done | bytes 147488 | tf_op jit(solution)/shard_map/ppermute | solution.py:20
  76.4 1.2 %fusion.53 = f32[24,12,128]{2,0,1:T(8,128)S(1)} fusion(f32[24,12,128]{2,0,1:T(8,128)} %collective-permute-done.9, s32[24]{0:T(128)S(1)} %get-tuple-element.50), kind=kOutput, calls=%fused_computation.78 | convolution fusion | flops 10617408 | bytes 295008 | tf_op jit(solution)/shard_map/st,tzc->szc/dot_general | solution.py:26
  77.6 4.7 %fusion.10 = f32[24,12,8,128]{3,0,1,2:T(8,128)S(1)} fusion(f32[24,12,8,128]{3,0,1,2:T(8,128)S(1)} %fusion.15, f32[24,12,1,128]{3,0,1,2:T(8,128)} %get-tuple-element.8, f32[24,12,7,128]{3,0,1,2:T(8,128)} %get-tuple-element.18, f32[24,12,7,128]{3,0,1,2:T(8,128)} %get-tuple-element.17, f32[24,12,1,128]{3,0,1,2:T(8,128)} %get-tuple-element.7, ...), kind=kOutput, calls=%fused_computation.10 | output fusion | flops 9154583 | bytes 9947432 | tf_op jit(solution)/shard_map/sub | solution.py:45
  82.4 1.7 %copy.54 = f32[24,12,8,128]{3,2,1,0:T(8,128)} copy(f32[24,12,8,128]{3,0,1,2:T(8,128)S(1)} %fusion.10) | data formatting | bytes 2359296 | tf_op jit(solution)/shard_map/sub | solution.py:48
  (42 shorter events, 0.1 us)
Async XLA Ops:
  0.0 8.9 %copy-start = (f32[24,12,8,128]{3,2,1,0:T(8,128)S(1)}, f32[24,12,8,128]{3,2,1,0:T(8,128)}, u32[]{:S(2)}) copy-start(f32[24,12,8,128]{3,2,1,0:T(8,128)} %param.4) | copy-start | bytes 3538948
  2.9 16.9 %collective-permute-start = (f32[24,12,128]{2,0,1:T(8,128)}, f32[24,12,128]{2,0,1:T(8,128)}, u32[]{:S(2)}, u32[]{:S(2)}) collective-permute-start(f32[24,12,128]{2,0,1:T(8,128)} %get-tuple-element.33), channel_id=1, source_target_pairs={{4,0},{8,4},{12,8},{16,12},{20,16},{24,20},{28,24},{0,28},{5,1},{9... | collective-permute-start | bytes 442376 | tf_op jit(solution)/shard_map/ppermute | solution.py:20
  8.9 12.1 %collective-permute-start.1 = (f32[24,12,128]{2,0,1:T(8,128)}, f32[24,12,128]{2,0,1:T(8,128)}, u32[]{:S(2)}, u32[]{:S(2)}) collective-permute-start(f32[24,12,128]{2,0,1:T(8,128)} %get-tuple-element.36), channel_id=1, source_target_pairs={{28,0},{0,4},{4,8},{8,12},{12,16},{16,20},{20,24},{24,28},{29,1},{... | collective-permute-start | bytes 442376 | tf_op jit(solution)/shard_map/ppermute | solution.py:20
  11.9 6.6 %collective-permute-start.2 = (f32[24,12,8]{0,1,2:T(8,128)}, f32[24,12,8]{0,1,2:T(8,128)}, u32[]{:S(2)}, u32[]{:S(2)}) collective-permute-start(f32[24,12,8]{0,1,2:T(8,128)} %bitcast.68), channel_id=1, source_target_pairs={{1,0},{2,1},{3,2},{0,3},{5,4},{6,5},{7,6},{4,7},{9,8},{10,9},{11,1... | collective-permute-start | bytes 27656 | tf_op jit(solution)/shard_map/ppermute | solution.py:20
  15.3 4.2 %collective-permute-start.3 = (f32[24,12,8]{0,1,2:T(8,128)}, f32[24,12,8]{0,1,2:T(8,128)S(1)}, u32[]{:S(2)}, u32[]{:S(2)}) collective-permute-start(f32[24,12,8]{0,1,2:T(8,128)} %bitcast.69), channel_id=1, source_target_pairs={{3,0},{0,1},{1,2},{2,3},{7,4},{4,5},{5,6},{6,7},{11,8},{8,9},{9,10... | collective-permute-start | bytes 27656 | tf_op jit(solution)/shard_map/ppermute | solution.py:20
  15.3 6.9 %copy-start.10 = (pred[8]{0:T(512)(128)(4,1)}, pred[8]{0:T(512)(128)(4,1)S(1)}, u32[]{:S(2)}) copy-start(pred[8]{0:T(512)(128)(4,1)S(1)} %get-tuple-element.57) | copy-start | bytes 28
  15.3 6.9 %copy-start.11 = (pred[8]{0:T(512)(128)(4,1)}, pred[8]{0:T(512)(128)(4,1)S(1)}, u32[]{:S(2)}) copy-start(pred[8]{0:T(512)(128)(4,1)S(1)} %get-tuple-element.58) | copy-start | bytes 28
  15.3 6.8 %copy-start.12 = (pred[128]{0:T(512)(128)(4,1)}, pred[128]{0:T(512)(128)(4,1)S(1)}, u32[]{:S(2)}) copy-start(pred[128]{0:T(512)(128)(4,1)S(1)} %get-tuple-element.55) | copy-start | bytes 388
  15.3 6.8 %copy-start.13 = (pred[128]{0:T(512)(128)(4,1)}, pred[128]{0:T(512)(128)(4,1)S(1)}, u32[]{:S(2)}) copy-start(pred[128]{0:T(512)(128)(4,1)S(1)} %get-tuple-element.56) | copy-start | bytes 388
  15.7 0.7 copy-start.9
  15.7 0.7 copy-start.8
  15.7 0.7 copy-start.7
  15.8 1.3 %copy-start.1 = (f32[24,12,8,1]{3,2,1,0:T(8,128)S(1)}, f32[24,12,8,1]{3,2,1,0:T(8,128)}, u32[]{:S(2)}) copy-start(f32[24,12,8,1]{3,2,1,0:T(8,128)} %get-tuple-element.41) | copy-start | bytes 27652
  16.6 5.6 %copy-start.5 = (f32[24,8,128]{2,0,1:T(8,128)}, f32[24,8,128]{2,0,1:T(8,128)S(1)}, u32[]{:S(2)}) copy-start(f32[24,8,128]{2,0,1:T(8,128)S(1)} %get-tuple-element.47) | copy-start | bytes 294916
  16.6 5.6 %copy-start.6 = (f32[24,8,128]{2,0,1:T(8,128)}, f32[24,8,128]{2,0,1:T(8,128)S(1)}, u32[]{:S(2)}) copy-start(f32[24,8,128]{2,0,1:T(8,128)S(1)} %get-tuple-element.48) | copy-start | bytes 294916
  17.0 5.2 %copy-start.14 = (pred[12]{0:T(512)(128)(4,1)}, pred[12]{0:T(512)(128)(4,1)S(1)}, u32[]{:S(2)}) copy-start(pred[12]{0:T(512)(128)(4,1)S(1)} %get-tuple-element.53) | copy-start | bytes 40
  17.0 5.2 %copy-start.15 = (pred[12]{0:T(512)(128)(4,1)}, pred[12]{0:T(512)(128)(4,1)S(1)}, u32[]{:S(2)}) copy-start(pred[12]{0:T(512)(128)(4,1)S(1)} %get-tuple-element.54) | copy-start | bytes 40
  17.7 4.5 %copy-start.3 = (f32[24,12,1,128]{3,0,1,2:T(8,128)S(1)}, f32[24,12,1,128]{3,0,1,2:T(8,128)}, u32[]{:S(2)}) copy-start(f32[24,12,1,128]{3,0,1,2:T(8,128)} %get-tuple-element.34) | copy-start | bytes 442372
  17.7 4.5 %copy-start.4 = (f32[24,12,1,128]{3,0,1,2:T(8,128)S(1)}, f32[24,12,1,128]{3,0,1,2:T(8,128)}, u32[]{:S(2)}) copy-start(f32[24,12,1,128]{3,0,1,2:T(8,128)} %get-tuple-element.35) | copy-start | bytes 442372
  33.2 9.8 %copy-start.2 = (f32[24,12,8,1]{3,0,1,2:T(8,128)}, f32[24,12,8,1]{3,0,1,2:T(8,128)S(1)}, u32[]{:S(2)}) copy-start(f32[24,12,8,1]{3,0,1,2:T(8,128)S(1)} %get-tuple-element.28) | copy-start | bytes 27652
  34.7 8.3 %collective-permute-start.6 = (f32[24,12,8]{0,1,2:T(8,128)}, f32[24,12,8]{0,1,2:T(8,128)}, u32[]{:S(2)}, u32[]{:S(2)}) collective-permute-start(f32[24,12,8]{0,1,2:T(8,128)} %bitcast.70), channel_id=1, source_target_pairs={{1,0},{2,1},{3,2},{0,3},{5,4},{6,5},{7,6},{4,7},{9,8},{10,9},{11,1... | collective-permute-start | bytes 27656 | tf_op jit(solution)/shard_map/ppermute | solution.py:20
  37.1 10.0 %collective-permute-start.4 = (f32[24,12,128]{2,0,1:T(8,128)}, f32[24,12,128]{2,0,1:T(8,128)}, u32[]{:S(2)}, u32[]{:S(2)}) collective-permute-start(f32[24,12,128]{2,0,1:T(8,128)} %get-tuple-element.19), channel_id=1, source_target_pairs={{4,0},{8,4},{12,8},{16,12},{20,16},{24,20},{28,24},{0,28},{5,1},{9... | collective-permute-start | bytes 442376 | tf_op jit(solution)/shard_map/ppermute | solution.py:20
  41.6 8.2 %collective-permute-start.5 = (f32[24,12,128]{2,0,1:T(8,128)}, f32[24,12,128]{2,0,1:T(8,128)}, u32[]{:S(2)}, u32[]{:S(2)}) collective-permute-start(f32[24,12,128]{2,0,1:T(8,128)} %get-tuple-element.20), channel_id=1, source_target_pairs={{28,0},{0,4},{4,8},{8,12},{12,16},{16,20},{20,24},{24,28},{29,1},{... | collective-permute-start | bytes 442376 | tf_op jit(solution)/shard_map/ppermute | solution.py:20
  43.0 3.9 %collective-permute-start.7 = (f32[24,12,8]{0,1,2:T(8,128)}, f32[24,12,8]{0,1,2:T(8,128)S(1)}, u32[]{:S(2)}, u32[]{:S(2)}) collective-permute-start(f32[24,12,8]{0,1,2:T(8,128)} %bitcast.73), channel_id=1, source_target_pairs={{3,0},{0,1},{1,2},{2,3},{7,4},{4,5},{5,6},{6,7},{11,8},{8,9},{9,10... | collective-permute-start | bytes 27656 | tf_op jit(solution)/shard_map/ppermute | solution.py:20
  63.4 5.7 %collective-permute-start.10 = (f32[24,12,8]{0,1,2:T(8,128)}, f32[24,12,8]{0,1,2:T(8,128)}, u32[]{:S(2)}, u32[]{:S(2)}) collective-permute-start(f32[24,12,8]{0,1,2:T(8,128)} %bitcast.71), channel_id=1, source_target_pairs={{1,0},{2,1},{3,2},{0,3},{5,4},{6,5},{7,6},{4,7},{9,8},{10,9},{11,1... | collective-permute-start | bytes 27656 | tf_op jit(solution)/shard_map/ppermute | solution.py:20
  64.1 8.9 %collective-permute-start.8 = (f32[24,12,128]{2,0,1:T(8,128)}, f32[24,12,128]{2,0,1:T(8,128)}, u32[]{:S(2)}, u32[]{:S(2)}) collective-permute-start(f32[24,12,128]{2,0,1:T(8,128)} %get-tuple-element.5), channel_id=1, source_target_pairs={{4,0},{8,4},{12,8},{16,12},{20,16},{24,20},{28,24},{0,28},{5,1},{9... | collective-permute-start | bytes 442376 | tf_op jit(solution)/shard_map/ppermute | solution.py:20
  67.4 9.0 %collective-permute-start.9 = (f32[24,12,128]{2,0,1:T(8,128)}, f32[24,12,128]{2,0,1:T(8,128)}, u32[]{:S(2)}, u32[]{:S(2)}) collective-permute-start(f32[24,12,128]{2,0,1:T(8,128)} %get-tuple-element.6), channel_id=1, source_target_pairs={{28,0},{0,4},{4,8},{8,12},{12,16},{16,20},{20,24},{24,28},{29,1},{... | collective-permute-start | bytes 442376 | tf_op jit(solution)/shard_map/ppermute | solution.py:20
  68.9 3.9 %collective-permute-start.11 = (f32[24,12,8]{0,1,2:T(8,128)}, f32[24,12,8]{0,1,2:T(8,128)S(1)}, u32[]{:S(2)}, u32[]{:S(2)}) collective-permute-start(f32[24,12,8]{0,1,2:T(8,128)} %bitcast.72), channel_id=1, source_target_pairs={{3,0},{0,1},{1,2},{2,3},{7,4},{4,5},{5,6},{6,7},{11,8},{8,9},{9,10... | collective-permute-start | bytes 27656 | tf_op jit(solution)/shard_map/ppermute | solution.py:20
where the time goes:
time: 84.6 us; the launch traced here: 84.1 us
  local copies, waits for them, and re-layouts  32.5 us (38%)
  starting transfers between devices  16.4 us (19%)
  other arithmetic  14.7 us (17%)
  matrix products  10.9 us (13%)
  waiting for transfers between devices  9.05 us (11%)
    ppermute x12, starting transfers between devices, shifted(): return lax.ppermute(block, axis, route)  16.4 us
    sub x3, other arithmetic, advance(): total - field * field  14.6 us
    dot_general x12, matrix products, reorder(): jnp.einsum('st,tzc->szc', select, rim, precision=lax.Precision.HIGHEST)  10.9 us
    ppermute x12, waiting for transfers between devices, shifted(): return lax.ppermute(block, axis, route)  9.05 us
    unnamed x35, local copies, waits for them, and re-layouts  7.11 us
    slice x6, local copies, waits for them, and re-layouts, advance(): jnp.roll(field, 1, axis=1)  4.55 us
    slice x3, local copies, waits for them, and re-layouts, advance(): jnp.roll(field, 1, axis=3)  3.98 us
    slice x3, local copies, waits for them, and re-layouts, advance(): jnp.roll(field, 1, axis=2)  3.29 us
  transfers between devices with their start and end apart: 12, of which 4 were waited for; matrix products, arithmetic and copies ran while one was open for 23% of the time, Pallas kernels for 0%

commit v1 on v0

v1 whole, which is shorter than its diff:
```python
import functools

import jax
import jax.numpy as jnp
from jax import lax
from jax.experimental import pallas as pl
from jax.experimental.pallas import tpu as pltpu
from jax.sharding import PartitionSpec as P


LINKS = 6
SPAN = 8
GROUP = 16
RATE = 0.1
UNROLL = 4


def row_and_lane(rows, cols):
    row = lax.broadcasted_iota(jnp.int32, (rows, cols), 0)
    lane = lax.broadcasted_iota(jnp.int32, (rows, cols), 1)
    return row, lane


def spin(tile, amount):
    cols = tile.shape[1]
    amount = amount % cols
    return tile if amount == 0 else pltpu.roll(tile, amount, 1)


def group_sum(tile):
    shift = GROUP
    while shift < tile.shape[1]:
        tile = tile + spin(tile, shift)
        shift *= 2
    return tile


def step(src, dst, slots, depth, rows, cols, squares=None):
    row, lane = row_and_lane(rows, cols)
    first_row, last_row = row == 0, row == rows - 1
    first_lane, last_lane = lane == 0, lane == cols - 1

    def add(parts, s, term):
        parts[s % 4] = term if parts[s % 4] is None else parts[s % 4] + term

    def total(parts):
        return (parts[0] + parts[1]) + (parts[2] + parts[3])

    def at(z):
        return pl.ds(pl.multiple_of((z + 1) * rows, rows), rows)

    def layer(z, factor):
        following, parts = [None] * 4, [None] * 4
        for s in range(slots):
            v, below, above = src[s, at(z), :], src[s, at(z - 1), :], src[s, at(z + 1), :]
            add(following, s, above * above)
            x_sum = jnp.where(first_row, 0.0, pltpu.roll(v, 1, 0)) + jnp.where(
                last_row, 0.0, pltpu.roll(v, rows - 1, 0)
            )
            y_sum = jnp.where(first_lane, 0.0, pltpu.roll(v, 1, 1)) + jnp.where(
                last_lane, 0.0, pltpu.roll(v, cols - 1, 1)
            )
            new = RATE * (v * (factor + v * v) + ((x_sum + y_sum) + (below + above)))
            dst[s, at(z), :] = new
            if squares is not None:
                add(parts, s, new * new)
        if squares is not None:
            squares[pl.ds(pl.multiple_of(z * rows, rows), rows), :] = total(parts)
        return 4.5 - 1.5 * total(following)

    def layers(i, factor):
        for j in range(UNROLL):
            factor = layer(i * UNROLL + j, factor)
        return factor

    first = [None] * 4
    for s in range(slots):
        v = src[s, at(0), :]
        add(first, s, v * v)
    lax.fori_loop(0, depth // UNROLL, layers, 4.5 - 1.5 * total(first))


def gather_columns(tile_of, c, depth, rows, cols, beside=0):
    _, lane = row_and_lane(rows, cols)
    result, other = jnp.zeros((rows, cols), jnp.float32), jnp.zeros((rows, cols), jnp.float32)
    for k in range(LINKS):
        near, far = jnp.zeros_like(result), jnp.zeros_like(other)
        for z in range(depth):
            place = GROUP * k + z
            moved = spin(tile_of(k, z), place - c)
            near = jnp.where(lane == place, moved, near)
            if beside:
                far = jnp.where(lane == (place + beside) % cols, moved, far)
        result = result + near
        other = other + far
    return result, spin(other, -beside)


def raw_kernel(
    slots, depth, rows, cols,
    field, planes, grains, maps,
    now, y_low, y_up, lists,
    planes_in, grains_in, maps_in, inverse, arrived,
):
    copies = [
        pltpu.make_async_copy(maps, maps_in, arrived.at[0]),
        pltpu.make_async_copy(grains, grains_in, arrived.at[1]),
        pltpu.make_async_copy(planes, planes_in, arrived.at[2]),
        pltpu.make_async_copy(field, now.at[pl.ds(0, slots), pl.ds(rows, depth * rows), :], arrived.at[3]),
    ]
    for copy in copies:
        copy.start()
    now[slots] = jnp.zeros(((depth + 2) * rows, cols), jnp.float32)
    for face in range(4):
        for place in range(SPAN):
            lists[face * SPAN + place] = slots
    for t in range(slots + 1):
        inverse[t] = slots
        inverse[slots + 1 + t] = slots

    copies[0].wait()
    for s in range(slots):
        for face in (0, 2):
            partner = maps_in[0, 0, face, s]
            inverse[face // 2 * (slots + 1) + jnp.where(partner >= 0, partner, slots)] = s
    counts = [jnp.int32(face * SPAN) for face in range(4)]
    for s in range(slots):
        for face in range(4):
            if face in (1, 3):
                valid = maps_in[0, 0, face, s] >= 0
                slot = jnp.where(valid, s, slots)
            else:
                slot = inverse[face // 2 * (slots + 1) + s]
                valid = slot < slots
            lists[counts[face]] = slot
            counts[face] = counts[face] + valid.astype(jnp.int32)

    top = (depth + 1) * rows
    copies[1].wait()
    copies[2].wait()
    for s in range(slots):
        grain = grains_in[0, 0, s]
        now[s, pl.ds(0, rows), :] = jnp.where(planes_in[0] == grain, 1.0, 0.0)
        now[s, pl.ds(top, rows), :] = jnp.where(planes_in[1] == grain, 1.0, 0.0)
    copies[3].wait()

    y_low[pl.ds(0, rows), :], _ = gather_columns(
        lambda k, z: now[lists[2 * SPAN + k], pl.ds((z + 1) * rows, rows), :], 0, depth, rows, cols
    )
    y_up[pl.ds(0, rows), :], _ = gather_columns(
        lambda k, z: now[lists[3 * SPAN + k], pl.ds((z + 1) * rows, rows), :], cols - 1, depth, rows, cols
    )
    y_low[pl.ds(rows, rows), :], y_up[pl.ds(rows, rows), :] = gather_corners(now, lists, depth, rows, cols)


def gather_corners(ref, lists, depth, rows, cols):
    row, _ = row_and_lane(rows, cols)

    def both(k, z):
        at = pl.ds((z + 1) * rows, rows)
        return jnp.where(row < rows // 2, ref[lists[k], at, :], ref[lists[SPAN + k], at, :])

    return gather_columns(both, 0, depth, rows, cols, beside=-1)


def first_kernel(
    slots, depth, rows, cols,
    now, lists,
    stepped, x_low, x_up, y_low, y_up,
    squares,
):
    top = (depth + 1) * rows
    for s in range(slots):
        for at in (0, top):
            stepped[s, pl.ds(at, rows), :] = now[s, pl.ds(at, rows), :]
    stepped[slots] = jnp.zeros(((depth + 2) * rows, cols), jnp.float32)

    step(now, stepped, slots, depth, rows, cols, squares)

    row, lane = row_and_lane(rows, cols)
    block = LINKS * depth
    last_group = (lane >= LINKS * GROUP) & (lane < (LINKS + 1) * GROUP)

    partials = []
    for side, out in ((0, y_low), (1, y_up)):
        c, inward = (0, 1) if side == 0 else (cols - 1, -1)
        base = (2 + side) * SPAN
        partial, inner = gather_columns(
            lambda k, z: stepped[lists[base + k], pl.ds((z + 1) * rows, rows), :], c, depth, rows, cols, beside=inward
        )
        for k in range(LINKS):
            for z, at in ((0, 0), (depth - 1, top)):
                place = GROUP * k + z
                frozen = spin(now[lists[base + k], pl.ds(at, rows), :], place - c)
                inner = inner + jnp.where(lane == place, frozen, 0.0)
        total = jnp.zeros((rows, cols), jnp.float32)
        for z in range(depth):
            place = LINKS * GROUP + z
            total = jnp.where(lane == place, spin(squares[pl.ds(z * rows, rows), :], place - c), total)
        inner = jnp.where(last_group, total - group_sum(partial * partial), inner)
        out[pl.ds(0, rows), :] = partial
        out[pl.ds(rows, rows), :] = inner
        partials.append(partial)
    y_low[pl.ds(2 * rows, rows), :], y_up[pl.ds(2 * rows, rows), :] = gather_corners(stepped, lists, depth, rows, cols)

    for face, out in ((0, x_low), (1, x_up)):
        r, inner_r = (0, 1) if face == 0 else (rows - 1, rows - 2)
        out[pl.ds(3 * block, out.shape[0] - 3 * block), :] = jnp.zeros((out.shape[0] - 3 * block, cols), jnp.float32)
        rest = squares[pl.ds(r, depth, stride=rows), :]
        edge_row, _ = row_and_lane(depth, cols)
        for k in range(LINKS):
            slot = lists[face * SPAN + k]
            rim = now[slot, pl.ds(rows + r, depth, stride=rows), :]
            partial = stepped[slot, pl.ds(rows + r, depth, stride=rows), :]
            inner = stepped[slot, pl.ds(rows + inner_r, depth, stride=rows), :]
            below = jnp.broadcast_to(now[slot, pl.ds(r, 1), :], (depth, cols))
            above = jnp.broadcast_to(now[slot, pl.ds(top + r, 1), :], (depth, cols))
            inner = inner + jnp.where(edge_row == 0, below, jnp.where(edge_row == depth - 1, above, 0.0))
            rest = rest - partial * partial
            out[pl.ds(k * depth, depth), :] = rim
            out[pl.ds(block + k * depth, depth), :] = partial
            out[pl.ds(2 * block + k * depth, depth), :] = inner
        out[pl.ds(3 * block, depth), :] = rest
        for side in range(2):
            out[pl.ds(3 * block + depth + side, 1), :] = partials[side][r : r + 1]


def corner_kernel(depth, rows, cols, x_low_in, x_up_in, y_low, y_up, x_low, x_up):
    start = 3 * LINKS * depth + depth + 2
    for r, out in ((0, x_low), (rows - 1, x_up)):
        for side, got in ((0, y_low), (1, y_up)):
            out[pl.ds(start + side, 1), :] = got[pl.ds(r, 1), :]
            out[pl.ds(start + 2 + side, 1), :] = got[pl.ds(rows + r, 1), :]


def second_kernel(
    slots, depth, rows, cols,
    stepped_in, x_low_own, x_up_own, x_low, x_up, raw_low_own, raw_up_own, raw_low, raw_up,
    y_low_own, y_up_own, y_low, y_up, lists,
    now, result,
    later, x_one, x_two, sent,
):
    row, lane = row_and_lane(rows, cols)
    block = LINKS * depth
    tail = 3 * block + depth
    top = (depth + 1) * rows

    for s in range(slots):
        for at in (0, top):
            later[s, pl.ds(at, rows), :] = now[s, pl.ds(at, rows), :]
    later[slots] = jnp.zeros(((depth + 2) * rows, cols), jnp.float32)

    x_one[...] = jnp.zeros(x_one.shape, jnp.float32)
    tall_row, tall_lane = row_and_lane(GROUP, cols)
    for face, own, got in ((0, x_low_own, x_low), (1, x_up_own, x_up)):
        r = 0 if face == 0 else rows - 1
        total = got[pl.ds(3 * block, depth), :]
        ones, own_ones = [], []
        for k in range(LINKS):
            one = got[pl.ds(block + k * depth, depth), :] + RATE * own[pl.ds(k * depth, depth), :]
            own_one = own[pl.ds(block + k * depth, depth), :] + RATE * got[pl.ds(k * depth, depth), :]
            total = total + one * one
            x_one[face, pl.ds(k * GROUP + 1, depth), :] = one
            ones.append(one)
            own_ones.append(own_one)
        for k in range(LINKS):
            now[lists[face * SPAN + k], pl.ds(rows + r, depth, stride=rows), :] = own_ones[k]
        for side in range(2):
            c = 0 if side == 0 else cols - 1
            term = RATE * got[pl.ds(tail + 2 + side, 1), :]
            term = group_sum(term * (2.0 * got[pl.ds(tail + side, 1), :] + term))
            spread = jnp.where(tall_row == tall_lane, jnp.broadcast_to(term, (GROUP, cols)), 0.0)
            column = jnp.sum(spread, axis=1, keepdims=True)
            total = total + jnp.where(tall_lane == c, column, 0.0)[:depth]
        factor = 4.5 - 1.5 * total
        for k in range(LINKS):
            one = ones[k]
            z_sum = x_one[face, pl.ds(k * GROUP, depth), :] + x_one[face, pl.ds(k * GROUP + 2, depth), :]
            y_sum = jnp.where(tall_lane[:depth] == 0, 0.0, pltpu.roll(one, 1, 1)) + jnp.where(
                tall_lane[:depth] == cols - 1, 0.0, pltpu.roll(one, cols - 1, 1)
            )
            inner = got[pl.ds(2 * block + k * depth, depth), :]
            x_two[face, pl.ds(k * GROUP, depth), :] = RATE * (
                one * (factor + one * one) + ((inner + own_ones[k]) + (z_sum + y_sum))
            )

    y_own_one, y_one, y_two = [], [], []
    for side, raw_own, raw_got, own, got in (
        (0, raw_low_own, raw_low, y_low_own, y_low),
        (1, raw_up_own, raw_up, y_up_own, y_up),
    ):
        tile = lambda ref, i: ref[pl.ds(i * rows, rows), :]
        own_one = tile(own, 0) + RATE * tile(raw_got, 0)
        one = tile(got, 0) + RATE * tile(raw_own, 0)
        inner = tile(got, 1)
        term = RATE * jnp.where(
            row == 0,
            jnp.broadcast_to(x_low[pl.ds(tail + 4 + side, 1), :], (rows, cols)),
            jnp.where(
                row == rows - 1, jnp.broadcast_to(x_up[pl.ds(tail + 4 + side, 1), :], (rows, cols)), 0.0
            ),
        )
        rest = jnp.where((lane >= LINKS * GROUP) & (lane < (LINKS + 1) * GROUP), inner, 0.0)
        total = group_sum((one * one + rest) + term * (2.0 * tile(got, 2) + term))
        x_sum = jnp.where(row == 0, 0.0, pltpu.roll(one, 1, 0)) + jnp.where(
            row == rows - 1, 0.0, pltpu.roll(one, rows - 1, 0)
        )
        z_sum = spin(one, 1) + spin(one, -1)
        two = RATE * (one * ((4.5 - 1.5 * total) + one * one) + ((inner + own_one) + (x_sum + z_sum)))
        y_own_one.append(own_one)
        y_one.append(RATE * one)
        y_two.append(RATE * two)

    def y_faces(ref, tiles, replace):
        for k in range(LINKS):
            for side in range(2):
                c = 0 if side == 0 else cols - 1
                slot = lists[(2 + side) * SPAN + k]
                old = [ref[slot, pl.ds((z + 1) * rows, rows), :] for z in range(depth)]
                for z in range(depth):
                    moved = spin(tiles[side], c - GROUP * k - z)
                    new = jnp.where(lane == c, moved if replace else old[z] + moved, old[z])
                    ref[slot, pl.ds((z + 1) * rows, rows), :] = new

    def x_faces(ref, rim, offset):
        for face in range(2):
            at = pl.ds(rows + (0 if face == 0 else rows - 1), depth, stride=rows)
            old = [ref[lists[face * SPAN + k], at, :] for k in range(LINKS)]
            for k in range(LINKS):
                ref[lists[face * SPAN + k], at, :] = old[k] + RATE * rim[face, pl.ds(k * GROUP + offset, depth), :]

    y_faces(now, y_own_one, True)
    step(now, later, slots, depth, rows, cols)
    x_faces(later, x_one, 1)
    y_faces(later, y_one, False)
    step(later, now, slots, depth, rows, cols)
    x_faces(now, x_two, 0)
    y_faces(now, y_two, False)
    copy = pltpu.make_async_copy(now.at[pl.ds(0, slots), pl.ds(rows, depth * rows), :], result, sent)
    copy.start()
    copy.wait()


def shifted(block, axis, distance):
    size = lax.axis_size(axis)
    return lax.ppermute(block, axis, [((i - distance) % size, i) for i in range(size)])


def on_device(order_params, grain_ids, channel_maps, zplanes):
    slots, depth, rows, cols = order_params.shape
    f32 = jnp.float32
    shape = jax.ShapeDtypeStruct
    padded = pltpu.VMEM((slots + 1, (depth + 2) * rows, cols), f32)
    x_pack = shape((-(-(3 * LINKS * depth + depth + 6) // rows) * rows, cols), f32)
    vmem = pl.BlockSpec(memory_space=pltpu.VMEM)
    smem = pl.BlockSpec(memory_space=pltpu.SMEM)
    hbm = pl.BlockSpec(memory_space=pltpu.HBM)
    params = pltpu.CompilerParams(vmem_limit_bytes=24 * 1024 * 1024)
    field = order_params.reshape(slots, depth * rows, cols)
    sizes = (slots, depth, rows, cols)

    now, raw_low, raw_up, lists = pl.pallas_call(
        functools.partial(raw_kernel, *sizes),
        out_shape=[padded, shape((2 * rows, cols), f32), shape((2 * rows, cols), f32), shape((4 * SPAN,), jnp.int32)],
        in_specs=[hbm] * 4,
        out_specs=[vmem] * 3 + [smem],
        scratch_shapes=[
            pltpu.VMEM(zplanes.shape, jnp.int32),
            pltpu.SMEM(grain_ids.shape, jnp.int32),
            pltpu.SMEM(channel_maps.shape, jnp.int32),
            pltpu.SMEM((2 * (slots + 1),), jnp.int32),
            pltpu.SemaphoreType.DMA((4,)),
        ],
        compiler_params=params,
        name="raw_rims",
    )(*(pltpu.with_memory_space_constraint(x, pltpu.HBM) for x in (field, zplanes, grain_ids, channel_maps)))

    raw_from_right = shifted(raw_low, "gy", -1)
    raw_from_left = shifted(raw_up, "gy", 1)

    stepped, x_low, x_up, y_low, y_up = pl.pallas_call(
        functools.partial(first_kernel, *sizes),
        out_shape=[padded, x_pack, x_pack, shape((3 * rows, cols), f32), shape((3 * rows, cols), f32)],
        in_specs=[vmem, smem],
        out_specs=[vmem] * 5,
        scratch_shapes=[pltpu.VMEM((depth * rows, cols), f32)],
        compiler_params=params,
        name="first_step",
    )(now, lists)

    x_low, x_up = pl.pallas_call(
        functools.partial(corner_kernel, depth, rows, cols),
        out_shape=[x_pack, x_pack],
        in_specs=[vmem] * 4,
        out_specs=[vmem] * 2,
        input_output_aliases={0: 0, 1: 1},
        compiler_params=params,
        name="corners",
    )(x_low, x_up, raw_from_left, raw_from_right)

    from_up = shifted(x_low, "gx", -1)
    from_low = shifted(x_up, "gx", 1)
    from_right = shifted(y_low, "gy", -1)
    from_left = shifted(y_up, "gy", 1)

    _, result = pl.pallas_call(
        functools.partial(second_kernel, *sizes),
        out_shape=[padded, shape(field.shape, f32)],
        in_specs=[vmem] * 13 + [smem],
        out_specs=[vmem, hbm],
        scratch_shapes=[
            padded,
            pltpu.VMEM((2, LINKS * GROUP, cols), f32),
            pltpu.VMEM((2, LINKS * GROUP, cols), f32),
            pltpu.SemaphoreType.DMA,
        ],
        input_output_aliases={0: 0},
        compiler_params=params,
        name="later_steps",
    )(
        stepped, x_low, x_up, from_low, from_up, raw_low, raw_up, raw_from_left, raw_from_right,
        y_low, y_up, from_left, from_right, lists,
    )
    return result.reshape(order_params.shape)


def solution(mesh):
    in_specs = (
        P(None, None, "gx", "gy"),
        P("gx", "gy", None),
        P("gx", "gy", None, None),
        P(None, "gx", "gy"),
    )
    return jax.shard_map(
        on_device, mesh=mesh, in_specs=in_specs, out_specs=P(None, None, "gx", "gy"), check_vma=False
    )
```

time: 84.6 us -> 25 us (0.30)
  local copies, waits for them, and re-layouts: 32.5 us -> 0 us
  other arithmetic: 14.7 us -> 0 us
  matrix products: 10.9 us -> 0 us
  Pallas kernels: 0 us -> 8.38 us
  starting transfers between devices: 16.4 us -> 8.57 us
  waiting for transfers between devices: 9.05 us -> 7.81 us
    slice x17 -> x0, local copies, waits for them, and re-layouts: 15.4 us -> none  [the longest x6 4.55 us: advance(): jnp.roll(field, 1, axis=1)]
    sub x3 -> x0, other arithmetic: 14.6 us -> none  [advance(): total - field * field]
    dot_general x12 -> x0, matrix products: 10.9 us -> none  [reorder(): jnp.einsum('st,tzc->szc', select, rim, precision=lax.Precision.HIGHEST)]
    pallas_call x0 -> x4, Pallas kernels: none -> 8.38 us  [the longest x1 4.26 us: on_device(): pl.pallas_call(functools.partial(second_kernel, *sizes), out_shape=[padde...]
    squeeze x7 -> x0, local copies, waits for them, and re-layouts: 8.3 us -> none  [the longest x2 2.87 us: on_device(): lower_y = reorder(shifted(field[:, :, :, -1], 'gy', 1), face_maps[2])]
    ppermute x12 -> x6, starting transfers between devices: 16.4 us -> 8.57 us  [shifted(): lax.ppermute(block, axis, [((i - distance) % size, i) for i in range(size)])]
    unnamed x35 -> x0, local copies, waits for them, and re-layouts: 7.11 us -> none
    sub x1 -> x0, local copies, waits for them, and re-layouts: 1.7 us -> none  [advance(): return field - time_step * mobility * rate]
  transfers between devices with their start and end apart: 12 -> 6, of which waited for: 4 -> 3; matrix products, arithmetic and copies ran while one was open for 23% -> 0% of each run, Pallas kernels for 0% -> 8%
where the time goes in v1:
time: 25 us; the launch traced here: 24.8 us
  starting transfers between devices  8.57 us (34%)
  Pallas kernels  8.38 us (34%)
  waiting for transfers between devices  7.81 us (31%)
    ppermute x6, starting transfers between devices, shifted(): lax.ppermute(block, axis, [((i - distance) % size, i) for i in range(size)])  8.57 us
    ppermute x6, waiting for transfers between devices, shifted(): lax.ppermute(block, axis, [((i - distance) % size, i) for i in range(size)])  7.81 us
    pallas_call x1, Pallas kernels, on_device(): pl.pallas_call(functools.partial(second_kernel, *sizes), out_shape=[padde...  4.26 us
    pallas_call x1, Pallas kernels, on_device(): pl.pallas_call(functools.partial(raw_kernel, *sizes), out_shape=[padded,...  2.13 us
    pallas_call x1, Pallas kernels, on_device(): pl.pallas_call(functools.partial(first_kernel, *sizes), out_shape=[padded...  1.98 us
  transfers between devices with their start and end apart: 6, of which 3 were waited for; matrix products, arithmetic and copies ran while one was open for 0% of the time, Pallas kernels for 8%

profile of v1, /device:TPU:0, one launch (start us, length us, event | category | flops | bytes accessed | tf_op | source)
XLA Modules:
  0.0 24.8 jit_solution(15790998728863492449)
XLA Ops:
  0.0 2.1 %raw_rims.1 = (f32[25,112,128]{2,1,0:T(8,128)S(1)}, f32[16,128]{1,0:T(8,128)S(1)}, f32[16,128]{1,0:T(8,128)S(1)}, s32[32]{0:T(128)S(1)}) custom-call(f32[24,96,128]{2,1,0:T(8,128)} %bitcast.2, s32[2,8,128]{2,1,0:T(8,128)} %planes.1, s32[1,1,24]{2,1,0:T(1,128)} %grains.1, s32[1,1,4,24]{3,2,1,0:T(4,128)} %maps.1), custom_call_target="tpu_custom_call" | custom-call | tf_op jit(solution)/shard_map/raw_rims/pallas_call | solution.py:362
  2.1 0.5 %collective-permute-start = (f32[16,128]{1,0:T(8,128)S(1)}, f32[16,128]{1,0:T(8,128)S(1)}, u32[]{:S(2)}, u32[]{:S(2)}) collective-permute-start(f32[16,128]{1,0:T(8,128)S(1)} %get-tuple-element.22.raw_up_own), channel_id=1, source_target_pairs={{3,0},{0,1},{1,2},{2,3},{7,4},{4,5},{5,6},{6,7},{11,8},{8,9},{9,10... | collective-permute-start | bytes 24584 | tf_op jit(solution)/shard_map/ppermute | solution.py:346
  2.6 2.0 %collective-permute-start.1 = (f32[16,128]{1,0:T(8,128)S(1)}, f32[16,128]{1,0:T(8,128)S(1)}, u32[]{:S(2)}, u32[]{:S(2)}) collective-permute-start(f32[16,128]{1,0:T(8,128)S(1)} %get-tuple-element.23.raw_low_own), channel_id=1, source_target_pairs={{1,0},{2,1},{3,2},{0,3},{5,4},{6,5},{7,6},{4,7},{9,8},{10,9},{11,1... | collective-permute-start | bytes 24584 | tf_op jit(solution)/shard_map/ppermute | solution.py:346
  4.7 2.0 %first_step.1 = (f32[25,112,128]{2,1,0:T(8,128)S(1)}, f32[240,128]{1,0:T(8,128)S(1)}, f32[240,128]{1,0:T(8,128)S(1)}, f32[24,128]{1,0:T(8,128)S(1)}, f32[24,128]{1,0:T(8,128)S(1)}) custom-call(f32[25,112,128]{2,1,0:T(8,128)S(1)} %get-tuple-element.17.now, s32[32]{0:T(128)S(1)} %get-tuple-element.18.lists), custom_call_target="tpu_custom_call" | custom-call | tf_op jit(solution)/shard_map/first_step/pallas_call | solution.py:381
  6.6 0.0 collective-permute-done.y_low.raw_low
  6.7 0.0 collective-permute-done.1.y_up.raw_up
  6.7 5.3 %collective-permute-start.3 = (f32[240,128]{1,0:T(8,128)S(1)}, f32[240,128]{1,0:T(8,128)S(1)}, u32[]{:S(2)}, u32[]{:S(2)}) collective-permute-start(f32[240,128]{1,0:T(8,128)S(1)} %get-tuple-element.24.x_low_own), channel_id=1, source_target_pairs={{4,0},{8,4},{12,8},{16,12},{20,16},{24,20},{28,24},{0,28},{5,1},{9... | collective-permute-start | bytes 368648 | tf_op jit(solution)/shard_map/ppermute | solution.py:346
  12.0 0.0 collective-permute-start.2
  12.0 0.7 %collective-permute-start.5 = (f32[24,128]{1,0:T(8,128)S(1)}, f32[24,128]{1,0:T(8,128)S(1)}, u32[]{:S(2)}, u32[]{:S(2)}) collective-permute-start(f32[24,128]{1,0:T(8,128)S(1)} %get-tuple-element.26.y_low_own), channel_id=1, source_target_pairs={{1,0},{2,1},{3,2},{0,3},{5,4},{6,5},{7,6},{4,7},{9,8},{10,9},{11,1... | collective-permute-start | bytes 36872 | tf_op jit(solution)/shard_map/ppermute | solution.py:346
  12.7 0.0 collective-permute-start.4
  12.7 1.4 %collective-permute-done.5.y_up = f32[24,128]{1,0:T(8,128)S(1)} collective-permute-done((f32[24,128]{1,0:T(8,128)S(1)}, f32[24,128]{1,0:T(8,128)S(1)}, u32[]{:S(2)}, u32[]{:S(2)}) %collective-permute-start.5) | collective-permute-done | bytes 12320 | tf_op jit(solution)/shard_map/ppermute | solution.py:346
  14.1 1.8 %collective-permute-done.4.y_low = f32[24,128]{1,0:T(8,128)S(1)} collective-permute-done((f32[24,128]{1,0:T(8,128)S(1)}, f32[24,128]{1,0:T(8,128)S(1)}, u32[]{:S(2)}, u32[]{:S(2)}) %collective-permute-start.4) | collective-permute-done | bytes 12320 | tf_op jit(solution)/shard_map/ppermute | solution.py:346
  15.9 0.0 collective-permute-done.3.x_up
  15.9 4.6 %collective-permute-done.2.x_low = f32[240,128]{1,0:T(8,128)S(1)} collective-permute-done((f32[240,128]{1,0:T(8,128)S(1)}, f32[240,128]{1,0:T(8,128)S(1)}, u32[]{:S(2)}, u32[]{:S(2)}) %collective-permute-start.2) | collective-permute-done | bytes 122912 | tf_op jit(solution)/shard_map/ppermute | solution.py:346
  20.5 4.3 %later_steps.1 = (f32[25,112,128]{2,1,0:T(8,128)S(1)}, f32[24,96,128]{2,1,0:T(8,128)}) custom-call(f32[25,112,128]{2,1,0:T(8,128)S(1)} %get-tuple-element.19.stepped_in, f32[240,128]{1,0:T(8,128)S(1)} %get-tuple-element.24.x_low_own, f32[240,128]{1,0:T(8,128)S(1)} %get-tuple-element.25.x_up_own, ...), custom_call_target="tpu_custom_call", output_to_operand_aliasing={{0}: (0, {})} | custom-call | tf_op jit(solution)/shard_map/later_steps/pallas_call | solution.py:406
  (1 shorter events, 0.0 us)
Async XLA Ops:
  2.1 4.5 %collective-permute-start = (f32[16,128]{1,0:T(8,128)S(1)}, f32[16,128]{1,0:T(8,128)S(1)}, u32[]{:S(2)}, u32[]{:S(2)}) collective-permute-start(f32[16,128]{1,0:T(8,128)S(1)} %get-tuple-element.22.raw_up_own), channel_id=1, source_target_pairs={{3,0},{0,1},{1,2},{2,3},{7,4},{4,5},{5,6},{6,7},{11,8},{8,9},{9,10... | collective-permute-start | bytes 24584 | tf_op jit(solution)/shard_map/ppermute | solution.py:346
  2.6 4.0 %collective-permute-start.1 = (f32[16,128]{1,0:T(8,128)S(1)}, f32[16,128]{1,0:T(8,128)S(1)}, u32[]{:S(2)}, u32[]{:S(2)}) collective-permute-start(f32[16,128]{1,0:T(8,128)S(1)} %get-tuple-element.23.raw_low_own), channel_id=1, source_target_pairs={{1,0},{2,1},{3,2},{0,3},{5,4},{6,5},{7,6},{4,7},{9,8},{10,9},{11,1... | collective-permute-start | bytes 24584 | tf_op jit(solution)/shard_map/ppermute | solution.py:346
  6.7 9.2 %collective-permute-start.3 = (f32[240,128]{1,0:T(8,128)S(1)}, f32[240,128]{1,0:T(8,128)S(1)}, u32[]{:S(2)}, u32[]{:S(2)}) collective-permute-start(f32[240,128]{1,0:T(8,128)S(1)} %get-tuple-element.24.x_low_own), channel_id=1, source_target_pairs={{4,0},{8,4},{12,8},{16,12},{20,16},{24,20},{28,24},{0,28},{5,1},{9... | collective-permute-start | bytes 368648 | tf_op jit(solution)/shard_map/ppermute | solution.py:346
  12.0 8.6 %collective-permute-start.2 = (f32[240,128]{1,0:T(8,128)S(1)}, f32[240,128]{1,0:T(8,128)S(1)}, u32[]{:S(2)}, u32[]{:S(2)}) collective-permute-start(f32[240,128]{1,0:T(8,128)S(1)} %get-tuple-element.25.x_up_own), channel_id=1, source_target_pairs={{28,0},{0,4},{4,8},{8,12},{12,16},{16,20},{20,24},{24,28},{29,1},{... | collective-permute-start | bytes 368648 | tf_op jit(solution)/shard_map/ppermute | solution.py:346
  12.0 2.1 %collective-permute-start.5 = (f32[24,128]{1,0:T(8,128)S(1)}, f32[24,128]{1,0:T(8,128)S(1)}, u32[]{:S(2)}, u32[]{:S(2)}) collective-permute-start(f32[24,128]{1,0:T(8,128)S(1)} %get-tuple-element.26.y_low_own), channel_id=1, source_target_pairs={{1,0},{2,1},{3,2},{0,3},{5,4},{6,5},{7,6},{4,7},{9,8},{10,9},{11,1... | collective-permute-start | bytes 36872 | tf_op jit(solution)/shard_map/ppermute | solution.py:346
  12.7 3.2 %collective-permute-start.4 = (f32[24,128]{1,0:T(8,128)S(1)}, f32[24,128]{1,0:T(8,128)S(1)}, u32[]{:S(2)}, u32[]{:S(2)}) collective-permute-start(f32[24,128]{1,0:T(8,128)S(1)} %get-tuple-element.27.y_up_own), channel_id=1, source_target_pairs={{3,0},{0,1},{1,2},{2,3},{7,4},{4,5},{5,6},{6,7},{11,8},{8,9},{9,10... | collective-permute-start | bytes 36872 | tf_op jit(solution)/shard_map/ppermute | solution.py:346

commit v2 on v1

v2 whole, which is shorter than its diff:
```python
import functools

import jax
import jax.numpy as jnp
from jax import lax
from jax.experimental import pallas as pl
from jax.experimental.pallas import tpu as pltpu
from jax.sharding import PartitionSpec as P


LINKS = 6
SPAN = 8
GROUP = 16
RATE = 0.1
UNROLL = 4


def row_and_lane(rows, cols):
    row = lax.broadcasted_iota(jnp.int32, (rows, cols), 0)
    lane = lax.broadcasted_iota(jnp.int32, (rows, cols), 1)
    return row, lane


def spin(tile, amount):
    cols = tile.shape[1]
    amount = amount % cols
    return tile if amount == 0 else pltpu.roll(tile, amount, 1)


def group_sum(tile):
    shift = GROUP
    while shift < tile.shape[1]:
        tile = tile + spin(tile, shift)
        shift *= 2
    return tile


def step(src, dst, slots, depth, rows, cols, squares=None):
    row, lane = row_and_lane(rows, cols)
    first_row, last_row = row == 0, row == rows - 1
    first_lane, last_lane = lane == 0, lane == cols - 1

    def add(parts, s, term):
        parts[s % 4] = term if parts[s % 4] is None else parts[s % 4] + term

    def total(parts):
        return (parts[0] + parts[1]) + (parts[2] + parts[3])

    def at(z):
        return pl.ds(pl.multiple_of((z + 1) * rows, rows), rows)

    def layer(z, factor):
        following, parts = [None] * 4, [None] * 4
        for s in range(slots):
            v, below, above = src[s, at(z), :], src[s, at(z - 1), :], src[s, at(z + 1), :]
            add(following, s, above * above)
            x_sum = jnp.where(first_row, 0.0, pltpu.roll(v, 1, 0)) + jnp.where(
                last_row, 0.0, pltpu.roll(v, rows - 1, 0)
            )
            y_sum = jnp.where(first_lane, 0.0, pltpu.roll(v, 1, 1)) + jnp.where(
                last_lane, 0.0, pltpu.roll(v, cols - 1, 1)
            )
            new = RATE * (v * (factor + v * v) + ((x_sum + y_sum) + (below + above)))
            dst[s, at(z), :] = new
            if squares is not None:
                add(parts, s, new * new)
        if squares is not None:
            squares[pl.ds(pl.multiple_of(z * rows, rows), rows), :] = total(parts)
        return 4.5 - 1.5 * total(following)

    def layers(i, factor):
        for j in range(UNROLL):
            factor = layer(i * UNROLL + j, factor)
        return factor

    first = [None] * 4
    for s in range(slots):
        v = src[s, at(0), :]
        add(first, s, v * v)
    lax.fori_loop(0, depth // UNROLL, layers, 4.5 - 1.5 * total(first))


def gather_columns(tile_of, c, depth, rows, cols, beside=0):
    _, lane = row_and_lane(rows, cols)
    result, other = jnp.zeros((rows, cols), jnp.float32), jnp.zeros((rows, cols), jnp.float32)
    for k in range(LINKS):
        near, far = jnp.zeros_like(result), jnp.zeros_like(other)
        for z in range(depth):
            place = GROUP * k + z
            moved = spin(tile_of(k, z), place - c)
            near = jnp.where(lane == place, moved, near)
            if beside:
                far = jnp.where(lane == (place + beside) % cols, moved, far)
        result = result + near
        other = other + far
    return result, spin(other, -beside)


def first_kernel(
    slots, depth, rows, cols,
    field, planes, grains, maps,
    now, stepped, squares, x_low, x_up, lists,
    planes_in, grains_in, maps_in, inverse, arrived,
):
    copies = [
        pltpu.make_async_copy(maps, maps_in, arrived.at[0]),
        pltpu.make_async_copy(grains, grains_in, arrived.at[1]),
        pltpu.make_async_copy(planes, planes_in, arrived.at[2]),
        pltpu.make_async_copy(field, now.at[pl.ds(0, slots), pl.ds(rows, depth * rows), :], arrived.at[3]),
    ]
    for copy in copies:
        copy.start()
    for ref in (now, stepped):
        ref[slots] = jnp.zeros(((depth + 2) * rows, cols), jnp.float32)
    for face in range(4):
        for place in range(SPAN):
            lists[face * SPAN + place] = slots
    for t in range(slots + 1):
        inverse[t] = slots
        inverse[slots + 1 + t] = slots

    copies[0].wait()
    for s in range(slots):
        for face in (0, 2):
            partner = maps_in[0, 0, face, s]
            inverse[face // 2 * (slots + 1) + jnp.where(partner >= 0, partner, slots)] = s
    counts = [jnp.int32(face * SPAN) for face in range(4)]
    for s in range(slots):
        for face in range(4):
            if face in (1, 3):
                valid = maps_in[0, 0, face, s] >= 0
                slot = jnp.where(valid, s, slots)
            else:
                slot = inverse[face // 2 * (slots + 1) + s]
                valid = slot < slots
            lists[counts[face]] = slot
            counts[face] = counts[face] + valid.astype(jnp.int32)

    top = (depth + 1) * rows
    copies[1].wait()
    copies[2].wait()
    for s in range(slots):
        grain = grains_in[0, 0, s]
        below = jnp.where(planes_in[0] == grain, 1.0, 0.0)
        above = jnp.where(planes_in[1] == grain, 1.0, 0.0)
        for ref in (now, stepped):
            ref[s, pl.ds(0, rows), :] = below
            ref[s, pl.ds(top, rows), :] = above
    copies[3].wait()

    step(now, stepped, slots, depth, rows, cols, squares)

    block = LINKS * depth
    edge_row, _ = row_and_lane(depth, cols)
    for face, out in ((0, x_low), (1, x_up)):
        r, inner_r = (0, 1) if face == 0 else (rows - 1, rows - 2)
        out[pl.ds(3 * block, out.shape[0] - 3 * block), :] = jnp.zeros((out.shape[0] - 3 * block, cols), jnp.float32)
        rest = squares[pl.ds(r, depth, stride=rows), :]
        for k in range(LINKS):
            slot = lists[face * SPAN + k]
            rim = now[slot, pl.ds(rows + r, depth, stride=rows), :]
            partial = stepped[slot, pl.ds(rows + r, depth, stride=rows), :]
            inner = stepped[slot, pl.ds(rows + inner_r, depth, stride=rows), :]
            below = jnp.broadcast_to(now[slot, pl.ds(r, 1), :], (depth, cols))
            above = jnp.broadcast_to(now[slot, pl.ds(top + r, 1), :], (depth, cols))
            inner = inner + jnp.where(edge_row == 0, below, jnp.where(edge_row == depth - 1, above, 0.0))
            rest = rest - partial * partial
            out[pl.ds(k * depth, depth), :] = rim
            out[pl.ds(block + k * depth, depth), :] = partial
            out[pl.ds(2 * block + k * depth, depth), :] = inner
        out[pl.ds(3 * block, depth), :] = rest


def gather_corners(ref, lists, depth, rows, cols):
    row, _ = row_and_lane(rows, cols)

    def both(k, z):
        at = pl.ds((z + 1) * rows, rows)
        return jnp.where(row < rows // 2, ref[lists[k], at, :], ref[lists[SPAN + k], at, :])

    return gather_columns(both, 0, depth, rows, cols, beside=-1)


def y_kernel(slots, depth, rows, cols, now, stepped, squares, lists, y_low, y_up):
    top = (depth + 1) * rows
    _, lane = row_and_lane(rows, cols)
    last_group = (lane >= LINKS * GROUP) & (lane < (LINKS + 1) * GROUP)
    for side, out in ((0, y_low), (1, y_up)):
        c, inward = (0, 1) if side == 0 else (cols - 1, -1)
        base = (2 + side) * SPAN
        rim, _ = gather_columns(
            lambda k, z: now[lists[base + k], pl.ds((z + 1) * rows, rows), :], c, depth, rows, cols
        )
        partial, inner = gather_columns(
            lambda k, z: stepped[lists[base + k], pl.ds((z + 1) * rows, rows), :], c, depth, rows, cols, beside=inward
        )
        for k in range(LINKS):
            for z, at in ((0, 0), (depth - 1, top)):
                place = GROUP * k + z
                frozen = spin(now[lists[base + k], pl.ds(at, rows), :], place - c)
                inner = inner + jnp.where(lane == place, frozen, 0.0)
        total = jnp.zeros((rows, cols), jnp.float32)
        for z in range(depth):
            place = LINKS * GROUP + z
            total = jnp.where(lane == place, spin(squares[pl.ds(z * rows, rows), :], place - c), total)
        inner = jnp.where(last_group, total - group_sum(partial * partial), inner)
        out[pl.ds(0, rows), :] = rim
        out[pl.ds(2 * rows, rows), :] = partial
        out[pl.ds(3 * rows, rows), :] = inner
    for i, ref in ((1, now), (4, stepped)):
        y_low[pl.ds(i * rows, rows), :], y_up[pl.ds(i * rows, rows), :] = gather_corners(ref, lists, depth, rows, cols)


def corner_kernel(rows, cols, y_low_own, y_up_own, y_low, y_up, c_low, c_up):
    for r, out in ((0, c_low), (rows - 1, c_up)):
        out[...] = jnp.zeros((rows, cols), jnp.float32)
        for side, own, got in ((0, y_low_own, y_low), (1, y_up_own, y_up)):
            out[pl.ds(side, 1), :] = own[pl.ds(2 * rows + r, 1), :]
            out[pl.ds(2 + side, 1), :] = got[pl.ds(r, 1), :]
            out[pl.ds(4 + side, 1), :] = got[pl.ds(rows + r, 1), :]


def y_faces(ref, tiles, lists, depth, rows, cols, replace):
    _, lane = row_and_lane(rows, cols)
    for k in range(LINKS):
        for side in range(2):
            c = 0 if side == 0 else cols - 1
            slot = lists[(2 + side) * SPAN + k]
            old = [ref[slot, pl.ds((z + 1) * rows, rows), :] for z in range(depth)]
            for z in range(depth):
                moved = spin(tiles[side], c - GROUP * k - z)
                new = jnp.where(lane == c, moved if replace else old[z] + moved, old[z])
                ref[slot, pl.ds((z + 1) * rows, rows), :] = new


def tile(ref, i, rows):
    return ref[pl.ds(i * rows, rows), :]


def middle_kernel(
    slots, depth, rows, cols,
    stepped_in, y_low_own, y_up_own, y_low, y_up, lists,
    now, later,
):
    top = (depth + 1) * rows
    for s in range(slots):
        for at in (0, top):
            later[s, pl.ds(at, rows), :] = now[s, pl.ds(at, rows), :]
    later[slots] = jnp.zeros(((depth + 2) * rows, cols), jnp.float32)
    pairs = ((y_low_own, y_low), (y_up_own, y_up))
    own_one = [tile(own, 2, rows) + RATE * tile(got, 0, rows) for own, got in pairs]
    one = [RATE * (tile(got, 2, rows) + RATE * tile(own, 0, rows)) for own, got in pairs]
    y_faces(now, own_one, lists, depth, rows, cols, True)
    step(now, later, slots, depth, rows, cols)
    y_faces(later, one, lists, depth, rows, cols, False)


def last_kernel(
    slots, depth, rows, cols,
    now, later_in, x_low_own, x_up_own, x_low, x_up, c_low, c_up, y_low_own, y_up_own, y_low, y_up, lists,
    later, result,
    last, x_one, x_own_one, x_two, sent,
):
    row, lane = row_and_lane(rows, cols)
    block = LINKS * depth
    last[slots] = jnp.zeros(((depth + 2) * rows, cols), jnp.float32)

    x_one[...] = jnp.zeros(x_one.shape, jnp.float32)
    x_own_one[...] = jnp.zeros(x_own_one.shape, jnp.float32)
    tall_row, tall_lane = row_and_lane(GROUP, cols)
    low_lane, high_lane = tall_lane[:depth] == 0, tall_lane[:depth] == cols - 1
    for face, own, got, corner in ((0, x_low_own, x_low, c_low), (1, x_up_own, x_up, c_up)):
        r, inner_r = (0, 1) if face == 0 else (rows - 1, rows - 2)
        rim_rows = pl.ds(rows + r, depth, stride=rows)
        total = got[pl.ds(3 * block, depth), :]
        ones, own_ones = [], []
        change = jnp.zeros((depth, cols), jnp.float32)
        for k in range(LINKS):
            partial = own[pl.ds(block + k * depth, depth), :]
            one = got[pl.ds(block + k * depth, depth), :] + RATE * own[pl.ds(k * depth, depth), :]
            own_one = partial + RATE * got[pl.ds(k * depth, depth), :]
            total = total + one * one
            change = change + (own_one * own_one - partial * partial)
            x_one[face, pl.ds(k * GROUP + 1, depth), :] = one
            x_own_one[face, pl.ds(k * GROUP + 1, depth), :] = own_one
            ones.append(one)
            own_ones.append(own_one)
        for side in range(2):
            c = 0 if side == 0 else cols - 1
            term = RATE * corner[pl.ds(2 + side, 1), :]
            term = group_sum(term * (2.0 * corner[pl.ds(side, 1), :] + term))
            spread = jnp.where(tall_row == tall_lane, jnp.broadcast_to(term, (GROUP, cols)), 0.0)
            column = jnp.sum(spread, axis=1, keepdims=True)
            total = total + jnp.where(tall_lane == c, column, 0.0)[:depth]

        scaled = 0.15 * change
        own_total = change
        for s in range(slots):
            v = now[s, rim_rows, :]
            own_total = own_total + v * v
            later[s, rim_rows, :] = later[s, rim_rows, :] - scaled * v

        def rim_step(padded, k, one, factor, outer):
            z_sum = padded[face, pl.ds(k * GROUP, depth), :] + padded[face, pl.ds(k * GROUP + 2, depth), :]
            y_sum = jnp.where(low_lane, 0.0, pltpu.roll(one, 1, 1)) + jnp.where(
                high_lane, 0.0, pltpu.roll(one, cols - 1, 1)
            )
            return RATE * (one * (factor + one * one) + (outer + (z_sum + y_sum)))

        factor, own_factor = 4.5 - 1.5 * total, 4.5 - 1.5 * own_total
        for k in range(LINKS):
            inner = pl.ds(2 * block + k * depth, depth)
            x_two[face, pl.ds(k * GROUP, depth), :] = rim_step(x_one, k, ones[k], factor, got[inner, :] + own_ones[k])
            own_two = rim_step(x_own_one, k, own_ones[k], own_factor, own[inner, :] + ones[k])
            slot = lists[face * SPAN + k]
            inner_rows = pl.ds(rows + inner_r, depth, stride=rows)
            beside = later[slot, inner_rows, :] + RATE * RATE * got[pl.ds(k * depth, depth), :]
            later[slot, rim_rows, :] = own_two
            later[slot, inner_rows, :] = beside

    y_two = []
    for side, own, got in ((0, y_low_own, y_low), (1, y_up_own, y_up)):
        own_one = tile(own, 2, rows) + RATE * tile(got, 0, rows)
        one = tile(got, 2, rows) + RATE * tile(own, 0, rows)
        inner = tile(got, 3, rows)
        low = jnp.broadcast_to(c_low[pl.ds(4 + side, 1), :], (rows, cols))
        high = jnp.broadcast_to(c_up[pl.ds(4 + side, 1), :], (rows, cols))
        term = RATE * jnp.where(row == 0, low, jnp.where(row == rows - 1, high, 0.0))
        rest = jnp.where((lane >= LINKS * GROUP) & (lane < (LINKS + 1) * GROUP), inner, 0.0)
        total = group_sum((one * one + rest) + term * (2.0 * tile(got, 4, rows) + term))
        x_sum = jnp.where(row == 0, 0.0, pltpu.roll(one, 1, 0)) + jnp.where(
            row == rows - 1, 0.0, pltpu.roll(one, rows - 1, 0)
        )
        z_sum = spin(one, 1) + spin(one, -1)
        two = RATE * (one * ((4.5 - 1.5 * total) + one * one) + ((inner + own_one) + (x_sum + z_sum)))
        y_two.append(RATE * two)

    step(later, last, slots, depth, rows, cols)
    for face in range(2):
        rim_rows = pl.ds(rows + (0 if face == 0 else rows - 1), depth, stride=rows)
        old = [last[lists[face * SPAN + k], rim_rows, :] for k in range(LINKS)]
        for k in range(LINKS):
            last[lists[face * SPAN + k], rim_rows, :] = old[k] + RATE * x_two[face, pl.ds(k * GROUP, depth), :]
    y_faces(last, y_two, lists, depth, rows, cols, False)
    copy = pltpu.make_async_copy(last.at[pl.ds(0, slots), pl.ds(rows, depth * rows), :], result, sent)
    copy.start()
    copy.wait()


def shifted(block, axis, distance):
    size = lax.axis_size(axis)
    return lax.ppermute(block, axis, [((i - distance) % size, i) for i in range(size)])


def on_device(order_params, grain_ids, channel_maps, zplanes):
    slots, depth, rows, cols = order_params.shape
    f32 = jnp.float32
    shape = jax.ShapeDtypeStruct
    padded = pltpu.VMEM((slots + 1, (depth + 2) * rows, cols), f32)
    x_pack = shape((-(-(3 * LINKS * depth + depth) // rows) * rows, cols), f32)
    y_pack = shape((5 * rows, cols), f32)
    corner_pack = shape((rows, cols), f32)
    vmem = pl.BlockSpec(memory_space=pltpu.VMEM)
    smem = pl.BlockSpec(memory_space=pltpu.SMEM)
    hbm = pl.BlockSpec(memory_space=pltpu.HBM)
    params = pltpu.CompilerParams(vmem_limit_bytes=24 * 1024 * 1024)
    field = order_params.reshape(slots, depth * rows, cols)
    sizes = (slots, depth, rows, cols)

    now, stepped, squares, x_low, x_up, lists = pl.pallas_call(
        functools.partial(first_kernel, *sizes),
        out_shape=[
            padded, padded, pltpu.VMEM((depth * rows, cols), f32), x_pack, x_pack, shape((4 * SPAN,), jnp.int32)
        ],
        in_specs=[hbm] * 4,
        out_specs=[vmem] * 5 + [smem],
        scratch_shapes=[
            pltpu.VMEM(zplanes.shape, jnp.int32),
            pltpu.SMEM(grain_ids.shape, jnp.int32),
            pltpu.SMEM(channel_maps.shape, jnp.int32),
            pltpu.SMEM((2 * (slots + 1),), jnp.int32),
            pltpu.SemaphoreType.DMA((4,)),
        ],
        compiler_params=params,
        name="first_step",
    )(*(pltpu.with_memory_space_constraint(x, pltpu.HBM) for x in (field, zplanes, grain_ids, channel_maps)))

    from_up = shifted(x_low, "gx", -1)
    from_low = shifted(x_up, "gx", 1)

    y_low, y_up = pl.pallas_call(
        functools.partial(y_kernel, *sizes),
        out_shape=[y_pack, y_pack],
        in_specs=[vmem] * 3 + [smem],
        out_specs=[vmem] * 2,
        compiler_params=params,
        name="y_rims",
    )(now, stepped, squares, lists)

    from_right = shifted(y_low, "gy", -1)
    from_left = shifted(y_up, "gy", 1)

    c_low, c_up = pl.pallas_call(
        functools.partial(corner_kernel, rows, cols),
        out_shape=[corner_pack, corner_pack],
        in_specs=[vmem] * 4,
        out_specs=[vmem] * 2,
        compiler_params=params,
        name="corners",
    )(y_low, y_up, from_left, from_right)

    corner_from_up = shifted(c_low, "gx", -1)
    corner_from_low = shifted(c_up, "gx", 1)

    fixed, later = pl.pallas_call(
        functools.partial(middle_kernel, *sizes),
        out_shape=[padded, padded],
        in_specs=[vmem] * 5 + [smem],
        out_specs=[vmem] * 2,
        input_output_aliases={0: 0},
        compiler_params=params,
        name="second_step",
    )(stepped, y_low, y_up, from_left, from_right, lists)

    _, result = pl.pallas_call(
        functools.partial(last_kernel, *sizes),
        out_shape=[padded, shape(field.shape, f32)],
        in_specs=[vmem] * 12 + [smem],
        out_specs=[vmem, hbm],
        scratch_shapes=[padded]
        + [pltpu.VMEM((2, LINKS * GROUP, cols), f32)] * 3
        + [pltpu.SemaphoreType.DMA],
        input_output_aliases={1: 0},
        compiler_params=params,
        name="third_step",
    )(
        fixed, later, x_low, x_up, from_low, from_up, corner_from_low, corner_from_up,
        y_low, y_up, from_left, from_right, lists,
    )
    return result.reshape(order_params.shape)


def solution(mesh):
    in_specs = (
        P(None, None, "gx", "gy"),
        P("gx", "gy", None),
        P("gx", "gy", None, None),
        P(None, "gx", "gy"),
    )
    return jax.shard_map(
        on_device, mesh=mesh, in_specs=in_specs, out_specs=P(None, None, "gx", "gy"), check_vma=False
    )
```

time: 25 us -> 24.1 us (0.964)
  waiting for transfers between devices: 7.81 us -> 3.21 us
  starting transfers between devices: 8.57 us -> 11.4 us
  Pallas kernels: 8.38 us -> 9.21 us
    ppermute x6, waiting for transfers between devices: 7.81 us -> 3.21 us  [shifted(): lax.ppermute(block, axis, [((i - distance) % size, i) for i in range(size)])]
    ppermute x6, starting transfers between devices: 8.57 us -> 11.4 us  [shifted(): lax.ppermute(block, axis, [((i - distance) % size, i) for i in range(size)])]
    pallas_call x1, Pallas kernels: 1.98 us -> 2.8 us  [on_device(): pl.pallas_call(functools.partial(first_kernel, *sizes), out_shape=[padded...]
    pallas_call x3 -> x4, Pallas kernels: 6.4 us -> 6.41 us  [the longest x1 3.05 us: on_device(): pl.pallas_call(functools.partial(last_kernel, *sizes), out_shape=[padded,...]
  transfers between devices with their start and end apart: 6 -> 6, of which waited for: 3 -> 2; matrix products, arithmetic and copies ran while one was open for 0% -> 0% of each run, Pallas kernels for 8% -> 14%
where the time goes in v2:
time: 24.1 us; the launch traced here: 23.9 us
  starting transfers between devices  11.4 us (47%)
  Pallas kernels  9.21 us (38%)
  waiting for transfers between devices  3.21 us (13%)
    ppermute x6, starting transfers between devices, shifted(): lax.ppermute(block, axis, [((i - distance) % size, i) for i in range(size)])  11.4 us
    ppermute x6, waiting for transfers between devices, shifted(): lax.ppermute(block, axis, [((i - distance) % size, i) for i in range(size)])  3.21 us
    pallas_call x1, Pallas kernels, on_device(): pl.pallas_call(functools.partial(last_kernel, *sizes), out_shape=[padded,...  3.05 us
    pallas_call x1, Pallas kernels, on_device(): pl.pallas_call(functools.partial(first_kernel, *sizes), out_shape=[padded...  2.8 us
    pallas_call x1, Pallas kernels, on_device(): pl.pallas_call(functools.partial(middle_kernel, *sizes), out_shape=[padde...  1.82 us
    pallas_call x1, Pallas kernels, on_device(): pl.pallas_call(functools.partial(y_kernel, *sizes), out_shape=[y_pack, y_...  1.54 us
  transfers between devices with their start and end apart: 6, of which 2 were waited for; matrix products, arithmetic and copies ran while one was open for 0% of the time, Pallas kernels for 14%

profile of v2, /device:TPU:0, one launch (start us, length us, event | category | flops | bytes accessed | tf_op | source)
XLA Modules:
  0.0 23.9 jit_solution(10322740942104230516)
XLA Ops:
  0.0 2.8 %first_step.1 = (f32[25,112,128]{2,1,0:T(8,128)S(1)}, f32[25,112,128]{2,1,0:T(8,128)S(1)}, f32[96,128]{1,0:T(8,128)S(1)}, f32[232,128]{1,0:T(8,128)S(1)}, f32[232,128]{1,0:T(8,128)S(1)}, /*index=5*/s32[32]{0:T(128)S(1)}) custom-call(f32[24,96,128]{2,1,0:T(8,128)} %bitcast.2, s32[2,8,128]{2,1,0:T(8,128)} %planes.1, s32[1,1,24]{2,1,0:T(1,128)} %grains.1, ...), custom_call_target="tpu_custom_call" | custom-call | tf_op jit(solution)/shard_map/first_step/pallas_call | solution.py:370
  2.8 6.0 %collective-permute-start.3 = (f32[232,128]{1,0:T(8,128)S(1)}, f32[232,128]{1,0:T(8,128)S(1)}, u32[]{:S(2)}, u32[]{:S(2)}) collective-permute-start(f32[232,128]{1,0:T(8,128)S(1)} %get-tuple-element.26.x_low_own), channel_id=1, source_target_pairs={{4,0},{8,4},{12,8},{16,12},{20,16},{24,20},{28,24},{0,28},{5,1},{9... | collective-permute-start | bytes 356360 | tf_op jit(solution)/shard_map/ppermute | solution.py:352
  8.8 0.0 collective-permute-start.2
  8.8 1.5 %y_rims.1 = (f32[40,128]{1,0:T(8,128)S(1)}, f32[40,128]{1,0:T(8,128)S(1)}) custom-call(f32[25,112,128]{2,1,0:T(8,128)S(1)} %get-tuple-element.19.now, f32[25,112,128]{2,1,0:T(8,128)S(1)} %get-tuple-element.18.stepped.stepped_in, f32[96,128]{1,0:T(8,128)S(1)} %get-tuple-element.20.squares, s32[32]{0:T(128)S(1)} %get-tuple-element.21.lists), custom_call_target="tpu_custom_call" | custom-call | tf_op jit(solution)/shard_map/y_rims/pallas_call | solution.py:391
  10.4 0.7 %collective-permute-start.1 = (f32[40,128]{1,0:T(8,128)S(1)}, f32[40,128]{1,0:T(8,128)S(1)}, u32[]{:S(2)}, u32[]{:S(2)}) collective-permute-start(f32[40,128]{1,0:T(8,128)S(1)} %get-tuple-element.22.y_low_own), channel_id=1, source_target_pairs={{1,0},{2,1},{3,2},{0,3},{5,4},{6,5},{7,6},{4,7},{9,8},{10,9},{11,1... | collective-permute-start | bytes 61448 | tf_op jit(solution)/shard_map/ppermute | solution.py:352
  11.1 0.0 collective-permute-start
  11.1 1.5 %collective-permute-done.1.y_up = f32[40,128]{1,0:T(8,128)S(1)} collective-permute-done((f32[40,128]{1,0:T(8,128)S(1)}, f32[40,128]{1,0:T(8,128)S(1)}, u32[]{:S(2)}, u32[]{:S(2)}) %collective-permute-start.1) | collective-permute-done | bytes 20512 | tf_op jit(solution)/shard_map/ppermute | solution.py:352
  12.5 1.7 %collective-permute-done.y_low = f32[40,128]{1,0:T(8,128)S(1)} collective-permute-done((f32[40,128]{1,0:T(8,128)S(1)}, f32[40,128]{1,0:T(8,128)S(1)}, u32[]{:S(2)}, u32[]{:S(2)}) %collective-permute-start) | collective-permute-done | bytes 20512 | tf_op jit(solution)/shard_map/ppermute | solution.py:352
  14.3 0.0 collective-permute-start.4
  14.3 4.7 %collective-permute-start.5 = (f32[8,128]{1,0:T(8,128)S(1)}, f32[8,128]{1,0:T(8,128)S(1)}, u32[]{:S(2)}, u32[]{:S(2)}) collective-permute-start(f32[8,128]{1,0:T(8,128)S(1)} %get-tuple-element.29), channel_id=1, source_target_pairs={{4,0},{8,4},{12,8},{16,12},{20,16},{24,20},{28,24},{0,28},{5,1},{9... | collective-permute-start | bytes 12296 | tf_op jit(solution)/shard_map/ppermute | solution.py:352
  19.0 1.8 %second_step.1 = (f32[25,112,128]{2,1,0:T(8,128)S(1)}, f32[25,112,128]{2,1,0:T(8,128)S(1)}) custom-call(f32[25,112,128]{2,1,0:T(8,128)S(1)} %get-tuple-element.18.stepped.stepped_in, f32[40,128]{1,0:T(8,128)S(1)} %get-tuple-element.22.y_low_own, f32[40,128]{1,0:T(8,128)S(1)} %get-tuple-element.23.y_up_own, ...), custom_call_target="tpu_custom_call", output_to_operand_aliasing={{0}: (0, {})} | custom-call | tf_op jit(solution)/shard_map/second_step/pallas_call | solution.py:415
  20.8 0.0 collective-permute-done.4.c_low
  20.8 0.0 collective-permute-done.5.c_up
  20.9 0.0 collective-permute-done.3.x_up
  20.9 0.0 collective-permute-done.2.x_low
  20.9 3.0 %third_step.1 = (f32[25,112,128]{2,1,0:T(8,128)S(1)}, f32[24,96,128]{2,1,0:T(8,128)}) custom-call(f32[25,112,128]{2,1,0:T(8,128)S(1)} %get-tuple-element.24.now, f32[25,112,128]{2,1,0:T(8,128)S(1)} %get-tuple-element.25.later_in, f32[232,128]{1,0:T(8,128)S(1)} %get-tuple-element.26.x_low_own, ...), custom_call_target="tpu_custom_call", output_to_operand_aliasing={{0}: (1, {})} | custom-call | tf_op jit(solution)/shard_map/third_step/pallas_call | solution.py:425
  (1 shorter events, 0.0 us)
Async XLA Ops:
  2.8 18.0 %collective-permute-start.3 = (f32[232,128]{1,0:T(8,128)S(1)}, f32[232,128]{1,0:T(8,128)S(1)}, u32[]{:S(2)}, u32[]{:S(2)}) collective-permute-start(f32[232,128]{1,0:T(8,128)S(1)} %get-tuple-element.26.x_low_own), channel_id=1, source_target_pairs={{4,0},{8,4},{12,8},{16,12},{20,16},{24,20},{28,24},{0,28},{5,1},{9... | collective-permute-start | bytes 356360 | tf_op jit(solution)/shard_map/ppermute | solution.py:352
  8.8 12.0 %collective-permute-start.2 = (f32[232,128]{1,0:T(8,128)S(1)}, f32[232,128]{1,0:T(8,128)S(1)}, u32[]{:S(2)}, u32[]{:S(2)}) collective-permute-start(f32[232,128]{1,0:T(8,128)S(1)} %get-tuple-element.27.x_up_own), channel_id=1, source_target_pairs={{28,0},{0,4},{4,8},{8,12},{12,16},{16,20},{20,24},{24,28},{29,1},{... | collective-permute-start | bytes 356360 | tf_op jit(solution)/shard_map/ppermute | solution.py:352
  10.4 2.2 %collective-permute-start.1 = (f32[40,128]{1,0:T(8,128)S(1)}, f32[40,128]{1,0:T(8,128)S(1)}, u32[]{:S(2)}, u32[]{:S(2)}) collective-permute-start(f32[40,128]{1,0:T(8,128)S(1)} %get-tuple-element.22.y_low_own), channel_id=1, source_target_pairs={{1,0},{2,1},{3,2},{0,3},{5,4},{6,5},{7,6},{4,7},{9,8},{10,9},{11,1... | collective-permute-start | bytes 61448 | tf_op jit(solution)/shard_map/ppermute | solution.py:352
  11.1 3.2 %collective-permute-start = (f32[40,128]{1,0:T(8,128)S(1)}, f32[40,128]{1,0:T(8,128)S(1)}, u32[]{:S(2)}, u32[]{:S(2)}) collective-permute-start(f32[40,128]{1,0:T(8,128)S(1)} %get-tuple-element.23.y_up_own), channel_id=1, source_target_pairs={{3,0},{0,1},{1,2},{2,3},{7,4},{4,5},{5,6},{6,7},{11,8},{8,9},{9,10... | collective-permute-start | bytes 61448 | tf_op jit(solution)/shard_map/ppermute | solution.py:352
  14.3 6.6 %collective-permute-start.4 = (f32[8,128]{1,0:T(8,128)S(1)}, f32[8,128]{1,0:T(8,128)S(1)}, u32[]{:S(2)}, u32[]{:S(2)}) collective-permute-start(f32[8,128]{1,0:T(8,128)S(1)} %get-tuple-element.28), channel_id=1, source_target_pairs={{28,0},{0,4},{4,8},{8,12},{12,16},{16,20},{20,24},{24,28},{29,1},{... | collective-permute-start | bytes 12296 | tf_op jit(solution)/shard_map/ppermute | solution.py:352
  14.3 6.6 %collective-permute-start.5 = (f32[8,128]{1,0:T(8,128)S(1)}, f32[8,128]{1,0:T(8,128)S(1)}, u32[]{:S(2)}, u32[]{:S(2)}) collective-permute-start(f32[8,128]{1,0:T(8,128)S(1)} %get-tuple-element.29), channel_id=1, source_target_pairs={{4,0},{8,4},{12,8},{16,12},{20,16},{24,20},{28,24},{0,28},{5,1},{9... | collective-permute-start | bytes 12296 | tf_op jit(solution)/shard_map/ppermute | solution.py:352

commit v3 on v2

v3 whole, which is shorter than its diff:
```python
import functools

import jax
import jax.numpy as jnp
from jax import lax
from jax.experimental import pallas as pl
from jax.experimental.pallas import tpu as pltpu
from jax.sharding import PartitionSpec as P


LINKS = 6
SPAN = 8
GROUP = 16
RATE = 0.1
UNROLL = 4


def row_and_lane(rows, cols):
    row = lax.broadcasted_iota(jnp.int32, (rows, cols), 0)
    lane = lax.broadcasted_iota(jnp.int32, (rows, cols), 1)
    return row, lane


def spin(tile, amount):
    cols = tile.shape[1]
    amount = amount % cols
    return tile if amount == 0 else pltpu.roll(tile, amount, 1)


def group_sum(tile):
    shift = GROUP
    while shift < tile.shape[1]:
        tile = tile + spin(tile, shift)
        shift *= 2
    return tile


def step(src, dst, slots, depth, rows, cols, squares=None, wait=None):
    row, lane = row_and_lane(rows, cols)
    first_row, last_row = row == 0, row == rows - 1
    first_lane, last_lane = lane == 0, lane == cols - 1

    def add(parts, s, term):
        parts[s % 4] = term if parts[s % 4] is None else parts[s % 4] + term

    def total(parts):
        return (parts[0] + parts[1]) + (parts[2] + parts[3])

    def at(z):
        return pl.ds(pl.multiple_of((z + 1) * rows, rows), rows)

    def layer(z, factor):
        following, parts = [None] * 4, [None] * 4
        for s in range(slots):
            v, below, above = src[s, at(z), :], src[s, at(z - 1), :], src[s, at(z + 1), :]
            add(following, s, above * above)
            x_sum = jnp.where(first_row, 0.0, pltpu.roll(v, 1, 0)) + jnp.where(
                last_row, 0.0, pltpu.roll(v, rows - 1, 0)
            )
            y_sum = jnp.where(first_lane, 0.0, pltpu.roll(v, 1, 1)) + jnp.where(
                last_lane, 0.0, pltpu.roll(v, cols - 1, 1)
            )
            new = RATE * (v * (factor + v * v) + ((x_sum + y_sum) + (below + above)))
            dst[s, at(z), :] = new
            if squares is not None:
                add(parts, s, new * new)
        if squares is not None:
            squares[pl.ds(pl.multiple_of(z * rows, rows), rows), :] = total(parts)
        return 4.5 - 1.5 * total(following)

    def layers(i, factor):
        if wait is not None:
            pl.when(i + 1 < depth // UNROLL)(lambda: wait(i + 1))
        for j in range(UNROLL):
            factor = layer(i * UNROLL + j, factor)
        return factor

    first = [None] * 4
    for s in range(slots):
        v = src[s, at(0), :]
        add(first, s, v * v)
    lax.fori_loop(0, depth // UNROLL, layers, 4.5 - 1.5 * total(first))


def gather_columns(tile_of, c, depth, rows, cols, beside=0):
    _, lane = row_and_lane(rows, cols)
    result, other = jnp.zeros((rows, cols), jnp.float32), jnp.zeros((rows, cols), jnp.float32)
    for k in range(LINKS):
        near, far = jnp.zeros_like(result), jnp.zeros_like(other)
        for z in range(depth):
            place = GROUP * k + z
            moved = spin(tile_of(k, z), place - c)
            near = jnp.where(lane == place, moved, near)
            if beside:
                far = jnp.where(lane == (place + beside) % cols, moved, far)
        result = result + near
        other = other + far
    return result, spin(other, -beside)


def first_kernel(
    slots, depth, rows, cols,
    field, planes, grains, maps,
    now, stepped, squares, x_up, lists,
    planes_in, grains_in, maps_in, inverse, arrived,
):
    copies = [
        pltpu.make_async_copy(maps, maps_in, arrived.at[0]),
        pltpu.make_async_copy(grains, grains_in, arrived.at[1]),
        pltpu.make_async_copy(planes, planes_in, arrived.at[2]),
    ]
    part = UNROLL * rows

    def field_part(i):
        to = pl.ds(pl.multiple_of(i * part + rows, rows), part)
        source = field.at[:, pl.ds(pl.multiple_of(i * part, rows), part), :]
        return pltpu.make_async_copy(source, now.at[pl.ds(0, slots), to, :], arrived.at[3 + i])

    for copy in copies:
        copy.start()
    for i in range(depth // UNROLL):
        field_part(i).start()
    for ref in (now, stepped):
        ref[slots] = jnp.zeros(((depth + 2) * rows, cols), jnp.float32)
    for face in range(4):
        for place in range(SPAN):
            lists[face * SPAN + place] = slots
    for t in range(slots + 1):
        inverse[t] = slots
        inverse[slots + 1 + t] = slots

    copies[0].wait()
    for s in range(slots):
        for face in (0, 2):
            partner = maps_in[0, 0, face, s]
            inverse[face // 2 * (slots + 1) + jnp.where(partner >= 0, partner, slots)] = s
    counts = [jnp.int32(face * SPAN) for face in range(4)]
    for s in range(slots):
        partners = [maps_in[0, 0, face, s] for face in range(4)]
        best = jnp.maximum(jnp.maximum(partners[0], partners[1]), jnp.maximum(partners[2], partners[3]))
        lists[4 * SPAN + s] = (best >= 0).astype(jnp.int32)
        for face in range(4):
            if face in (1, 3):
                valid = partners[face] >= 0
                slot = jnp.where(valid, s, slots)
            else:
                slot = inverse[face // 2 * (slots + 1) + s]
                valid = slot < slots
            lists[counts[face]] = slot
            counts[face] = counts[face] + valid.astype(jnp.int32)

    top = (depth + 1) * rows
    copies[1].wait()
    copies[2].wait()
    for s in range(slots):
        grain = grains_in[0, 0, s]
        below = jnp.where(planes_in[0] == grain, 1.0, 0.0)
        above = jnp.where(planes_in[1] == grain, 1.0, 0.0)
        for ref in (now, stepped):
            ref[s, pl.ds(0, rows), :] = below
            ref[s, pl.ds(top, rows), :] = above
    field_part(0).wait()

    step(now, stepped, slots, depth, rows, cols, squares, lambda i: field_part(i).wait())
    pack_x(1, now, stepped, squares, lists, x_up, depth, rows, cols)


def x_low_kernel(depth, rows, cols, now, stepped, squares, lists, x_low):
    pack_x(0, now, stepped, squares, lists, x_low, depth, rows, cols)


def pack_x(face, now, stepped, squares, lists, out, depth, rows, cols):
    block = LINKS * depth
    edge_row, edge_lane = row_and_lane(depth, cols)
    top = (depth + 1) * rows
    r, inner_r = (0, 1) if face == 0 else (rows - 1, rows - 2)
    rim_rows = pl.ds(rows + r, depth, stride=rows)
    rest = squares[pl.ds(r, depth, stride=rows), :]
    for k in range(LINKS):
        slot = lists[face * SPAN + k]
        partial = stepped[slot, rim_rows, :]
        inner = stepped[slot, pl.ds(rows + inner_r, depth, stride=rows), :]
        below = jnp.broadcast_to(now[slot, pl.ds(r, 1), :], (depth, cols))
        above = jnp.broadcast_to(now[slot, pl.ds(top + r, 1), :], (depth, cols))
        inner = inner + jnp.where(edge_row == 0, below, jnp.where(edge_row == depth - 1, above, 0.0))
        rest = rest - partial * partial
        out[pl.ds(k * depth, depth), :] = now[slot, rim_rows, :]
        out[pl.ds(block + k * depth, depth), :] = partial
        out[pl.ds(2 * block + k * depth, depth), :] = inner
    out[pl.ds(3 * block + depth, depth), :] = rest
    corners = jnp.zeros((depth, cols), jnp.float32)
    for i, ref in enumerate((stepped, now)):
        for side in range(2):
            for k in range(LINKS):
                place = (2 * i + side) * LINKS + k
                moved = spin(ref[lists[(2 + side) * SPAN + k], rim_rows, :], place - side * (cols - 1))
                corners = jnp.where(edge_lane == place, moved, corners)
    out[pl.ds(3 * block, depth), :] = corners
    end = 3 * block + 2 * depth
    if out.shape[0] > end:
        out[pl.ds(end, out.shape[0] - end), :] = jnp.zeros((out.shape[0] - end, cols), jnp.float32)


def y_kernel(slots, depth, rows, cols, now, stepped, squares, lists, y_low, y_up):
    top = (depth + 1) * rows
    _, lane = row_and_lane(rows, cols)
    for side, out in ((0, y_low), (1, y_up)):
        c, inward = (0, 1) if side == 0 else (cols - 1, -1)
        base = (2 + side) * SPAN
        rim, _ = gather_columns(
            lambda k, z: now[lists[base + k], pl.ds((z + 1) * rows, rows), :], c, depth, rows, cols
        )
        partial, inner = gather_columns(
            lambda k, z: stepped[lists[base + k], pl.ds((z + 1) * rows, rows), :], c, depth, rows, cols, beside=inward
        )
        for k in range(LINKS):
            for z, at in ((0, 0), (depth - 1, top)):
                place = GROUP * k + z
                frozen = spin(now[lists[base + k], pl.ds(at, rows), :], place - c)
                inner = inner + jnp.where(lane == place, frozen, 0.0)
        total = jnp.zeros((rows, cols), jnp.float32)
        for z in range(depth):
            place = LINKS * GROUP + z
            total = jnp.where(lane == place, spin(tile(squares, z, rows), place - c), total)
        inner = jnp.where(in_last_group(lane), total - group_sum(partial * partial), inner)
        out[pl.ds(0, rows), :] = rim
        out[pl.ds(rows, rows), :] = partial
        out[pl.ds(2 * rows, rows), :] = inner


def in_last_group(lane):
    return (lane >= LINKS * GROUP) & (lane < (LINKS + 1) * GROUP)


def tile(ref, i, rows):
    return ref[pl.ds(i * rows, rows), :]


def y_faces(ref, tiles, lists, depth, rows, cols, replace=False, done=None):
    _, lane = row_and_lane(rows, cols)
    for k in range(LINKS):
        for side in range(2):
            c = side * (cols - 1)
            slot = lists[(2 + side) * SPAN + k]
            ats = [pl.ds((z + 1) * rows, rows) for z in range(depth)]
            old = [ref[slot, at, :] for at in ats]
            for z in range(depth):
                moved = spin(tiles[side], c - GROUP * k - z)
                ref[slot, ats[z], :] = jnp.where(lane == c, moved if replace else old[z] + moved, old[z])
            if done is not None:
                done(slot)


def second_kernel(
    slots, depth, rows, cols, stepped_in, y_low_own, y_up_own, y_low, y_up, lists, now, later
):
    for s in range(slots):
        for at in (0, (depth + 1) * rows):
            later[s, pl.ds(at, rows), :] = now[s, pl.ds(at, rows), :]
    later[slots] = jnp.zeros(((depth + 2) * rows, cols), jnp.float32)
    pairs = ((y_low_own, y_low), (y_up_own, y_up))
    own_one = [tile(own, 1, rows) + RATE * tile(got, 0, rows) for own, got in pairs]
    one = [RATE * (tile(got, 1, rows) + RATE * tile(own, 0, rows)) for own, got in pairs]
    y_faces(now, own_one, lists, depth, rows, cols, replace=True)
    step(now, later, slots, depth, rows, cols)
    y_faces(later, one, lists, depth, rows, cols)


def x_rims(own, got, k, depth):
    zero, one = pl.ds(k * depth, depth), pl.ds((LINKS + k) * depth, depth)
    return own[one, :] + RATE * got[zero, :], got[one, :] + RATE * own[zero, :]


def change_kernel(depth, cols, own, got, before, out):
    change = jnp.zeros((depth, cols), jnp.float32)
    for k in range(LINKS):
        own_one, _ = x_rims(own, got, k, depth)
        partial = own[pl.ds((LINKS + k) * depth, depth), :]
        change = change + (own_one * own_one - partial * partial)
    out[pl.ds(0, depth), :] = change
    out[pl.ds(depth, depth), :] = got[pl.ds(3 * LINKS * depth, depth), :]


def both_changes_kernel(depth, cols, own, got, before, out):
    out[pl.ds(0, 2 * depth), :] = before[...]
    change_kernel(depth, cols, own, got, None, out.at[pl.ds(2 * depth, 2 * depth), :])


def x_rim_step(padded, face, k, one, factor, outer, depth, cols):
    _, lane = row_and_lane(depth, cols)
    z_sum = padded[face, pl.ds(k * GROUP, depth), :] + padded[face, pl.ds(k * GROUP + 2, depth), :]
    y_sum = jnp.where(lane == 0, 0.0, pltpu.roll(one, 1, 1)) + jnp.where(
        lane == cols - 1, 0.0, pltpu.roll(one, cols - 1, 1)
    )
    return RATE * (one * (factor + one * one) + (outer + (z_sum + y_sum)))


def y_rim_step(one, factor, outer):
    rows, cols = one.shape
    row, _ = row_and_lane(rows, cols)
    x_sum = jnp.where(row == 0, 0.0, pltpu.roll(one, 1, 0)) + jnp.where(
        row == rows - 1, 0.0, pltpu.roll(one, rows - 1, 0)
    )
    z_sum = spin(one, 1) + spin(one, -1)
    return RATE * (one * (factor + one * one) + (outer + (x_sum + z_sum)))


def third_kernel(
    slots, depth, rows, cols,
    now, later_in, x_low_own, x_up_own, x_low, x_up, changes, lists,
    later, last,
    x_own_one,
):
    last[slots] = jnp.zeros(((depth + 2) * rows, cols), jnp.float32)
    x_own_one[...] = jnp.zeros(x_own_one.shape, jnp.float32)
    for face, own, got in ((0, x_low_own, x_low), (1, x_up_own, x_up)):
        r, inner_r = (0, 1) if face == 0 else (rows - 1, rows - 2)
        rim_rows = pl.ds(rows + r, depth, stride=rows)
        inner_rows = pl.ds(rows + inner_r, depth, stride=rows)
        rims = [x_rims(own, got, k, depth) for k in range(LINKS)]
        for k in range(LINKS):
            x_own_one[face, pl.ds(k * GROUP + 1, depth), :] = rims[k][0]

        change = changes[pl.ds(2 * face * depth, depth), :]
        scaled = 0.15 * change
        parts = [change, None, None, None]
        for first in range(0, slots, 4):
            rim = [now[first + i, rim_rows, :] for i in range(4)]
            old = [later[first + i, rim_rows, :] for i in range(4)]
            for i in range(4):
                parts[i] = rim[i] * rim[i] if parts[i] is None else parts[i] + rim[i] * rim[i]
                later[first + i, rim_rows, :] = old[i] - scaled * rim[i]
        factor = 4.5 - 1.5 * ((parts[0] + parts[1]) + (parts[2] + parts[3]))

        beside = [later[lists[face * SPAN + k], inner_rows, :] for k in range(LINKS)]
        two = []
        for k in range(LINKS):
            outer = own[pl.ds((2 * LINKS + k) * depth, depth), :] + rims[k][1]
            two.append(x_rim_step(x_own_one, face, k, rims[k][0], factor, outer, depth, cols))
        for k in range(LINKS):
            slot = lists[face * SPAN + k]
            later[slot, rim_rows, :] = two[k]
            later[slot, inner_rows, :] = beside[k] + RATE * RATE * got[pl.ds(k * depth, depth), :]

    step(later, last, slots, depth, rows, cols)


def last_kernel(
    slots, depth, rows, cols,
    last_in, x_low_own, x_up_own, x_low, x_up, y_low_own, y_up_own, y_low, y_up, from_left, from_right,
    lists,
    last, result,
    x_one, sent,
):
    whole = last.at[pl.ds(0, slots), pl.ds(rows, depth * rows), :]

    def send(slot):
        pltpu.make_async_copy(last.at[slot, pl.ds(rows, depth * rows), :], result.at[slot], sent).start()

    def send_linked(slot):
        pl.when(slot < slots)(lambda: send(slot))

    for s in range(slots):
        pl.when(lists[4 * SPAN + s] == 0)(functools.partial(send, s))

    row, lane = row_and_lane(rows, cols)
    _, flat_lane = row_and_lane(depth, cols)
    tall_row, tall_lane = row_and_lane(GROUP, cols)
    block = LINKS * depth
    passed_on = (from_left, from_right)
    x_one[...] = jnp.zeros(x_one.shape, jnp.float32)
    for face, own, got in ((0, x_low_own, x_low), (1, x_up_own, x_up)):
        rims = [x_rims(own, got, k, depth) for k in range(LINKS)]
        total = got[pl.ds(3 * block + depth, depth), :]
        for k in range(LINKS):
            total = total + rims[k][1] * rims[k][1]
            x_one[face, pl.ds(k * GROUP + 1, depth), :] = rims[k][1]
        corners = got[pl.ds(3 * block, depth), :]
        for side in range(2):
            place = side * LINKS
            came_from = (3 - side) * LINKS
            term = RATE * spin(passed_on[side][pl.ds((2 * face + 1) * depth, depth), :], place - came_from)
            term = term * (2.0 * corners + term)
            term = jnp.where((flat_lane >= place) & (flat_lane < place + LINKS), term, 0.0)
            column = jnp.sum(term, axis=1, keepdims=True)
            total = total + jnp.where(flat_lane == side * (cols - 1), column, 0.0)
        factor = 4.5 - 1.5 * total
        rim_rows = pl.ds(rows + (0 if face == 0 else rows - 1), depth, stride=rows)
        old = [last[lists[face * SPAN + k], rim_rows, :] for k in range(LINKS)]
        for k in range(LINKS):
            outer = got[pl.ds(2 * block + k * depth, depth), :] + rims[k][0]
            two = x_rim_step(x_one, face, k, rims[k][1], factor, outer, depth, cols)
            last[lists[face * SPAN + k], rim_rows, :] = old[k] + RATE * two
        for k in range(LINKS):
            send_linked(lists[face * SPAN + k])

    twos = []
    for side, own, got in ((0, y_low_own, y_low), (1, y_up_own, y_up)):
        c = side * (cols - 1)
        own_one = tile(own, 1, rows) + RATE * tile(got, 0, rows)
        one = tile(got, 1, rows) + RATE * tile(own, 0, rows)
        inner = tile(got, 2, rows)
        squares = one * one + jnp.where(in_last_group(lane), inner, 0.0)
        for face in range(2):
            change = passed_on[side][pl.ds(2 * face * depth, depth), :]
            column = jnp.sum(jnp.where(flat_lane == cols - 1 - c, change, 0.0), axis=1, keepdims=True)
            line = jnp.sum(jnp.where(tall_row == tall_lane, 1.0, 0.0)[:depth] * column, axis=0, keepdims=True)
            at_row = row == (0 if face == 0 else rows - 1)
            squares = squares + jnp.where(at_row, jnp.broadcast_to(line, (rows, cols)), 0.0)
        factor = 4.5 - 1.5 * group_sum(squares)
        twos.append(RATE * y_rim_step(one, factor, inner + own_one))
    y_faces(last, twos, lists, depth, rows, cols, done=send_linked)
    pltpu.make_async_copy(whole, result, sent).wait()


def shifted(block, axis, distance):
    size = lax.axis_size(axis)
    return lax.ppermute(block, axis, [((i - distance) % size, i) for i in range(size)])


def on_device(order_params, grain_ids, channel_maps, zplanes):
    slots, depth, rows, cols = order_params.shape
    f32 = jnp.float32
    shape = jax.ShapeDtypeStruct
    padded = pltpu.VMEM((slots + 1, (depth + 2) * rows, cols), f32)
    planes = pltpu.VMEM((depth * rows, cols), f32)
    x_pack = shape((-(-(3 * LINKS + 2) * depth // rows) * rows, cols), f32)
    y_pack = shape((3 * rows, cols), f32)
    rims = pltpu.VMEM((2, LINKS * GROUP, cols), f32)
    vmem = pl.BlockSpec(memory_space=pltpu.VMEM)
    smem = pl.BlockSpec(memory_space=pltpu.SMEM)
    hbm = pl.BlockSpec(memory_space=pltpu.HBM)
    params = pltpu.CompilerParams(vmem_limit_bytes=24 * 1024 * 1024)
    field = order_params.reshape(slots, depth * rows, cols)
    sizes = (slots, depth, rows, cols)
    work = pl.CostEstimate(flops=20 * field.size, bytes_accessed=2 * 4 * field.size, transcendentals=0)

    now, stepped, squares, x_up, lists = pl.pallas_call(
        functools.partial(first_kernel, *sizes),
        out_shape=[padded, padded, planes, x_pack, shape((4 * SPAN + slots,), jnp.int32)],
        in_specs=[hbm] * 4,
        out_specs=[vmem] * 4 + [smem],
        scratch_shapes=[
            pltpu.VMEM(zplanes.shape, jnp.int32),
            pltpu.SMEM(grain_ids.shape, jnp.int32),
            pltpu.SMEM(channel_maps.shape, jnp.int32),
            pltpu.SMEM((2 * (slots + 1),), jnp.int32),
            pltpu.SemaphoreType.DMA((3 + depth // UNROLL,)),
        ],
        compiler_params=params,
        name="first_step",
    )(*(pltpu.with_memory_space_constraint(x, pltpu.HBM) for x in (field, zplanes, grain_ids, channel_maps)))

    from_low = shifted(x_up, "gx", 1)

    x_low = pl.pallas_call(
        functools.partial(x_low_kernel, depth, rows, cols),
        out_shape=x_pack,
        in_specs=[vmem] * 3 + [smem],
        out_specs=vmem,
        compiler_params=params,
        cost_estimate=work,
        name="x_low_rims",
    )(now, stepped, squares, lists)

    from_up = shifted(x_low, "gx", -1)

    y_low, y_up = pl.pallas_call(
        functools.partial(y_kernel, *sizes),
        out_shape=[y_pack, y_pack],
        in_specs=[vmem] * 3 + [smem],
        out_specs=[vmem] * 2,
        compiler_params=params,
        cost_estimate=work,
        name="y_rims",
    )(now, stepped, squares, lists)

    from_right = shifted(y_low, "gy", -1)
    from_left = shifted(y_up, "gy", 1)

    fixed, later = pl.pallas_call(
        functools.partial(second_kernel, *sizes),
        out_shape=[padded, padded],
        in_specs=[vmem] * 5 + [smem],
        out_specs=[vmem] * 2,
        input_output_aliases={0: 0},
        compiler_params=params,
        cost_estimate=work,
        name="second_step",
    )(stepped, y_low, y_up, from_left, from_right, lists)

    changes = later
    for body, own, got, name in (
        (change_kernel, x_low, from_low, "corners_low"),
        (both_changes_kernel, x_up, from_up, "corners_up"),
    ):
        changes = pl.pallas_call(
            functools.partial(body, depth, cols),
            out_shape=shape(((2 if body is change_kernel else 4) * depth, cols), f32),
            in_specs=[vmem] * 3,
            out_specs=vmem,
            compiler_params=params,
            name=name,
        )(own, got, changes)

    changes_from_right = shifted(changes, "gy", -1)
    changes_from_left = shifted(changes, "gy", 1)

    _, last = pl.pallas_call(
        functools.partial(third_kernel, *sizes),
        out_shape=[padded, padded],
        in_specs=[vmem] * 7 + [smem],
        out_specs=[vmem] * 2,
        scratch_shapes=[rims],
        input_output_aliases={1: 0},
        compiler_params=params,
        name="third_step",
    )(
        fixed, later, x_low, x_up, from_low, from_up, changes, lists,
    )

    _, result = pl.pallas_call(
        functools.partial(last_kernel, *sizes),
        out_shape=[padded, shape(field.shape, f32)],
        in_specs=[vmem] * 11 + [smem],
        out_specs=[vmem, hbm],
        scratch_shapes=[rims, pltpu.SemaphoreType.DMA],
        input_output_aliases={0: 0},
        compiler_params=params,
        name="last_rims",
    )(
        last, x_low, x_up, from_low, from_up,
        y_low, y_up, from_left, from_right, changes_from_left, changes_from_right, lists,
    )
    return result.reshape(order_params.shape)


def solution(mesh):
    in_specs = (
        P(None, None, "gx", "gy"),
        P("gx", "gy", None),
        P("gx", "gy", None, None),
        P(None, "gx", "gy"),
    )
    return jax.shard_map(
        on_device, mesh=mesh, in_specs=in_specs, out_specs=P(None, None, "gx", "gy"), check_vma=False
    )
```

time: 24.1 us -> 22.1 us (0.917)
  starting transfers between devices: 11.4 us -> 7.39 us
  waiting for transfers between devices: 3.21 us -> 4.49 us
  Pallas kernels: 9.21 us -> 9.95 us
    ppermute x6, starting transfers between devices: 11.4 us -> 7.39 us  [shifted(): lax.ppermute(block, axis, [((i - distance) % size, i) for i in range(size)])]
    pallas_call x2 -> x5, Pallas kernels: 1.82 us -> 4.17 us  [the longest x1 1.82 us: on_device(): pl.pallas_call(functools.partial(second_kernel, *sizes), out_shape=[padde...]
    ppermute x6, waiting for transfers between devices: 3.21 us -> 4.49 us  [shifted(): lax.ppermute(block, axis, [((i - distance) % size, i) for i in range(size)])]
    pallas_call x1, Pallas kernels: 3.05 us -> 1.8 us  [on_device(): pl.pallas_call(functools.partial(last_kernel, *sizes), out_shape=[padded,...]
    pallas_call x1, Pallas kernels: 1.54 us -> 1.26 us  [on_device(): pl.pallas_call(functools.partial(y_kernel, *sizes), out_shape=[y_pack, y_...]
  transfers between devices with their start and end apart: 6 -> 6, of which waited for: 2 -> 3; matrix products, arithmetic and copies ran while one was open for 0% -> 0% of each run, Pallas kernels for 14% -> 25%
where the time goes in v3:
time: 22.1 us; the launch traced here: 21.9 us
  Pallas kernels  9.95 us (45%)
  starting transfers between devices  7.39 us (33%)
  waiting for transfers between devices  4.49 us (20%)
    ppermute x6, starting transfers between devices, shifted(): lax.ppermute(block, axis, [((i - distance) % size, i) for i in range(size)])  7.39 us
    ppermute x6, waiting for transfers between devices, shifted(): lax.ppermute(block, axis, [((i - distance) % size, i) for i in range(size)])  4.49 us
    pallas_call x1, Pallas kernels, on_device(): pl.pallas_call(functools.partial(first_kernel, *sizes), out_shape=[padded...  2.71 us
    pallas_call x1, Pallas kernels, on_device(): pl.pallas_call(functools.partial(second_kernel, *sizes), out_shape=[padde...  1.82 us
    pallas_call x1, Pallas kernels, on_device(): pl.pallas_call(functools.partial(last_kernel, *sizes), out_shape=[padded,...  1.8 us
    pallas_call x1, Pallas kernels, on_device(): pl.pallas_call(functools.partial(third_kernel, *sizes), out_shape=[padded...  1.65 us
    pallas_call x1, Pallas kernels, on_device(): pl.pallas_call(functools.partial(y_kernel, *sizes), out_shape=[y_pack, y_...  1.26 us
    pallas_call x1, Pallas kernels, on_device(): pl.pallas_call(functools.partial(x_low_kernel, depth, rows, cols), out_sh...  0.66 us
  transfers between devices with their start and end apart: 6, of which 3 were waited for; matrix products, arithmetic and copies ran while one was open for 0% of the time, Pallas kernels for 25%

profile of v3, /device:TPU:0, one launch (start us, length us, event | category | flops | bytes accessed | tf_op | source)
XLA Modules:
  0.0 21.9 jit_solution(12631427798335725486)
XLA Ops:
  0.0 2.7 %first_step.1 = (f32[25,112,128]{2,1,0:T(8,128)S(1)}, f32[25,112,128]{2,1,0:T(8,128)S(1)}, f32[96,128]{1,0:T(8,128)S(1)}, f32[240,128]{1,0:T(8,128)S(1)}, s32[56]{0:T(128)S(1)}) custom-call(f32[24,96,128]{2,1,0:T(8,128)} %bitcast.2, s32[2,8,128]{2,1,0:T(8,128)} %planes.1, s32[1,1,24]{2,1,0:T(1,128)} %grains.1, s32[1,1,4,24]{3,2,1,0:T(4,128)} %maps.1), custom_call_target="tpu_custom_call" | custom-call | tf_op jit(solution)/shard_map/first_step/pallas_call | solution.py:438
  2.7 3.0 %collective-permute-start.2 = (f32[240,128]{1,0:T(8,128)S(1)}, f32[240,128]{1,0:T(8,128)S(1)}, u32[]{:S(2)}, u32[]{:S(2)}) collective-permute-start(f32[240,128]{1,0:T(8,128)S(1)} %get-tuple-element.24.own.x_up_own), channel_id=1, source_target_pairs={{28,0},{0,4},{4,8},{8,12},{12,16},{16,20},{20,24},{24,28},{29,1},{... | collective-permute-start | bytes 368648 | tf_op jit(solution)/shard_map/ppermute | solution.py:418
  5.7 0.7 %x_low_rims.1.own.x_low_own = f32[240,128]{1,0:T(8,128)S(1)} custom-call(f32[25,112,128]{2,1,0:T(8,128)S(1)} %get-tuple-element.17.now, f32[25,112,128]{2,1,0:T(8,128)S(1)} %get-tuple-element.16.stepped.stepped_in, f32[96,128]{1,0:T(8,128)S(1)} %get-tuple-element.18.squares, s32[56]{0:T(128)S(1)} %get-tuple-element.19.lists), custom_call_target="tpu_custom_call" | custom-call | flops 5898240 | bytes 2359296 | tf_op jit(solution)/shard_map/x_low_rims/pallas_call | solution.py:456
  6.4 3.1 %collective-permute-start.3 = (f32[240,128]{1,0:T(8,128)S(1)}, f32[240,128]{1,0:T(8,128)S(1)}, u32[]{:S(2)}, u32[]{:S(2)}) collective-permute-start(f32[240,128]{1,0:T(8,128)S(1)} %x_low_rims.1.own.x_low_own), channel_id=1, source_target_pairs={{4,0},{8,4},{12,8},{16,12},{20,16},{24,20},{28,24},{0,28},{5,1},{9... | collective-permute-start | bytes 368648 | tf_op jit(solution)/shard_map/ppermute | solution.py:418
  9.5 1.3 %y_rims.1 = (f32[24,128]{1,0:T(8,128)S(1)}, f32[24,128]{1,0:T(8,128)S(1)}) custom-call(f32[25,112,128]{2,1,0:T(8,128)S(1)} %get-tuple-element.17.now, f32[25,112,128]{2,1,0:T(8,128)S(1)} %get-tuple-element.16.stepped.stepped_in, f32[96,128]{1,0:T(8,128)S(1)} %get-tuple-element.18.squares, s32[56]{0:T(128)S(1)} %get-tuple-element.19.lists), custom_call_target="tpu_custom_call" | custom-call | flops 5898240 | bytes 2359296 | tf_op jit(solution)/shard_map/y_rims/pallas_call | solution.py:468
  10.8 0.7 %collective-permute-start.1 = (f32[24,128]{1,0:T(8,128)S(1)}, f32[24,128]{1,0:T(8,128)S(1)}, u32[]{:S(2)}, u32[]{:S(2)}) collective-permute-start(f32[24,128]{1,0:T(8,128)S(1)} %get-tuple-element.20.y_low_own), channel_id=1, source_target_pairs={{1,0},{2,1},{3,2},{0,3},{5,4},{6,5},{7,6},{4,7},{9,8},{10,9},{11,1... | collective-permute-start | bytes 36872 | tf_op jit(solution)/shard_map/ppermute | solution.py:418
  11.5 0.0 collective-permute-start
  11.5 1.4 %collective-permute-done.1.y_up = f32[24,128]{1,0:T(8,128)S(1)} collective-permute-done((f32[24,128]{1,0:T(8,128)S(1)}, f32[24,128]{1,0:T(8,128)S(1)}, u32[]{:S(2)}, u32[]{:S(2)}) %collective-permute-start.1) | collective-permute-done | bytes 12320 | tf_op jit(solution)/shard_map/ppermute | solution.py:418
  12.9 1.7 %collective-permute-done.y_low = f32[24,128]{1,0:T(8,128)S(1)} collective-permute-done((f32[24,128]{1,0:T(8,128)S(1)}, f32[24,128]{1,0:T(8,128)S(1)}, u32[]{:S(2)}, u32[]{:S(2)}) %collective-permute-start) | collective-permute-done | bytes 12320 | tf_op jit(solution)/shard_map/ppermute | solution.py:418
  14.6 1.8 %second_step.1 = (f32[25,112,128]{2,1,0:T(8,128)S(1)}, f32[25,112,128]{2,1,0:T(8,128)S(1)}) custom-call(f32[25,112,128]{2,1,0:T(8,128)S(1)} %get-tuple-element.16.stepped.stepped_in, f32[24,128]{1,0:T(8,128)S(1)} %get-tuple-element.20.y_low_own, f32[24,128]{1,0:T(8,128)S(1)} %get-tuple-element.21.y_up_own, ...), custom_call_target="tpu_custom_call", output_to_operand_aliasing={{0}: (0, {})} | custom-call | flops 5898240 | bytes 2359296 | tf_op jit(solution)/shard_map/second_step/pallas_call | solution.py:481
  16.4 0.0 collective-permute-done.2.got.x_low
  16.5 0.0 collective-permute-done.3.got.x_up
  16.5 0.4 %collective-permute-start.5 = (f32[48,128]{1,0:T(8,128)S(1)}, f32[48,128]{1,0:T(8,128)S(1)}, u32[]{:S(2)}, u32[]{:S(2)}) collective-permute-start(f32[48,128]{1,0:T(8,128)S(1)} %corners_up.1.changes), channel_id=1, source_target_pairs={{1,0},{2,1},{3,2},{0,3},{5,4},{6,5},{7,6},{4,7},{9,8},{10,9},{11,1... | collective-permute-start | bytes 73736 | tf_op jit(solution)/shard_map/ppermute | solution.py:418
  16.9 0.2 collective-permute-start.4
  17.1 1.7 %third_step.1 = (f32[25,112,128]{2,1,0:T(8,128)S(1)}, f32[25,112,128]{2,1,0:T(8,128)S(1)}) custom-call(f32[25,112,128]{2,1,0:T(8,128)S(1)} %get-tuple-element.22.now, f32[25,112,128]{2,1,0:T(8,128)S(1)} %get-tuple-element.23.before.later_in, f32[240,128]{1,0:T(8,128)S(1)} %x_low_rims.1.own.x_low_own, ...), custom_call_target="tpu_custom_call", output_to_operand_aliasing={{0}: (1, {})} | custom-call | tf_op jit(solution)/shard_map/third_step/pallas_call | solution.py:509
  18.7 0.0 collective-permute-done.5.from_right
  18.7 1.4 %collective-permute-done.4.from_left = f32[48,128]{1,0:T(8,128)S(1)} collective-permute-done((f32[48,128]{1,0:T(8,128)S(1)}, f32[48,128]{1,0:T(8,128)S(1)}, u32[]{:S(2)}, u32[]{:S(2)}) %collective-permute-start.4) | collective-permute-done | bytes 24608 | tf_op jit(solution)/shard_map/ppermute | solution.py:418
  20.1 1.8 %last_rims.1 = (f32[25,112,128]{2,1,0:T(8,128)S(1)}, f32[24,96,128]{2,1,0:T(8,128)}) custom-call(f32[25,112,128]{2,1,0:T(8,128)S(1)} %get-tuple-element.25.last_in, f32[240,128]{1,0:T(8,128)S(1)} %x_low_rims.1.own.x_low_own, f32[240,128]{1,0:T(8,128)S(1)} %get-tuple-element.24.own.x_up_own, ...), custom_call_target="tpu_custom_call", output_to_operand_aliasing={{0}: (0, {})} | custom-call | tf_op jit(solution)/shard_map/last_rims/pallas_call | solution.py:522
  (2 shorter events, 0.0 us)
Async XLA Ops:
  2.7 13.7 %collective-permute-start.2 = (f32[240,128]{1,0:T(8,128)S(1)}, f32[240,128]{1,0:T(8,128)S(1)}, u32[]{:S(2)}, u32[]{:S(2)}) collective-permute-start(f32[240,128]{1,0:T(8,128)S(1)} %get-tuple-element.24.own.x_up_own), channel_id=1, source_target_pairs={{28,0},{0,4},{4,8},{8,12},{12,16},{16,20},{20,24},{24,28},{29,1},{... | collective-permute-start | bytes 368648 | tf_op jit(solution)/shard_map/ppermute | solution.py:418
  6.4 10.1 %collective-permute-start.3 = (f32[240,128]{1,0:T(8,128)S(1)}, f32[240,128]{1,0:T(8,128)S(1)}, u32[]{:S(2)}, u32[]{:S(2)}) collective-permute-start(f32[240,128]{1,0:T(8,128)S(1)} %x_low_rims.1.own.x_low_own), channel_id=1, source_target_pairs={{4,0},{8,4},{12,8},{16,12},{20,16},{24,20},{28,24},{0,28},{5,1},{9... | collective-permute-start | bytes 368648 | tf_op jit(solution)/shard_map/ppermute | solution.py:418
  10.8 2.1 %collective-permute-start.1 = (f32[24,128]{1,0:T(8,128)S(1)}, f32[24,128]{1,0:T(8,128)S(1)}, u32[]{:S(2)}, u32[]{:S(2)}) collective-permute-start(f32[24,128]{1,0:T(8,128)S(1)} %get-tuple-element.20.y_low_own), channel_id=1, source_target_pairs={{1,0},{2,1},{3,2},{0,3},{5,4},{6,5},{7,6},{4,7},{9,8},{10,9},{11,1... | collective-permute-start | bytes 36872 | tf_op jit(solution)/shard_map/ppermute | solution.py:418
  11.5 3.1 %collective-permute-start = (f32[24,128]{1,0:T(8,128)S(1)}, f32[24,128]{1,0:T(8,128)S(1)}, u32[]{:S(2)}, u32[]{:S(2)}) collective-permute-start(f32[24,128]{1,0:T(8,128)S(1)} %get-tuple-element.21.y_up_own), channel_id=1, source_target_pairs={{3,0},{0,1},{1,2},{2,3},{7,4},{4,5},{5,6},{6,7},{11,8},{8,9},{9,10... | collective-permute-start | bytes 36872 | tf_op jit(solution)/shard_map/ppermute | solution.py:418
  16.5 2.2 %collective-permute-start.5 = (f32[48,128]{1,0:T(8,128)S(1)}, f32[48,128]{1,0:T(8,128)S(1)}, u32[]{:S(2)}, u32[]{:S(2)}) collective-permute-start(f32[48,128]{1,0:T(8,128)S(1)} %corners_up.1.changes), channel_id=1, source_target_pairs={{1,0},{2,1},{3,2},{0,3},{5,4},{6,5},{7,6},{4,7},{9,8},{10,9},{11,1... | collective-permute-start | bytes 73736 | tf_op jit(solution)/shard_map/ppermute | solution.py:418
  16.9 3.3 %collective-permute-start.4 = (f32[48,128]{1,0:T(8,128)S(1)}, f32[48,128]{1,0:T(8,128)S(1)}, u32[]{:S(2)}, u32[]{:S(2)}) collective-permute-start(f32[48,128]{1,0:T(8,128)S(1)} %corners_up.1.changes), channel_id=1, source_target_pairs={{3,0},{0,1},{1,2},{2,3},{7,4},{4,5},{5,6},{6,7},{11,8},{8,9},{9,10... | collective-permute-start | bytes 73736 | tf_op jit(solution)/shard_map/ppermute | solution.py:418

commit v4 on v3

--- a/solution.py
+++ b/solution.py
@@ -82,14 +82,15 @@
     lax.fori_loop(0, depth // UNROLL, layers, 4.5 - 1.5 * total(first))
 
 
-def gather_columns(tile_of, c, depth, rows, cols, beside=0):
+def gather_columns(ref, linked, c, depth, rows, cols, beside=0):
     _, lane = row_and_lane(rows, cols)
     result, other = jnp.zeros((rows, cols), jnp.float32), jnp.zeros((rows, cols), jnp.float32)
     for k in range(LINKS):
+        slot = linked[k]
         near, far = jnp.zeros_like(result), jnp.zeros_like(other)
         for z in range(depth):
             place = GROUP * k + z
-            moved = spin(tile_of(k, z), place - c)
+            moved = spin(ref[slot, pl.ds((z + 1) * rows, rows), :], place - c)
             near = jnp.where(lane == place, moved, near)
             if beside:
                 far = jnp.where(lane == (place + beside) % cols, moved, far)
@@ -98,10 +99,14 @@
     return result, spin(other, -beside)
 
 
+def x_rows(part, k, depth):
+    return pl.ds(part * LINKS * depth + k, depth, stride=LINKS)
+
+
 def first_kernel(
     slots, depth, rows, cols,
     field, planes, grains, maps,
-    now, stepped, squares, x_up, lists,
+    now, stepped, squares, x_low, x_up, lists,
     planes_in, grains_in, maps_in, inverse, arrived,
 ):
     copies = [
@@ -162,43 +167,38 @@
     field_part(0).wait()
 
     step(now, stepped, slots, depth, rows, cols, squares, lambda i: field_part(i).wait())
-    pack_x(1, now, stepped, squares, lists, x_up, depth, rows, cols)
-
-
-def x_low_kernel(depth, rows, cols, now, stepped, squares, lists, x_low):
-    pack_x(0, now, stepped, squares, lists, x_low, depth, rows, cols)
-
-
-def pack_x(face, now, stepped, squares, lists, out, depth, rows, cols):
-    block = LINKS * depth
+
+    linked = [[lists[face * SPAN + k] for k in range(LINKS)] for face in range(4)]
+    end = 3 * LINKS * depth
     edge_row, edge_lane = row_and_lane(depth, cols)
-    top = (depth + 1) * rows
-    r, inner_r = (0, 1) if face == 0 else (rows - 1, rows - 2)
-    rim_rows = pl.ds(rows + r, depth, stride=rows)
-    rest = squares[pl.ds(r, depth, stride=rows), :]
-    for k in range(LINKS):
-        slot = lists[face * SPAN + k]
-        partial = stepped[slot, rim_rows, :]
-        inner = stepped[slot, pl.ds(rows + inner_r, depth, stride=rows), :]
-        below = jnp.broadcast_to(now[slot, pl.ds(r, 1), :], (depth, cols))
-        above = jnp.broadcast_to(now[slot, pl.ds(top + r, 1), :], (depth, cols))
-        inner = inner + jnp.where(edge_row == 0, below, jnp.where(edge_row == depth - 1, above, 0.0))
-        rest = rest - partial * partial
-        out[pl.ds(k * depth, depth), :] = now[slot, rim_rows, :]
-        out[pl.ds(block + k * depth, depth), :] = partial
-        out[pl.ds(2 * block + k * depth, depth), :] = inner
-    out[pl.ds(3 * block + depth, depth), :] = rest
-    corners = jnp.zeros((depth, cols), jnp.float32)
-    for i, ref in enumerate((stepped, now)):
-        for side in range(2):
-            for k in range(LINKS):
-                place = (2 * i + side) * LINKS + k
-                moved = spin(ref[lists[(2 + side) * SPAN + k], rim_rows, :], place - side * (cols - 1))
-                corners = jnp.where(edge_lane == place, moved, corners)
-    out[pl.ds(3 * block, depth), :] = corners
-    end = 3 * block + 2 * depth
-    if out.shape[0] > end:
-        out[pl.ds(end, out.shape[0] - end), :] = jnp.zeros((out.shape[0] - end, cols), jnp.float32)
+    for face, out in ((1, x_up), (0, x_low)):
+        r, inner_r = (0, 1) if face == 0 else (rows - 1, rows - 2)
+        rim_rows = pl.ds(rows + r, depth, stride=rows)
+        rest = squares[pl.ds(r, depth, stride=rows), :]
+        for k in range(LINKS):
+            slot = linked[face][k]
+            partial = stepped[slot, rim_rows, :]
+            inner = stepped[slot, pl.ds(rows + inner_r, depth, stride=rows), :]
+            below = jnp.broadcast_to(now[slot, pl.ds(r, 1), :], (depth, cols))
+            above = jnp.broadcast_to(now[slot, pl.ds(top + r, 1), :], (depth, cols))
+            inner = inner + jnp.where(edge_row == 0, below, jnp.where(edge_row == depth - 1, above, 0.0))
+            rest = rest - partial * partial
+            out[x_rows(0, k, depth), :] = now[slot, rim_rows, :]
+            out[x_rows(1, k, depth), :] = partial
+            out[x_rows(2, k, depth), :] = inner
+        corners = [jnp.zeros((depth, cols), jnp.float32)] * 4
+        for k in range(LINKS):
+            for side in range(2):
+                slot = linked[2 + side][k]
+                for i, ref in enumerate((stepped, now)):
+                    place = (2 * i + side) * LINKS + k
+                    moved = spin(ref[slot, rim_rows, :], place - side * (cols - 1))
+                    corners[2 * i + side] = jnp.where(edge_lane == place, moved, corners[2 * i + side])
+        out[pl.ds(end, depth), :] = (corners[0] + corners[1]) + (corners[2] + corners[3])
+        out[pl.ds(end + depth, depth), :] = rest
+        if out.shape[0] > end + 2 * depth:
+            left = out.shape[0] - end - 2 * depth
+            out[pl.ds(end + 2 * depth, left), :] = jnp.zeros((left, cols), jnp.float32)
 
 
 def y_kernel(slots, depth, rows, cols, now, stepped, squares, lists, y_low, y_up):
@@ -206,17 +206,13 @@
     _, lane = row_and_lane(rows, cols)
     for side, out in ((0, y_low), (1, y_up)):
         c, inward = (0, 1) if side == 0 else (cols - 1, -1)
-        base = (2 + side) * SPAN
-        rim, _ = gather_columns(
-            lambda k, z: now[lists[base + k], pl.ds((z + 1) * rows, rows), :], c, depth, rows, cols
-        )
-        partial, inner = gather_columns(
-            lambda k, z: stepped[lists[base + k], pl.ds((z + 1) * rows, rows), :], c, depth, rows, cols, beside=inward
-        )
+        linked = [lists[(2 + side) * SPAN + k] for k in range(LINKS)]
+        rim, _ = gather_columns(now, linked, c, depth, rows, cols)
+        partial, inner = gather_columns(stepped, linked, c, depth, rows, cols, beside=inward)
         for k in range(LINKS):
             for z, at in ((0, 0), (depth - 1, top)):
                 place = GROUP * k + z
-                frozen = spin(now[lists[base + k], pl.ds(at, rows), :], place - c)
+                frozen = spin(now[linked[k], pl.ds(at, rows), :], place - c)
                 inner = inner + jnp.where(lane == place, frozen, 0.0)
         total = jnp.zeros((rows, cols), jnp.float32)
         for z in range(depth):
@@ -267,7 +263,7 @@
 
 
 def x_rims(own, got, k, depth):
-    zero, one = pl.ds(k * depth, depth), pl.ds((LINKS + k) * depth, depth)
+    zero, one = x_rows(0, k, depth), x_rows(1, k, depth)
     return own[one, :] + RATE * got[zero, :], got[one, :] + RATE * own[zero, :]
 
 
@@ -275,7 +271,7 @@
     change = jnp.zeros((depth, cols), jnp.float32)
     for k in range(LINKS):
         own_one, _ = x_rims(own, got, k, depth)
-        partial = own[pl.ds((LINKS + k) * depth, depth), :]
+        partial = own[x_rows(1, k, depth), :]
         change = change + (own_one * own_one - partial * partial)
     out[pl.ds(0, depth), :] = change
     out[pl.ds(depth, depth), :] = got[pl.ds(3 * LINKS * depth, depth), :]
@@ -288,7 +284,7 @@
 
 def x_rim_step(padded, face, k, one, factor, outer, depth, cols):
     _, lane = row_and_lane(depth, cols)
-    z_sum = padded[face, pl.ds(k * GROUP, depth), :] + padded[face, pl.ds(k * GROUP + 2, depth), :]
+    z_sum = padded[face, pl.ds(k, depth, stride=SPAN), :] + padded[face, pl.ds(2 * SPAN + k, depth, stride=SPAN), :]
     y_sum = jnp.where(lane == 0, 0.0, pltpu.roll(one, 1, 1)) + jnp.where(
         lane == cols - 1, 0.0, pltpu.roll(one, cols - 1, 1)
     )
@@ -319,7 +315,7 @@
         inner_rows = pl.ds(rows + inner_r, depth, stride=rows)
         rims = [x_rims(own, got, k, depth) for k in range(LINKS)]
         for k in range(LINKS):
-            x_own_one[face, pl.ds(k * GROUP + 1, depth), :] = rims[k][0]
+            x_own_one[face, pl.ds(SPAN + k, depth, stride=SPAN), :] = rims[k][0]
 
         change = changes[pl.ds(2 * face * depth, depth), :]
         scaled = 0.15 * change
@@ -332,15 +328,15 @@
                 later[first + i, rim_rows, :] = old[i] - scaled * rim[i]
         factor = 4.5 - 1.5 * ((parts[0] + parts[1]) + (parts[2] + parts[3]))
 
-        beside = [later[lists[face * SPAN + k], inner_rows, :] for k in range(LINKS)]
+        linked = [lists[face * SPAN + k] for k in range(LINKS)]
+        beside = [later[slot, inner_rows, :] for slot in linked]
         two = []
         for k in range(LINKS):
-            outer = own[pl.ds((2 * LINKS + k) * depth, depth), :] + rims[k][1]
+            outer = own[x_rows(2, k, depth), :] + rims[k][1]
             two.append(x_rim_step(x_own_one, face, k, rims[k][0], factor, outer, depth, cols))
         for k in range(LINKS):
-            slot = lists[face * SPAN + k]
-            later[slot, rim_rows, :] = two[k]
-            later[slot, inner_rows, :] = beside[k] + RATE * RATE * got[pl.ds(k * depth, depth), :]
+            later[linked[k], rim_rows, :] = two[k]
+            later[linked[k], inner_rows, :] = beside[k] + RATE * RATE * got[x_rows(0, k, depth), :]
 
     step(later, last, slots, depth, rows, cols)
 
@@ -374,7 +370,7 @@
         total = got[pl.ds(3 * block + depth, depth), :]
         for k in range(LINKS):
             total = total + rims[k][1] * rims[k][1]
-            x_one[face, pl.ds(k * GROUP + 1, depth), :] = rims[k][1]
+            x_one[face, pl.ds(SPAN + k, depth, stride=SPAN), :] = rims[k][1]
         corners = got[pl.ds(3 * block, depth), :]
         for side in range(2):
             place = side * LINKS
@@ -386,13 +382,14 @@
             total = total + jnp.where(flat_lane == side * (cols - 1), column, 0.0)
         factor = 4.5 - 1.5 * total
         rim_rows = pl.ds(rows + (0 if face == 0 else rows - 1), depth, stride=rows)
-        old = [last[lists[face * SPAN + k], rim_rows, :] for k in range(LINKS)]
-        for k in range(LINKS):
-            outer = got[pl.ds(2 * block + k * depth, depth), :] + rims[k][0]
+        linked = [lists[face * SPAN + k] for k in range(LINKS)]
+        old = [last[slot, rim_rows, :] for slot in linked]
+        for k in range(LINKS):
+            outer = got[x_rows(2, k, depth), :] + rims[k][0]
             two = x_rim_step(x_one, face, k, rims[k][1], factor, outer, depth, cols)
-            last[lists[face * SPAN + k], rim_rows, :] = old[k] + RATE * two
-        for k in range(LINKS):
-            send_linked(lists[face * SPAN + k])
+            last[linked[k], rim_rows, :] = old[k] + RATE * two
+        for slot in linked:
+            send_linked(slot)
 
     twos = []
     for side, own, got in ((0, y_low_own, y_low), (1, y_up_own, y_up)):
@@ -426,7 +423,7 @@
     planes = pltpu.VMEM((depth * rows, cols), f32)
     x_pack = shape((-(-(3 * LINKS + 2) * depth // rows) * rows, cols), f32)
     y_pack = shape((3 * rows, cols), f32)
-    rims = pltpu.VMEM((2, LINKS * GROUP, cols), f32)
+    rims = pltpu.VMEM((2, (depth + 2) * SPAN, cols), f32)
     vmem = pl.BlockSpec(memory_space=pltpu.VMEM)
     smem = pl.BlockSpec(memory_space=pltpu.SMEM)
     hbm = pl.BlockSpec(memory_space=pltpu.HBM)
@@ -435,11 +432,11 @@
     sizes = (slots, depth, rows, cols)
     work = pl.CostEstimate(flops=20 * field.size, bytes_accessed=2 * 4 * field.size, transcendentals=0)
 
-    now, stepped, squares, x_up, lists = pl.pallas_call(
+    now, stepped, squares, x_low, x_up, lists = pl.pallas_call(
         functools.partial(first_kernel, *sizes),
-        out_shape=[padded, padded, planes, x_pack, shape((4 * SPAN + slots,), jnp.int32)],
+        out_shape=[padded, padded, planes, x_pack, x_pack, shape((4 * SPAN + slots,), jnp.int32)],
         in_specs=[hbm] * 4,
-        out_specs=[vmem] * 4 + [smem],
+        out_specs=[vmem] * 5 + [smem],
         scratch_shapes=[
             pltpu.VMEM(zplanes.shape, jnp.int32),
             pltpu.SMEM(grain_ids.shape, jnp.int32),
@@ -452,17 +449,6 @@
     )(*(pltpu.with_memory_space_constraint(x, pltpu.HBM) for x in (field, zplanes, grain_ids, channel_maps)))
 
     from_low = shifted(x_up, "gx", 1)
-
-    x_low = pl.pallas_call(
-        functools.partial(x_low_kernel, depth, rows, cols),
-        out_shape=x_pack,
-        in_specs=[vmem] * 3 + [smem],
-        out_specs=vmem,
-        compiler_params=params,
-        cost_estimate=work,
-        name="x_low_rims",
-    )(now, stepped, squares, lists)
-
     from_up = shifted(x_low, "gx", -1)
 
     y_low, y_up = pl.pallas_call(

time: 22.1 us -> 21.5 us (0.973)
  Pallas kernels: 9.95 us -> 9.36 us
    pallas_call x1 -> x0, Pallas kernels: 0.66 us -> none  [on_device(): pl.pallas_call(functools.partial(x_low_kernel, depth, rows, cols), out_sh...]
  transfers between devices with their start and end apart: 6 -> 6, of which waited for: 3 -> 3; matrix products, arithmetic and copies ran while one was open for 0% -> 0% of each run, Pallas kernels for 25% -> 22%
where the time goes in v4:
time: 21.5 us; the launch traced here: 21.3 us
  Pallas kernels  9.36 us (44%)
  starting transfers between devices  7.39 us (34%)
  waiting for transfers between devices  4.47 us (21%)
    ppermute x6, starting transfers between devices, shifted(): lax.ppermute(block, axis, [((i - distance) % size, i) for i in range(size)])  7.39 us
    ppermute x6, waiting for transfers between devices, shifted(): lax.ppermute(block, axis, [((i - distance) % size, i) for i in range(size)])  4.47 us
    pallas_call x1, Pallas kernels, on_device(): pl.pallas_call(functools.partial(first_kernel, *sizes), out_shape=[padded...  2.75 us
    pallas_call x1, Pallas kernels, on_device(): pl.pallas_call(functools.partial(second_kernel, *sizes), out_shape=[padde...  1.82 us
    pallas_call x1, Pallas kernels, on_device(): pl.pallas_call(functools.partial(last_kernel, *sizes), out_shape=[padded,...  1.8 us
    pallas_call x1, Pallas kernels, on_device(): pl.pallas_call(functools.partial(third_kernel, *sizes), out_shape=[padded...  1.68 us
    pallas_call x1, Pallas kernels, on_device(): pl.pallas_call(functools.partial(y_kernel, *sizes), out_shape=[y_pack, y_...  1.26 us
  transfers between devices with their start and end apart: 6, of which 3 were waited for; matrix products, arithmetic and copies ran while one was open for 0% of the time, Pallas kernels for 22%

profile of v4, /device:TPU:0, one launch (start us, length us, event | category | flops | bytes accessed | tf_op | source)
XLA Modules:
  0.0 21.3 jit_solution(1549048547302362336)
XLA Ops:
  0.0 2.8 %first_step.1 = (f32[25,112,128]{2,1,0:T(8,128)S(1)}, f32[25,112,128]{2,1,0:T(8,128)S(1)}, f32[96,128]{1,0:T(8,128)S(1)}, f32[240,128]{1,0:T(8,128)S(1)}, f32[240,128]{1,0:T(8,128)S(1)}, /*index=5*/s32[56]{0:T(128)S(1)}) custom-call(f32[24,96,128]{2,1,0:T(8,128)} %bitcast.2, s32[2,8,128]{2,1,0:T(8,128)} %planes.1, s32[1,1,24]{2,1,0:T(1,128)} %grains.1, ...), custom_call_target="tpu_custom_call" | custom-call | tf_op jit(solution)/shard_map/first_step/pallas_call | solution.py:435
  2.8 3.0 %collective-permute-start.2 = (f32[240,128]{1,0:T(8,128)S(1)}, f32[240,128]{1,0:T(8,128)S(1)}, u32[]{:S(2)}, u32[]{:S(2)}) collective-permute-start(f32[240,128]{1,0:T(8,128)S(1)} %get-tuple-element.26.own.x_up_own), channel_id=1, source_target_pairs={{28,0},{0,4},{4,8},{8,12},{12,16},{16,20},{20,24},{24,28},{29,1},{... | collective-permute-start | bytes 368648 | tf_op jit(solution)/shard_map/ppermute | solution.py:415
  5.8 3.1 %collective-permute-start.3 = (f32[240,128]{1,0:T(8,128)S(1)}, f32[240,128]{1,0:T(8,128)S(1)}, u32[]{:S(2)}, u32[]{:S(2)}) collective-permute-start(f32[240,128]{1,0:T(8,128)S(1)} %get-tuple-element.25.own.x_low_own), channel_id=1, source_target_pairs={{4,0},{8,4},{12,8},{16,12},{20,16},{24,20},{28,24},{0,28},{5,1},{9... | collective-permute-start | bytes 368648 | tf_op jit(solution)/shard_map/ppermute | solution.py:415
  8.9 1.3 %y_rims.1 = (f32[24,128]{1,0:T(8,128)S(1)}, f32[24,128]{1,0:T(8,128)S(1)}) custom-call(f32[25,112,128]{2,1,0:T(8,128)S(1)} %get-tuple-element.18.now, f32[25,112,128]{2,1,0:T(8,128)S(1)} %get-tuple-element.17.stepped.stepped_in, f32[96,128]{1,0:T(8,128)S(1)} %get-tuple-element.19.squares, s32[56]{0:T(128)S(1)} %get-tuple-element.20.lists), custom_call_target="tpu_custom_call" | custom-call | flops 5898240 | bytes 2359296 | tf_op jit(solution)/shard_map/y_rims/pallas_call | solution.py:454
  10.1 0.7 %collective-permute-start.1 = (f32[24,128]{1,0:T(8,128)S(1)}, f32[24,128]{1,0:T(8,128)S(1)}, u32[]{:S(2)}, u32[]{:S(2)}) collective-permute-start(f32[24,128]{1,0:T(8,128)S(1)} %get-tuple-element.21.y_low_own), channel_id=1, source_target_pairs={{1,0},{2,1},{3,2},{0,3},{5,4},{6,5},{7,6},{4,7},{9,8},{10,9},{11,1... | collective-permute-start | bytes 36872 | tf_op jit(solution)/shard_map/ppermute | solution.py:415
  10.9 0.0 collective-permute-start
  10.9 1.4 %collective-permute-done.1.y_up = f32[24,128]{1,0:T(8,128)S(1)} collective-permute-done((f32[24,128]{1,0:T(8,128)S(1)}, f32[24,128]{1,0:T(8,128)S(1)}, u32[]{:S(2)}, u32[]{:S(2)}) %collective-permute-start.1) | collective-permute-done | bytes 12320 | tf_op jit(solution)/shard_map/ppermute | solution.py:415
  12.3 1.7 %collective-permute-done.y_low = f32[24,128]{1,0:T(8,128)S(1)} collective-permute-done((f32[24,128]{1,0:T(8,128)S(1)}, f32[24,128]{1,0:T(8,128)S(1)}, u32[]{:S(2)}, u32[]{:S(2)}) %collective-permute-start) | collective-permute-done | bytes 12320 | tf_op jit(solution)/shard_map/ppermute | solution.py:415
  14.0 1.8 %second_step.1 = (f32[25,112,128]{2,1,0:T(8,128)S(1)}, f32[25,112,128]{2,1,0:T(8,128)S(1)}) custom-call(f32[25,112,128]{2,1,0:T(8,128)S(1)} %get-tuple-element.17.stepped.stepped_in, f32[24,128]{1,0:T(8,128)S(1)} %get-tuple-element.21.y_low_own, f32[24,128]{1,0:T(8,128)S(1)} %get-tuple-element.22.y_up_own, ...), custom_call_target="tpu_custom_call", output_to_operand_aliasing={{0}: (0, {})} | custom-call | flops 5898240 | bytes 2359296 | tf_op jit(solution)/shard_map/second_step/pallas_call | solution.py:467
  15.8 0.0 collective-permute-done.2.got.x_low
  15.8 0.0 collective-permute-done.3.got.x_up
  15.9 0.4 %collective-permute-start.5 = (f32[48,128]{1,0:T(8,128)S(1)}, f32[48,128]{1,0:T(8,128)S(1)}, u32[]{:S(2)}, u32[]{:S(2)}) collective-permute-start(f32[48,128]{1,0:T(8,128)S(1)} %corners_up.1.changes), channel_id=1, source_target_pairs={{1,0},{2,1},{3,2},{0,3},{5,4},{6,5},{7,6},{4,7},{9,8},{10,9},{11,1... | collective-permute-start | bytes 73736 | tf_op jit(solution)/shard_map/ppermute | solution.py:415
  16.2 0.2 collective-permute-start.4
  16.4 1.7 %third_step.1 = (f32[25,112,128]{2,1,0:T(8,128)S(1)}, f32[25,112,128]{2,1,0:T(8,128)S(1)}) custom-call(f32[25,112,128]{2,1,0:T(8,128)S(1)} %get-tuple-element.23.now, f32[25,112,128]{2,1,0:T(8,128)S(1)} %get-tuple-element.24.before.later_in, f32[240,128]{1,0:T(8,128)S(1)} %get-tuple-element.25.own.x_low_own, ...), custom_call_target="tpu_custom_call", output_to_operand_aliasing={{0}: (1, {})} | custom-call | tf_op jit(solution)/shard_map/third_step/pallas_call | solution.py:495
  18.1 0.0 collective-permute-done.5.from_right
  18.1 1.3 %collective-permute-done.4.from_left = f32[48,128]{1,0:T(8,128)S(1)} collective-permute-done((f32[48,128]{1,0:T(8,128)S(1)}, f32[48,128]{1,0:T(8,128)S(1)}, u32[]{:S(2)}, u32[]{:S(2)}) %collective-permute-start.4) | collective-permute-done | bytes 24608 | tf_op jit(solution)/shard_map/ppermute | solution.py:415
  19.5 1.8 %last_rims.1 = (f32[25,112,128]{2,1,0:T(8,128)S(1)}, f32[24,96,128]{2,1,0:T(8,128)}) custom-call(f32[25,112,128]{2,1,0:T(8,128)S(1)} %get-tuple-element.27.last_in, f32[240,128]{1,0:T(8,128)S(1)} %get-tuple-element.25.own.x_low_own, f32[240,128]{1,0:T(8,128)S(1)} %get-tuple-element.26.own.x_up_own, ...), custom_call_target="tpu_custom_call", output_to_operand_aliasing={{0}: (0, {})} | custom-call | tf_op jit(solution)/shard_map/last_rims/pallas_call | solution.py:508
  (2 shorter events, 0.0 us)
Async XLA Ops:
  2.8 13.1 %collective-permute-start.2 = (f32[240,128]{1,0:T(8,128)S(1)}, f32[240,128]{1,0:T(8,128)S(1)}, u32[]{:S(2)}, u32[]{:S(2)}) collective-permute-start(f32[240,128]{1,0:T(8,128)S(1)} %get-tuple-element.26.own.x_up_own), channel_id=1, source_target_pairs={{28,0},{0,4},{4,8},{8,12},{12,16},{16,20},{20,24},{24,28},{29,1},{... | collective-permute-start | bytes 368648 | tf_op jit(solution)/shard_map/ppermute | solution.py:415
  5.8 10.1 %collective-permute-start.3 = (f32[240,128]{1,0:T(8,128)S(1)}, f32[240,128]{1,0:T(8,128)S(1)}, u32[]{:S(2)}, u32[]{:S(2)}) collective-permute-start(f32[240,128]{1,0:T(8,128)S(1)} %get-tuple-element.25.own.x_low_own), channel_id=1, source_target_pairs={{4,0},{8,4},{12,8},{16,12},{20,16},{24,20},{28,24},{0,28},{5,1},{9... | collective-permute-start | bytes 368648 | tf_op jit(solution)/shard_map/ppermute | solution.py:415
  10.1 2.1 %collective-permute-start.1 = (f32[24,128]{1,0:T(8,128)S(1)}, f32[24,128]{1,0:T(8,128)S(1)}, u32[]{:S(2)}, u32[]{:S(2)}) collective-permute-start(f32[24,128]{1,0:T(8,128)S(1)} %get-tuple-element.21.y_low_own), channel_id=1, source_target_pairs={{1,0},{2,1},{3,2},{0,3},{5,4},{6,5},{7,6},{4,7},{9,8},{10,9},{11,1... | collective-permute-start | bytes 36872 | tf_op jit(solution)/shard_map/ppermute | solution.py:415
  10.9 3.1 %collective-permute-start = (f32[24,128]{1,0:T(8,128)S(1)}, f32[24,128]{1,0:T(8,128)S(1)}, u32[]{:S(2)}, u32[]{:S(2)}) collective-permute-start(f32[24,128]{1,0:T(8,128)S(1)} %get-tuple-element.22.y_up_own), channel_id=1, source_target_pairs={{3,0},{0,1},{1,2},{2,3},{7,4},{4,5},{5,6},{6,7},{11,8},{8,9},{9,10... | collective-permute-start | bytes 36872 | tf_op jit(solution)/shard_map/ppermute | solution.py:415
  15.9 2.2 %collective-permute-start.5 = (f32[48,128]{1,0:T(8,128)S(1)}, f32[48,128]{1,0:T(8,128)S(1)}, u32[]{:S(2)}, u32[]{:S(2)}) collective-permute-start(f32[48,128]{1,0:T(8,128)S(1)} %corners_up.1.changes), channel_id=1, source_target_pairs={{1,0},{2,1},{3,2},{0,3},{5,4},{6,5},{7,6},{4,7},{9,8},{10,9},{11,1... | collective-permute-start | bytes 73736 | tf_op jit(solution)/shard_map/ppermute | solution.py:415
  16.2 3.3 %collective-permute-start.4 = (f32[48,128]{1,0:T(8,128)S(1)}, f32[48,128]{1,0:T(8,128)S(1)}, u32[]{:S(2)}, u32[]{:S(2)}) collective-permute-start(f32[48,128]{1,0:T(8,128)S(1)} %corners_up.1.changes), channel_id=1, source_target_pairs={{3,0},{0,1},{1,2},{2,3},{7,4},{4,5},{5,6},{6,7},{11,8},{8,9},{9,10... | collective-permute-start | bytes 73736 | tf_op jit(solution)/shard_map/ppermute | solution.py:415

commit v5 on v4

--- a/solution.py
+++ b/solution.py
@@ -35,7 +35,7 @@
     return tile
 
 
-def step(src, dst, slots, depth, rows, cols, squares=None, wait=None):
+def step(src, dst, slots, depth, rows, cols, squares=None, wait=None, beside=None, carried=()):
     row, lane = row_and_lane(rows, cols)
     first_row, last_row = row == 0, row == rows - 1
     first_lane, last_lane = lane == 0, lane == cols - 1
@@ -68,35 +68,37 @@
             squares[pl.ds(pl.multiple_of(z * rows, rows), rows), :] = total(parts)
         return 4.5 - 1.5 * total(following)
 
-    def layers(i, factor):
+    def layers(i, carry):
+        factor, *carried = carry
         if wait is not None:
             pl.when(i + 1 < depth // UNROLL)(lambda: wait(i + 1))
+        if beside is not None:
+            carried = beside(i, carried)
         for j in range(UNROLL):
             factor = layer(i * UNROLL + j, factor)
-        return factor
+        return (factor, *carried)
 
     first = [None] * 4
     for s in range(slots):
         v = src[s, at(0), :]
         add(first, s, v * v)
-    lax.fori_loop(0, depth // UNROLL, layers, 4.5 - 1.5 * total(first))
-
-
-def gather_columns(ref, linked, c, depth, rows, cols, beside=0):
+    lax.fori_loop(0, depth // UNROLL, layers, (4.5 - 1.5 * total(first), *carried))
+
+
+def gather_columns(ref, low, up, depth, rows, cols, beside=False):
     _, lane = row_and_lane(rows, cols)
-    result, other = jnp.zeros((rows, cols), jnp.float32), jnp.zeros((rows, cols), jnp.float32)
+    shifts = (0, -1, 1, -2) if beside else (0, -1)
+    results = [jnp.zeros((rows, cols), jnp.float32)] * len(shifts)
     for k in range(LINKS):
-        slot = linked[k]
-        near, far = jnp.zeros_like(result), jnp.zeros_like(other)
+        parts = [jnp.zeros((rows, cols), jnp.float32)] * len(shifts)
         for z in range(depth):
+            at = pl.ds((z + 1) * rows, rows)
             place = GROUP * k + z
-            moved = spin(ref[slot, pl.ds((z + 1) * rows, rows), :], place - c)
-            near = jnp.where(lane == place, moved, near)
-            if beside:
-                far = jnp.where(lane == (place + beside) % cols, moved, far)
-        result = result + near
-        other = other + far
-    return result, spin(other, -beside)
+            moved = spin(jnp.where(lane < cols // 2, ref[low[k], at, :], ref[up[k], at, :]), place)
+            for i, shift in enumerate(shifts):
+                parts[i] = jnp.where(lane == (place + shift) % cols, moved, parts[i])
+        results = [result + part for result, part in zip(results, parts)]
+    return [spin(result, -shift) for result, shift in zip(results, shifts)]
 
 
 def x_rows(part, k, depth):
@@ -139,21 +141,6 @@
         for face in (0, 2):
             partner = maps_in[0, 0, face, s]
             inverse[face // 2 * (slots + 1) + jnp.where(partner >= 0, partner, slots)] = s
-    counts = [jnp.int32(face * SPAN) for face in range(4)]
-    for s in range(slots):
-        partners = [maps_in[0, 0, face, s] for face in range(4)]
-        best = jnp.maximum(jnp.maximum(partners[0], partners[1]), jnp.maximum(partners[2], partners[3]))
-        lists[4 * SPAN + s] = (best >= 0).astype(jnp.int32)
-        for face in range(4):
-            if face in (1, 3):
-                valid = partners[face] >= 0
-                slot = jnp.where(valid, s, slots)
-            else:
-                slot = inverse[face // 2 * (slots + 1) + s]
-                valid = slot < slots
-            lists[counts[face]] = slot
-            counts[face] = counts[face] + valid.astype(jnp.int32)
-
     top = (depth + 1) * rows
     copies[1].wait()
     copies[2].wait()
@@ -166,7 +153,31 @@
             ref[s, pl.ds(top, rows), :] = above
     field_part(0).wait()
 
-    step(now, stepped, slots, depth, rows, cols, squares, lambda i: field_part(i).wait())
+    share = -(-slots // (depth // UNROLL))
+
+    def enlist(i, counts):
+        for j in range(share):
+            s = i * share + j
+            s = s if slots % share == 0 else jnp.minimum(s, slots - 1)
+            fresh = True if slots % share == 0 else i * share + j < slots
+            partners = [maps_in[0, 0, face, s] for face in range(4)]
+            best = jnp.maximum(jnp.maximum(partners[0], partners[1]), jnp.maximum(partners[2], partners[3]))
+            lists[4 * SPAN + s] = (best >= 0).astype(jnp.int32)
+            for face in range(4):
+                if face in (1, 3):
+                    valid = partners[face] >= 0
+                    slot = jnp.where(valid, s, slots)
+                else:
+                    slot = inverse[face // 2 * (slots + 1) + s]
+                    valid = slot < slots
+                lists[counts[face]] = slot
+                counts[face] = counts[face] + (valid & fresh).astype(jnp.int32)
+        return counts
+
+    step(
+        now, stepped, slots, depth, rows, cols, squares,
+        lambda i: field_part(i).wait(), enlist, [jnp.int32(face * SPAN) for face in range(4)],
+    )
 
     linked = [[lists[face * SPAN + k] for k in range(LINKS)] for face in range(4)]
     end = 3 * LINKS * depth
@@ -204,24 +215,28 @@
 def y_kernel(slots, depth, rows, cols, now, stepped, squares, lists, y_low, y_up):
     top = (depth + 1) * rows
     _, lane = row_and_lane(rows, cols)
-    for side, out in ((0, y_low), (1, y_up)):
-        c, inward = (0, 1) if side == 0 else (cols - 1, -1)
-        linked = [lists[(2 + side) * SPAN + k] for k in range(LINKS)]
-        rim, _ = gather_columns(now, linked, c, depth, rows, cols)
-        partial, inner = gather_columns(stepped, linked, c, depth, rows, cols, beside=inward)
-        for k in range(LINKS):
-            for z, at in ((0, 0), (depth - 1, top)):
-                place = GROUP * k + z
-                frozen = spin(now[linked[k], pl.ds(at, rows), :], place - c)
-                inner = inner + jnp.where(lane == place, frozen, 0.0)
-        total = jnp.zeros((rows, cols), jnp.float32)
-        for z in range(depth):
-            place = LINKS * GROUP + z
-            total = jnp.where(lane == place, spin(tile(squares, z, rows), place - c), total)
-        inner = jnp.where(in_last_group(lane), total - group_sum(partial * partial), inner)
-        out[pl.ds(0, rows), :] = rim
-        out[pl.ds(rows, rows), :] = partial
-        out[pl.ds(2 * rows, rows), :] = inner
+    low, up = ([lists[face * SPAN + k] for k in range(LINKS)] for face in (2, 3))
+    rims = gather_columns(now, low, up, depth, rows, cols)
+    *partials, inner_low, inner_up = gather_columns(stepped, low, up, depth, rows, cols, beside=True)
+    frozen = [jnp.zeros((rows, cols), jnp.float32)] * 2
+    totals = [jnp.zeros((rows, cols), jnp.float32)] * 2
+    for k in range(LINKS):
+        for z, at in ((0, 0), (depth - 1, top)):
+            place = GROUP * k + z
+            at = pl.ds(at, rows)
+            moved = spin(jnp.where(lane < cols // 2, now[low[k], at, :], now[up[k], at, :]), place)
+            for side in range(2):
+                frozen[side] = jnp.where(lane == (place - side) % cols, moved, frozen[side])
+    for z in range(depth):
+        place = LINKS * GROUP + z
+        moved = spin(tile(squares, z, rows), place)
+        for side in range(2):
+            totals[side] = jnp.where(lane == place - side, moved, totals[side])
+    for side, out, inner in ((0, y_low, inner_low), (1, y_up, inner_up)):
+        rest = spin(totals[side], side) - group_sum(partials[side] * partials[side])
+        out[pl.ds(0, rows), :] = rims[side]
+        out[pl.ds(rows, rows), :] = partials[side]
+        out[pl.ds(2 * rows, rows), :] = jnp.where(in_last_group(lane), rest, inner + spin(frozen[side], side))
 
 
 def in_last_group(lane):
@@ -275,11 +290,12 @@
         change = change + (own_one * own_one - partial * partial)
     out[pl.ds(0, depth), :] = change
     out[pl.ds(depth, depth), :] = got[pl.ds(3 * LINKS * depth, depth), :]
+    out[pl.ds(2 * depth, depth), :] = own[pl.ds(3 * LINKS * depth, depth), :]
 
 
 def both_changes_kernel(depth, cols, own, got, before, out):
-    out[pl.ds(0, 2 * depth), :] = before[...]
-    change_kernel(depth, cols, own, got, None, out.at[pl.ds(2 * depth, 2 * depth), :])
+    out[pl.ds(0, 3 * depth), :] = before[...]
+    change_kernel(depth, cols, own, got, None, out.at[pl.ds(3 * depth, 3 * depth), :])
 
 
 def x_rim_step(padded, face, k, one, factor, outer, depth, cols):
@@ -317,7 +333,7 @@
         for k in range(LINKS):
             x_own_one[face, pl.ds(SPAN + k, depth, stride=SPAN), :] = rims[k][0]
 
-        change = changes[pl.ds(2 * face * depth, depth), :]
+        change = changes[pl.ds(3 * face * depth, depth), :]
         scaled = 0.15 * change
         parts = [change, None, None, None]
         for first in range(0, slots, 4):
@@ -341,45 +357,27 @@
     step(later, last, slots, depth, rows, cols)
 
 
-def last_kernel(
+def rims_kernel(
     slots, depth, rows, cols,
-    last_in, x_low_own, x_up_own, x_low, x_up, y_low_own, y_up_own, y_low, y_up, from_left, from_right,
-    lists,
+    last_in, x_low_own, x_up_own, x_low, x_up, y_low_own, y_up_own, y_low, y_up, lists,
     last, result,
     x_one, sent,
 ):
-    whole = last.at[pl.ds(0, slots), pl.ds(rows, depth * rows), :]
-
-    def send(slot):
-        pltpu.make_async_copy(last.at[slot, pl.ds(rows, depth * rows), :], result.at[slot], sent).start()
-
-    def send_linked(slot):
-        pl.when(slot < slots)(lambda: send(slot))
-
-    for s in range(slots):
-        pl.when(lists[4 * SPAN + s] == 0)(functools.partial(send, s))
-
-    row, lane = row_and_lane(rows, cols)
-    _, flat_lane = row_and_lane(depth, cols)
-    tall_row, tall_lane = row_and_lane(GROUP, cols)
-    block = LINKS * depth
-    passed_on = (from_left, from_right)
+    _, lane = row_and_lane(rows, cols)
+
+    def each_unlinked(act):
+        for s in range(slots):
+            copy = pltpu.make_async_copy(last.at[s, pl.ds(rows, depth * rows), :], result.at[s], sent)
+            pl.when(lists[4 * SPAN + s] == 0)(getattr(copy, act))
+
+    each_unlinked("start")
     x_one[...] = jnp.zeros(x_one.shape, jnp.float32)
     for face, own, got in ((0, x_low_own, x_low), (1, x_up_own, x_up)):
         rims = [x_rims(own, got, k, depth) for k in range(LINKS)]
-        total = got[pl.ds(3 * block + depth, depth), :]
+        total = got[pl.ds((3 * LINKS + 1) * depth, depth), :]
         for k in range(LINKS):
             total = total + rims[k][1] * rims[k][1]
             x_one[face, pl.ds(SPAN + k, depth, stride=SPAN), :] = rims[k][1]
-        corners = got[pl.ds(3 * block, depth), :]
-        for side in range(2):
-            place = side * LINKS
-            came_from = (3 - side) * LINKS
-            term = RATE * spin(passed_on[side][pl.ds((2 * face + 1) * depth, depth), :], place - came_from)
-            term = term * (2.0 * corners + term)
-            term = jnp.where((flat_lane >= place) & (flat_lane < place + LINKS), term, 0.0)
-            column = jnp.sum(term, axis=1, keepdims=True)
-            total = total + jnp.where(flat_lane == side * (cols - 1), column, 0.0)
         factor = 4.5 - 1.5 * total
         rim_rows = pl.ds(rows + (0 if face == 0 else rows - 1), depth, stride=rows)
         linked = [lists[face * SPAN + k] for k in range(LINKS)]
@@ -388,26 +386,72 @@
             outer = got[x_rows(2, k, depth), :] + rims[k][0]
             two = x_rim_step(x_one, face, k, rims[k][1], factor, outer, depth, cols)
             last[linked[k], rim_rows, :] = old[k] + RATE * two
-        for slot in linked:
-            send_linked(slot)
 
     twos = []
-    for side, own, got in ((0, y_low_own, y_low), (1, y_up_own, y_up)):
-        c = side * (cols - 1)
+    for own, got in ((y_low_own, y_low), (y_up_own, y_up)):
         own_one = tile(own, 1, rows) + RATE * tile(got, 0, rows)
         one = tile(got, 1, rows) + RATE * tile(own, 0, rows)
         inner = tile(got, 2, rows)
-        squares = one * one + jnp.where(in_last_group(lane), inner, 0.0)
-        for face in range(2):
-            change = passed_on[side][pl.ds(2 * face * depth, depth), :]
-            column = jnp.sum(jnp.where(flat_lane == cols - 1 - c, change, 0.0), axis=1, keepdims=True)
-            line = jnp.sum(jnp.where(tall_row == tall_lane, 1.0, 0.0)[:depth] * column, axis=0, keepdims=True)
-            at_row = row == (0 if face == 0 else rows - 1)
-            squares = squares + jnp.where(at_row, jnp.broadcast_to(line, (rows, cols)), 0.0)
-        factor = 4.5 - 1.5 * group_sum(squares)
+        factor = 4.5 - 1.5 * group_sum(one * one + jnp.where(in_last_group(lane), inner, 0.0))
         twos.append(RATE * y_rim_step(one, factor, inner + own_one))
-    y_faces(last, twos, lists, depth, rows, cols, done=send_linked)
-    pltpu.make_async_copy(whole, result, sent).wait()
+    y_faces(last, twos, lists, depth, rows, cols)
+    each_unlinked("wait")
+
+
+def last_kernel(
+    slots, depth, rows, cols,
+    last_in, result_in, x_low_own, x_up_own, x_low, x_up, from_left, from_right, lists,
+    last, result,
+    sent,
+):
+    _, lane = row_and_lane(depth, cols)
+    scale = -1.5 * RATE * RATE
+    passed_on = (from_left, from_right)
+    part = lambda ref, i: ref[pl.ds(i * depth, depth), :]
+    corner_cells = lambda ref: ref[pl.ds(3 * LINKS * depth, depth), :]
+
+    def each_linked(face, act):
+        for k in range(LINKS):
+            slot = lists[face * SPAN + k]
+
+            @pl.when(slot < slots)
+            def _():
+                copy = pltpu.make_async_copy(last.at[slot, pl.ds(rows, depth * rows), :], result.at[slot], sent)
+                getattr(copy, act)()
+
+    for face, own, got in ((0, x_low_own, x_low), (1, x_up_own, x_up)):
+        total = jnp.zeros((depth, cols), jnp.float32)
+        for side in range(2):
+            place = side * LINKS
+            term = RATE * spin(part(passed_on[side], 3 * face + 1), place - (3 - side) * LINKS)
+            term = term * (2.0 * corner_cells(got) + term)
+            term = jnp.where((lane >= place) & (lane < place + LINKS), term, 0.0)
+            column = jnp.sum(term, axis=1, keepdims=True)
+            total = total + jnp.where(lane == side * (cols - 1), column, 0.0)
+        total = scale * total
+        rim_rows = pl.ds(rows + (0 if face == 0 else rows - 1), depth, stride=rows)
+        linked = [lists[face * SPAN + k] for k in range(LINKS)]
+        old = [last[slot, rim_rows, :] for slot in linked]
+        for k in range(LINKS):
+            _, one = x_rims(own, got, k, depth)
+            last[linked[k], rim_rows, :] = old[k] + total * one
+        each_linked(face, "start")
+
+    for side in range(2):
+        c = side * (cols - 1)
+        linked = [lists[(2 + side) * SPAN + k] for k in range(LINKS)]
+        for face, own in ((0, x_low_own), (1, x_up_own)):
+            place = (1 - side) * LINKS
+            one = part(passed_on[side], 3 * face + 2) + RATE * spin(corner_cells(own), place - (2 + side) * LINKS)
+            change = jnp.where(lane == cols - 1 - c, part(passed_on[side], 3 * face), 0.0)
+            one = scale * one * jnp.sum(change, axis=1, keepdims=True)
+            rim_rows = pl.ds(rows + (0 if face == 0 else rows - 1), depth, stride=rows)
+            old = [last[slot, rim_rows, :] for slot in linked]
+            for k in range(LINKS):
+                last[linked[k], rim_rows, :] = old[k] + jnp.where(lane == c, spin(one, c - place - k), 0.0)
+        each_linked(2 + side, "start")
+    for face in range(4):
+        each_linked(face, "wait")
 
 
 def shifted(block, axis, distance):
@@ -482,7 +526,7 @@
     ):
         changes = pl.pallas_call(
             functools.partial(body, depth, cols),
-            out_shape=shape(((2 if body is change_kernel else 4) * depth, cols), f32),
+            out_shape=shape(((3 if body is change_kernel else 6) * depth, cols), f32),
             in_specs=[vmem] * 3,
             out_specs=vmem,
             compiler_params=params,
@@ -505,19 +549,28 @@
         fixed, later, x_low, x_up, from_low, from_up, changes, lists,
     )
 
-    _, result = pl.pallas_call(
-        functools.partial(last_kernel, *sizes),
-        out_shape=[padded, shape(field.shape, f32)],
-        in_specs=[vmem] * 11 + [smem],
+    out_shape = [padded, pltpu.HBM(field.shape, f32)]
+    last, result = pl.pallas_call(
+        functools.partial(rims_kernel, *sizes),
+        out_shape=out_shape,
+        in_specs=[vmem] * 9 + [smem],
         out_specs=[vmem, hbm],
         scratch_shapes=[rims, pltpu.SemaphoreType.DMA],
         input_output_aliases={0: 0},
         compiler_params=params,
-        name="last_rims",
-    )(
-        last, x_low, x_up, from_low, from_up,
-        y_low, y_up, from_left, from_right, changes_from_left, changes_from_right, lists,
-    )
+        name="rims",
+    )(last, x_low, x_up, from_low, from_up, y_low, y_up, from_left, from_right, lists)
+
+    _, result = pl.pallas_call(
+        functools.partial(last_kernel, *sizes),
+        out_shape=out_shape,
+        in_specs=[vmem, hbm] + [vmem] * 6 + [smem],
+        out_specs=[vmem, hbm],
+        scratch_shapes=[pltpu.SemaphoreType.DMA],
+        input_output_aliases={0: 0, 1: 1},
+        compiler_params=params,
+        name="corners_last",
+    )(last, result, x_low, x_up, from_low, from_up, changes_from_left, changes_from_right, lists)
     return result.reshape(order_params.shape)
 
 

time: 21.5 us -> 21.6 us (level)
  waiting for transfers between devices: 4.47 us -> 3.3 us
  Pallas kernels: 9.36 us -> 10.5 us
    ppermute x6, waiting for transfers between devices: 4.47 us -> 3.3 us  [shifted(): lax.ppermute(block, axis, [((i - distance) % size, i) for i in range(size)])]
    pallas_call x3 -> x4, Pallas kernels: 1.84 us -> 3.01 us  [the longest x1 1.69 us: on_device(): pl.pallas_call(functools.partial(last_kernel, *sizes), out_shape=out_shap...]
    pallas_call x1, Pallas kernels: 1.26 us -> 0.98 us  [on_device(): pl.pallas_call(functools.partial(y_kernel, *sizes), out_shape=[y_pack, y_...]
    pallas_call x1, Pallas kernels: 2.75 us -> 2.97 us  [on_device(): pl.pallas_call(functools.partial(first_kernel, *sizes), out_shape=[padded...]
  transfers between devices with their start and end apart: 6 -> 6, of which waited for: 3 -> 3; matrix products, arithmetic and copies ran while one was open for 0% -> 0% of each run, Pallas kernels for 22% -> 27%
where the time goes in v5:
time: 21.6 us; the launch traced here: 21.2 us
  Pallas kernels  10.5 us (49%)
  starting transfers between devices  7.35 us (34%)
  waiting for transfers between devices  3.3 us (15%)
    ppermute x6, starting transfers between devices, shifted(): lax.ppermute(block, axis, [((i - distance) % size, i) for i in range(size)])  7.35 us
    ppermute x6, waiting for transfers between devices, shifted(): lax.ppermute(block, axis, [((i - distance) % size, i) for i in range(size)])  3.3 us
    pallas_call x1, Pallas kernels, on_device(): pl.pallas_call(functools.partial(first_kernel, *sizes), out_shape=[padded...  2.97 us
    pallas_call x1, Pallas kernels, on_device(): pl.pallas_call(functools.partial(second_kernel, *sizes), out_shape=[padde...  1.81 us
    pallas_call x1, Pallas kernels, on_device(): pl.pallas_call(functools.partial(third_kernel, *sizes), out_shape=[padded...  1.69 us
    pallas_call x1, Pallas kernels, on_device(): pl.pallas_call(functools.partial(last_kernel, *sizes), out_shape=out_shap...  1.69 us
    pallas_call x1, Pallas kernels, on_device(): pl.pallas_call(functools.partial(rims_kernel, *sizes), out_shape=out_shap...  1.28 us
    pallas_call x1, Pallas kernels, on_device(): pl.pallas_call(functools.partial(y_kernel, *sizes), out_shape=[y_pack, y_...  0.98 us
  transfers between devices with their start and end apart: 6, of which 3 were waited for; matrix products, arithmetic and copies ran while one was open for 0% of the time, Pallas kernels for 27%

profile of v5, /device:TPU:0, one launch (start us, length us, event | category | flops | bytes accessed | tf_op | source)
XLA Modules:
  0.0 21.2 jit_solution(1587844190089882115)
XLA Ops:
  0.0 3.0 %first_step.1 = (f32[25,112,128]{2,1,0:T(8,128)S(1)}, f32[25,112,128]{2,1,0:T(8,128)S(1)}, f32[96,128]{1,0:T(8,128)S(1)}, f32[240,128]{1,0:T(8,128)S(1)}, f32[240,128]{1,0:T(8,128)S(1)}, /*index=5*/s32[56]{0:T(128)S(1)}) custom-call(f32[24,96,128]{2,1,0:T(8,128)} %bitcast.2, s32[2,8,128]{2,1,0:T(8,128)} %planes.1, s32[1,1,24]{2,1,0:T(1,128)} %grains.1, ...), custom_call_target="tpu_custom_call" | custom-call | tf_op jit(solution)/shard_map/first_step/pallas_call | solution.py:479
  3.0 3.0 %collective-permute-start.2 = (f32[240,128]{1,0:T(8,128)S(1)}, f32[240,128]{1,0:T(8,128)S(1)}, u32[]{:S(2)}, u32[]{:S(2)}) collective-permute-start(f32[240,128]{1,0:T(8,128)S(1)} %get-tuple-element.28.own.x_up_own), channel_id=1, source_target_pairs={{28,0},{0,4},{4,8},{8,12},{12,16},{16,20},{20,24},{24,28},{29,1},{... | collective-permute-start | bytes 368648 | tf_op jit(solution)/shard_map/ppermute | solution.py:459
  6.0 3.1 %collective-permute-start.3 = (f32[240,128]{1,0:T(8,128)S(1)}, f32[240,128]{1,0:T(8,128)S(1)}, u32[]{:S(2)}, u32[]{:S(2)}) collective-permute-start(f32[240,128]{1,0:T(8,128)S(1)} %get-tuple-element.27.own.x_low_own), channel_id=1, source_target_pairs={{4,0},{8,4},{12,8},{16,12},{20,16},{24,20},{28,24},{0,28},{5,1},{9... | collective-permute-start | bytes 368648 | tf_op jit(solution)/shard_map/ppermute | solution.py:459
  9.1 1.0 %y_rims.1 = (f32[24,128]{1,0:T(8,128)S(1)}, f32[24,128]{1,0:T(8,128)S(1)}) custom-call(f32[25,112,128]{2,1,0:T(8,128)S(1)} %get-tuple-element.20.now, f32[25,112,128]{2,1,0:T(8,128)S(1)} %get-tuple-element.19.stepped.stepped_in, f32[96,128]{1,0:T(8,128)S(1)} %get-tuple-element.21.squares, s32[56]{0:T(128)S(1)} %get-tuple-element.22.lists), custom_call_target="tpu_custom_call" | custom-call | flops 5898240 | bytes 2359296 | tf_op jit(solution)/shard_map/y_rims/pallas_call | solution.py:498
  10.1 0.7 %collective-permute-start.1 = (f32[24,128]{1,0:T(8,128)S(1)}, f32[24,128]{1,0:T(8,128)S(1)}, u32[]{:S(2)}, u32[]{:S(2)}) collective-permute-start(f32[24,128]{1,0:T(8,128)S(1)} %get-tuple-element.23.y_low_own), channel_id=1, source_target_pairs={{1,0},{2,1},{3,2},{0,3},{5,4},{6,5},{7,6},{4,7},{9,8},{10,9},{11,1... | collective-permute-start | bytes 36872 | tf_op jit(solution)/shard_map/ppermute | solution.py:459
  10.7 0.0 collective-permute-start
  10.8 1.4 %collective-permute-done.1.y_up = f32[24,128]{1,0:T(8,128)S(1)} collective-permute-done((f32[24,128]{1,0:T(8,128)S(1)}, f32[24,128]{1,0:T(8,128)S(1)}, u32[]{:S(2)}, u32[]{:S(2)}) %collective-permute-start.1) | collective-permute-done | bytes 12320 | tf_op jit(solution)/shard_map/ppermute | solution.py:459
  12.2 1.7 %collective-permute-done.y_low = f32[24,128]{1,0:T(8,128)S(1)} collective-permute-done((f32[24,128]{1,0:T(8,128)S(1)}, f32[24,128]{1,0:T(8,128)S(1)}, u32[]{:S(2)}, u32[]{:S(2)}) %collective-permute-start) | collective-permute-done | bytes 12320 | tf_op jit(solution)/shard_map/ppermute | solution.py:459
  13.9 1.8 %second_step.1 = (f32[25,112,128]{2,1,0:T(8,128)S(1)}, f32[25,112,128]{2,1,0:T(8,128)S(1)}) custom-call(f32[25,112,128]{2,1,0:T(8,128)S(1)} %get-tuple-element.19.stepped.stepped_in, f32[24,128]{1,0:T(8,128)S(1)} %get-tuple-element.23.y_low_own, f32[24,128]{1,0:T(8,128)S(1)} %get-tuple-element.24.y_up_own, ...), custom_call_target="tpu_custom_call", output_to_operand_aliasing={{0}: (0, {})} | custom-call | flops 5898240 | bytes 2359296 | tf_op jit(solution)/shard_map/second_step/pallas_call | solution.py:511
  15.7 0.0 collective-permute-done.2.got.x_low
  15.7 0.0 collective-permute-done.3.got.x_up
  15.8 0.4 %collective-permute-start.5 = (f32[72,128]{1,0:T(8,128)S(1)}, f32[72,128]{1,0:T(8,128)S(1)}, u32[]{:S(2)}, u32[]{:S(2)}) collective-permute-start(f32[72,128]{1,0:T(8,128)S(1)} %corners_up.1.changes), channel_id=1, source_target_pairs={{1,0},{2,1},{3,2},{0,3},{5,4},{6,5},{7,6},{4,7},{9,8},{10,9},{11,1... | collective-permute-start | bytes 110600 | tf_op jit(solution)/shard_map/ppermute | solution.py:459
  16.1 0.2 collective-permute-start.4
  16.3 1.7 %third_step.1 = (f32[25,112,128]{2,1,0:T(8,128)S(1)}, f32[25,112,128]{2,1,0:T(8,128)S(1)}) custom-call(f32[25,112,128]{2,1,0:T(8,128)S(1)} %get-tuple-element.25.now, f32[25,112,128]{2,1,0:T(8,128)S(1)} %get-tuple-element.26.before.later_in, f32[240,128]{1,0:T(8,128)S(1)} %get-tuple-element.27.own.x_low_own, ...), custom_call_target="tpu_custom_call", output_to_operand_aliasing={{0}: (1, {})} | custom-call | tf_op jit(solution)/shard_map/third_step/pallas_call | solution.py:539
  18.0 1.3 %rims.1 = (f32[25,112,128]{2,1,0:T(8,128)S(1)}, f32[24,96,128]{2,1,0:T(8,128)}) custom-call(f32[25,112,128]{2,1,0:T(8,128)S(1)} %get-tuple-element.29.last_in, f32[240,128]{1,0:T(8,128)S(1)} %get-tuple-element.27.own.x_low_own, f32[240,128]{1,0:T(8,128)S(1)} %get-tuple-element.28.own.x_up_own, ...), custom_call_target="tpu_custom_call", output_to_operand_aliasing={{0}: (0, {})} | custom-call | tf_op jit(solution)/shard_map/rims/pallas_call | solution.py:553
  19.3 0.0 collective-permute-done.5.from_right
  19.3 0.2 collective-permute-done.4.from_left
  19.5 1.7 %corners_last.1 = (f32[25,112,128]{2,1,0:T(8,128)S(1)}, f32[24,96,128]{2,1,0:T(8,128)}) custom-call(f32[25,112,128]{2,1,0:T(8,128)S(1)} %get-tuple-element.30.last_in, f32[24,96,128]{2,1,0:T(8,128)} %get-tuple-element.31.result_in, f32[240,128]{1,0:T(8,128)S(1)} %get-tuple-element.27.own.x_low_own, ...), custom_call_target="tpu_custom_call", output_to_operand_aliasing={{0}: (0, {}), {1}: (1, {})} | custom-call | tf_op jit(solution)/shard_map/corners_last/pallas_call | solution.py:564
  (2 shorter events, 0.0 us)
Async XLA Ops:
  3.0 12.7 %collective-permute-start.2 = (f32[240,128]{1,0:T(8,128)S(1)}, f32[240,128]{1,0:T(8,128)S(1)}, u32[]{:S(2)}, u32[]{:S(2)}) collective-permute-start(f32[240,128]{1,0:T(8,128)S(1)} %get-tuple-element.28.own.x_up_own), channel_id=1, source_target_pairs={{28,0},{0,4},{4,8},{8,12},{12,16},{16,20},{20,24},{24,28},{29,1},{... | collective-permute-start | bytes 368648 | tf_op jit(solution)/shard_map/ppermute | solution.py:459
  6.0 9.7 %collective-permute-start.3 = (f32[240,128]{1,0:T(8,128)S(1)}, f32[240,128]{1,0:T(8,128)S(1)}, u32[]{:S(2)}, u32[]{:S(2)}) collective-permute-start(f32[240,128]{1,0:T(8,128)S(1)} %get-tuple-element.27.own.x_low_own), channel_id=1, source_target_pairs={{4,0},{8,4},{12,8},{16,12},{20,16},{24,20},{28,24},{0,28},{5,1},{9... | collective-permute-start | bytes 368648 | tf_op jit(solution)/shard_map/ppermute | solution.py:459
  10.1 2.1 %collective-permute-start.1 = (f32[24,128]{1,0:T(8,128)S(1)}, f32[24,128]{1,0:T(8,128)S(1)}, u32[]{:S(2)}, u32[]{:S(2)}) collective-permute-start(f32[24,128]{1,0:T(8,128)S(1)} %get-tuple-element.23.y_low_own), channel_id=1, source_target_pairs={{1,0},{2,1},{3,2},{0,3},{5,4},{6,5},{7,6},{4,7},{9,8},{10,9},{11,1... | collective-permute-start | bytes 36872 | tf_op jit(solution)/shard_map/ppermute | solution.py:459
  10.7 3.1 %collective-permute-start = (f32[24,128]{1,0:T(8,128)S(1)}, f32[24,128]{1,0:T(8,128)S(1)}, u32[]{:S(2)}, u32[]{:S(2)}) collective-permute-start(f32[24,128]{1,0:T(8,128)S(1)} %get-tuple-element.24.y_up_own), channel_id=1, source_target_pairs={{3,0},{0,1},{1,2},{2,3},{7,4},{4,5},{5,6},{6,7},{11,8},{8,9},{9,10... | collective-permute-start | bytes 36872 | tf_op jit(solution)/shard_map/ppermute | solution.py:459
  15.8 3.6 %collective-permute-start.5 = (f32[72,128]{1,0:T(8,128)S(1)}, f32[72,128]{1,0:T(8,128)S(1)}, u32[]{:S(2)}, u32[]{:S(2)}) collective-permute-start(f32[72,128]{1,0:T(8,128)S(1)} %corners_up.1.changes), channel_id=1, source_target_pairs={{1,0},{2,1},{3,2},{0,3},{5,4},{6,5},{7,6},{4,7},{9,8},{10,9},{11,1... | collective-permute-start | bytes 110600 | tf_op jit(solution)/shard_map/ppermute | solution.py:459
  16.1 3.4 %collective-permute-start.4 = (f32[72,128]{1,0:T(8,128)S(1)}, f32[72,128]{1,0:T(8,128)S(1)}, u32[]{:S(2)}, u32[]{:S(2)}) collective-permute-start(f32[72,128]{1,0:T(8,128)S(1)} %corners_up.1.changes), channel_id=1, source_target_pairs={{3,0},{0,1},{1,2},{2,3},{7,4},{4,5},{5,6},{6,7},{11,8},{8,9},{9,10... | collective-permute-start | bytes 110600 | tf_op jit(solution)/shard_map/ppermute | solution.py:459

commit v6 on v5

--- a/solution.py
+++ b/solution.py
@@ -12,7 +12,8 @@
 SPAN = 8
 GROUP = 16
 RATE = 0.1
-UNROLL = 4
+UNROLL = 2
+PART = 4
 
 
 def row_and_lane(rows, cols):
@@ -35,7 +36,7 @@
     return tile
 
 
-def step(src, dst, slots, depth, rows, cols, squares=None, wait=None, beside=None, carried=()):
+def step(src, dst, slots, depth, rows, cols, squares=None, wait=None):
     row, lane = row_and_lane(rows, cols)
     first_row, last_row = row == 0, row == rows - 1
     first_lane, last_lane = lane == 0, lane == cols - 1
@@ -68,36 +69,37 @@
             squares[pl.ds(pl.multiple_of(z * rows, rows), rows), :] = total(parts)
         return 4.5 - 1.5 * total(following)
 
-    def layers(i, carry):
-        factor, *carried = carry
+    def layers(i, factor):
         if wait is not None:
-            pl.when(i + 1 < depth // UNROLL)(lambda: wait(i + 1))
-        if beside is not None:
-            carried = beside(i, carried)
+            turns = PART // UNROLL
+            pl.when((i % turns == turns - 1) & (i < depth // UNROLL - 1))(lambda: wait(i // turns + 1))
         for j in range(UNROLL):
             factor = layer(i * UNROLL + j, factor)
-        return (factor, *carried)
+        return factor
 
     first = [None] * 4
     for s in range(slots):
         v = src[s, at(0), :]
         add(first, s, v * v)
-    lax.fori_loop(0, depth // UNROLL, layers, (4.5 - 1.5 * total(first), *carried))
+    lax.fori_loop(0, depth // UNROLL, layers, 4.5 - 1.5 * total(first))
 
 
 def gather_columns(ref, low, up, depth, rows, cols, beside=False):
     _, lane = row_and_lane(rows, cols)
     shifts = (0, -1, 1, -2) if beside else (0, -1)
-    results = [jnp.zeros((rows, cols), jnp.float32)] * len(shifts)
-    for k in range(LINKS):
-        parts = [jnp.zeros((rows, cols), jnp.float32)] * len(shifts)
+
+    def link(i, results):
+        results = [spin(result, GROUP) for result in results]
+        low_slot, up_slot = low(LINKS - 1 - i), up(LINKS - 1 - i)
         for z in range(depth):
             at = pl.ds((z + 1) * rows, rows)
-            place = GROUP * k + z
-            moved = spin(jnp.where(lane < cols // 2, ref[low[k], at, :], ref[up[k], at, :]), place)
-            for i, shift in enumerate(shifts):
-                parts[i] = jnp.where(lane == (place + shift) % cols, moved, parts[i])
-        results = [result + part for result, part in zip(results, parts)]
+            moved = spin(jnp.where(lane < cols // 2, ref[low_slot, at, :], ref[up_slot, at, :]), z)
+            for j, shift in enumerate(shifts):
+                results[j] = jnp.where(lane == (z + shift) % cols, moved, results[j])
+        return tuple(results)
+
+    empty = jnp.zeros((rows, cols), jnp.float32)
+    results = lax.fori_loop(0, LINKS, link, (empty,) * len(shifts))
     return [spin(result, -shift) for result, shift in zip(results, shifts)]
 
 
@@ -116,7 +118,7 @@
         pltpu.make_async_copy(grains, grains_in, arrived.at[1]),
         pltpu.make_async_copy(planes, planes_in, arrived.at[2]),
     ]
-    part = UNROLL * rows
+    part = PART * rows
 
     def field_part(i):
         to = pl.ds(pl.multiple_of(i * part + rows, rows), part)
@@ -125,22 +127,45 @@
 
     for copy in copies:
         copy.start()
-    for i in range(depth // UNROLL):
+    for i in range(depth // PART):
         field_part(i).start()
     for ref in (now, stepped):
         ref[slots] = jnp.zeros(((depth + 2) * rows, cols), jnp.float32)
-    for face in range(4):
-        for place in range(SPAN):
-            lists[face * SPAN + place] = slots
-    for t in range(slots + 1):
+
+    for place in range(4 * SPAN):
+        lists[place] = slots
+
+    def empty(t, carry):
         inverse[t] = slots
-        inverse[slots + 1 + t] = slots
-
-    copies[0].wait()
-    for s in range(slots):
+        return carry
+
+    def invert(s, carry):
         for face in (0, 2):
             partner = maps_in[0, 0, face, s]
             inverse[face // 2 * (slots + 1) + jnp.where(partner >= 0, partner, slots)] = s
+        return carry
+
+    def enlist(s, counts):
+        partners = [maps_in[0, 0, face, s] for face in range(4)]
+        best = jnp.maximum(jnp.maximum(partners[0], partners[1]), jnp.maximum(partners[2], partners[3]))
+        lists[4 * SPAN + s] = (best >= 0).astype(jnp.int32)
+        following = []
+        for face in range(4):
+            if face in (1, 3):
+                valid = partners[face] >= 0
+                slot = jnp.where(valid, s, slots)
+            else:
+                slot = inverse[face // 2 * (slots + 1) + s]
+                valid = slot < slots
+            lists[counts[face]] = slot
+            following.append(counts[face] + valid.astype(jnp.int32))
+        return tuple(following)
+
+    lax.fori_loop(0, 2 * (slots + 1), empty, 0)
+    copies[0].wait()
+    lax.fori_loop(0, slots, invert, 0)
+    lax.fori_loop(0, slots, enlist, tuple(jnp.int32(face * SPAN) for face in range(4)))
+
     top = (depth + 1) * rows
     copies[1].wait()
     copies[2].wait()
@@ -153,31 +178,7 @@
             ref[s, pl.ds(top, rows), :] = above
     field_part(0).wait()
 
-    share = -(-slots // (depth // UNROLL))
-
-    def enlist(i, counts):
-        for j in range(share):
-            s = i * share + j
-            s = s if slots % share == 0 else jnp.minimum(s, slots - 1)
-            fresh = True if slots % share == 0 else i * share + j < slots
-            partners = [maps_in[0, 0, face, s] for face in range(4)]
-            best = jnp.maximum(jnp.maximum(partners[0], partners[1]), jnp.maximum(partners[2], partners[3]))
-            lists[4 * SPAN + s] = (best >= 0).astype(jnp.int32)
-            for face in range(4):
-                if face in (1, 3):
-                    valid = partners[face] >= 0
-                    slot = jnp.where(valid, s, slots)
-                else:
-                    slot = inverse[face // 2 * (slots + 1) + s]
-                    valid = slot < slots
-                lists[counts[face]] = slot
-                counts[face] = counts[face] + (valid & fresh).astype(jnp.int32)
-        return counts
-
-    step(
-        now, stepped, slots, depth, rows, cols, squares,
-        lambda i: field_part(i).wait(), enlist, [jnp.int32(face * SPAN) for face in range(4)],
-    )
+    step(now, stepped, slots, depth, rows, cols, squares, lambda i: field_part(i).wait())
 
     linked = [[lists[face * SPAN + k] for k in range(LINKS)] for face in range(4)]
     end = 3 * LINKS * depth
@@ -215,7 +216,7 @@
 def y_kernel(slots, depth, rows, cols, now, stepped, squares, lists, y_low, y_up):
     top = (depth + 1) * rows
     _, lane = row_and_lane(rows, cols)
-    low, up = ([lists[face * SPAN + k] for k in range(LINKS)] for face in (2, 3))
+    low, up = (lambda k: lists[2 * SPAN + k]), (lambda k: lists[3 * SPAN + k])
     rims = gather_columns(now, low, up, depth, rows, cols)
     *partials, inner_low, inner_up = gather_columns(stepped, low, up, depth, rows, cols, beside=True)
     frozen = [jnp.zeros((rows, cols), jnp.float32)] * 2
@@ -224,7 +225,7 @@
         for z, at in ((0, 0), (depth - 1, top)):
             place = GROUP * k + z
             at = pl.ds(at, rows)
-            moved = spin(jnp.where(lane < cols // 2, now[low[k], at, :], now[up[k], at, :]), place)
+            moved = spin(jnp.where(lane < cols // 2, now[low(k), at, :], now[up(k), at, :]), place)
             for side in range(2):
                 frozen[side] = jnp.where(lane == (place - side) % cols, moved, frozen[side])
     for z in range(depth):
@@ -247,19 +248,22 @@
     return ref[pl.ds(i * rows, rows), :]
 
 
-def y_faces(ref, tiles, lists, depth, rows, cols, replace=False, done=None):
+def y_faces(ref, tiles, lists, depth, rows, cols, replace=False):
     _, lane = row_and_lane(rows, cols)
-    for k in range(LINKS):
+    ats = [pl.ds((z + 1) * rows, rows) for z in range(depth)]
+
+    def link(k, tiles):
+        linked = [lists[(2 + side) * SPAN + k] for side in range(2)]
+        old = [[ref[slot, at, :] for at in ats] for slot in linked]
         for side in range(2):
             c = side * (cols - 1)
-            slot = lists[(2 + side) * SPAN + k]
-            ats = [pl.ds((z + 1) * rows, rows) for z in range(depth)]
-            old = [ref[slot, at, :] for at in ats]
             for z in range(depth):
-                moved = spin(tiles[side], c - GROUP * k - z)
-                ref[slot, ats[z], :] = jnp.where(lane == c, moved if replace else old[z] + moved, old[z])
-            if done is not None:
-                done(slot)
+                moved = spin(tiles[side], c - z)
+                new = jnp.where(lane == c, moved if replace else old[side][z] + moved, old[side][z])
+                ref[linked[side], ats[z], :] = new
+        return tuple(spin(tile, -GROUP) for tile in tiles)
+
+    lax.fori_loop(0, LINKS, link, tuple(tiles))
 
 
 def second_kernel(
@@ -486,7 +490,7 @@
             pltpu.SMEM(grain_ids.shape, jnp.int32),
             pltpu.SMEM(channel_maps.shape, jnp.int32),
             pltpu.SMEM((2 * (slots + 1),), jnp.int32),
-            pltpu.SemaphoreType.DMA((3 + depth // UNROLL,)),
+            pltpu.SemaphoreType.DMA((3 + depth // PART,)),
         ],
         compiler_params=params,
         name="first_step",

time: 21.6 us -> 24.1 us (1.12)
  Pallas kernels: 10.5 us -> 13.1 us
    pallas_call x1, Pallas kernels: 1.81 us -> 2.72 us  [on_device(): pl.pallas_call(functools.partial(second_kernel, *sizes), out_shape=[padde...]
    pallas_call x1, Pallas kernels: 0.98 us -> 1.89 us  [on_device(): pl.pallas_call(functools.partial(y_kernel, *sizes), out_shape=[y_pack, y_...]
    pallas_call x1, Pallas kernels: 2.97 us -> 3.44 us  [on_device(): pl.pallas_call(functools.partial(first_kernel, *sizes), out_shape=[padded...]
  transfers between devices with their start and end apart: 6 -> 6, of which waited for: 3 -> 2; matrix products, arithmetic and copies ran while one was open for 0% -> 0% of each run, Pallas kernels for 27% -> 34%
where the time goes in v6:
time: 24.1 us; the launch traced here: 23.7 us
  Pallas kernels  13.1 us (54%)
  starting transfers between devices  7.34 us (30%)
  waiting for transfers between devices  3.13 us (13%)
    ppermute x6, starting transfers between devices, shifted(): lax.ppermute(block, axis, [((i - distance) % size, i) for i in range(size)])  7.34 us
    pallas_call x1, Pallas kernels, on_device(): pl.pallas_call(functools.partial(first_kernel, *sizes), out_shape=[padded...  3.44 us
    ppermute x6, waiting for transfers between devices, shifted(): lax.ppermute(block, axis, [((i - distance) % size, i) for i in range(size)])  3.13 us
    pallas_call x1, Pallas kernels, on_device(): pl.pallas_call(functools.partial(second_kernel, *sizes), out_shape=[padde...  2.72 us
    pallas_call x1, Pallas kernels, on_device(): pl.pallas_call(functools.partial(third_kernel, *sizes), out_shape=[padded...  1.89 us
    pallas_call x1, Pallas kernels, on_device(): pl.pallas_call(functools.partial(y_kernel, *sizes), out_shape=[y_pack, y_...  1.89 us
    pallas_call x1, Pallas kernels, on_device(): pl.pallas_call(functools.partial(last_kernel, *sizes), out_shape=out_shap...  1.7 us
    pallas_call x1, Pallas kernels, on_device(): pl.pallas_call(functools.partial(rims_kernel, *sizes), out_shape=out_shap...  1.43 us
  transfers between devices with their start and end apart: 6, of which 2 were waited for; matrix products, arithmetic and copies ran while one was open for 0% of the time, Pallas kernels for 34%

profile of v6, /device:TPU:0, one launch (start us, length us, event | category | flops | bytes accessed | tf_op | source)
XLA Modules:
  0.0 23.7 jit_solution(4326321820457824280)
XLA Ops:
  0.0 3.4 %first_step.1 = (f32[25,112,128]{2,1,0:T(8,128)S(1)}, f32[25,112,128]{2,1,0:T(8,128)S(1)}, f32[96,128]{1,0:T(8,128)S(1)}, f32[240,128]{1,0:T(8,128)S(1)}, f32[240,128]{1,0:T(8,128)S(1)}, /*index=5*/s32[56]{0:T(128)S(1)}) custom-call(f32[24,96,128]{2,1,0:T(8,128)} %bitcast.2, s32[2,8,128]{2,1,0:T(8,128)} %planes.1, s32[1,1,24]{2,1,0:T(1,128)} %grains.1, ...), custom_call_target="tpu_custom_call" | custom-call | tf_op jit(solution)/shard_map/first_step/pallas_call | solution.py:483
  3.5 3.0 %collective-permute-start.2 = (f32[240,128]{1,0:T(8,128)S(1)}, f32[240,128]{1,0:T(8,128)S(1)}, u32[]{:S(2)}, u32[]{:S(2)}) collective-permute-start(f32[240,128]{1,0:T(8,128)S(1)} %get-tuple-element.28.own.x_up_own), channel_id=1, source_target_pairs={{28,0},{0,4},{4,8},{8,12},{12,16},{16,20},{20,24},{24,28},{29,1},{... | collective-permute-start | bytes 368648 | tf_op jit(solution)/shard_map/ppermute | solution.py:463
  6.4 3.1 %collective-permute-start.3 = (f32[240,128]{1,0:T(8,128)S(1)}, f32[240,128]{1,0:T(8,128)S(1)}, u32[]{:S(2)}, u32[]{:S(2)}) collective-permute-start(f32[240,128]{1,0:T(8,128)S(1)} %get-tuple-element.27.own.x_low_own), channel_id=1, source_target_pairs={{4,0},{8,4},{12,8},{16,12},{20,16},{24,20},{28,24},{0,28},{5,1},{9... | collective-permute-start | bytes 368648 | tf_op jit(solution)/shard_map/ppermute | solution.py:463
  9.5 1.9 %y_rims.1 = (f32[24,128]{1,0:T(8,128)S(1)}, f32[24,128]{1,0:T(8,128)S(1)}) custom-call(f32[25,112,128]{2,1,0:T(8,128)S(1)} %get-tuple-element.20.now, f32[25,112,128]{2,1,0:T(8,128)S(1)} %get-tuple-element.19.stepped.stepped_in, f32[96,128]{1,0:T(8,128)S(1)} %get-tuple-element.21.squares, s32[56]{0:T(128)S(1)} %get-tuple-element.22.lists), custom_call_target="tpu_custom_call" | custom-call | flops 5898240 | bytes 2359296 | tf_op jit(solution)/shard_map/y_rims/pallas_call | solution.py:502
  11.4 0.7 %collective-permute-start.1 = (f32[24,128]{1,0:T(8,128)S(1)}, f32[24,128]{1,0:T(8,128)S(1)}, u32[]{:S(2)}, u32[]{:S(2)}) collective-permute-start(f32[24,128]{1,0:T(8,128)S(1)} %get-tuple-element.23.y_low_own), channel_id=1, source_target_pairs={{1,0},{2,1},{3,2},{0,3},{5,4},{6,5},{7,6},{4,7},{9,8},{10,9},{11,1... | collective-permute-start | bytes 36872 | tf_op jit(solution)/shard_map/ppermute | solution.py:463
  12.1 0.0 collective-permute-start
  12.1 1.4 %collective-permute-done.1.y_up = f32[24,128]{1,0:T(8,128)S(1)} collective-permute-done((f32[24,128]{1,0:T(8,128)S(1)}, f32[24,128]{1,0:T(8,128)S(1)}, u32[]{:S(2)}, u32[]{:S(2)}) %collective-permute-start.1) | collective-permute-done | bytes 12320 | tf_op jit(solution)/shard_map/ppermute | solution.py:463
  13.5 1.7 %collective-permute-done.y_low = f32[24,128]{1,0:T(8,128)S(1)} collective-permute-done((f32[24,128]{1,0:T(8,128)S(1)}, f32[24,128]{1,0:T(8,128)S(1)}, u32[]{:S(2)}, u32[]{:S(2)}) %collective-permute-start) | collective-permute-done | bytes 12320 | tf_op jit(solution)/shard_map/ppermute | solution.py:463
  15.3 2.7 %second_step.1 = (f32[25,112,128]{2,1,0:T(8,128)S(1)}, f32[25,112,128]{2,1,0:T(8,128)S(1)}) custom-call(f32[25,112,128]{2,1,0:T(8,128)S(1)} %get-tuple-element.19.stepped.stepped_in, f32[24,128]{1,0:T(8,128)S(1)} %get-tuple-element.23.y_low_own, f32[24,128]{1,0:T(8,128)S(1)} %get-tuple-element.24.y_up_own, ...), custom_call_target="tpu_custom_call", output_to_operand_aliasing={{0}: (0, {})} | custom-call | flops 5898240 | bytes 2359296 | tf_op jit(solution)/shard_map/second_step/pallas_call | solution.py:515
  18.0 0.0 collective-permute-done.2.got.x_low
  18.0 0.0 collective-permute-done.3.got.x_up
  18.0 0.1 collective-permute-start.5
  18.1 0.5 %collective-permute-start.4 = (f32[72,128]{1,0:T(8,128)S(1)}, f32[72,128]{1,0:T(8,128)S(1)}, u32[]{:S(2)}, u32[]{:S(2)}) collective-permute-start(f32[72,128]{1,0:T(8,128)S(1)} %corners_up.1.changes), channel_id=1, source_target_pairs={{3,0},{0,1},{1,2},{2,3},{7,4},{4,5},{5,6},{6,7},{11,8},{8,9},{9,10... | collective-permute-start | bytes 110600 | tf_op jit(solution)/shard_map/ppermute | solution.py:463
  18.6 1.9 %third_step.1 = (f32[25,112,128]{2,1,0:T(8,128)S(1)}, f32[25,112,128]{2,1,0:T(8,128)S(1)}) custom-call(f32[25,112,128]{2,1,0:T(8,128)S(1)} %get-tuple-element.25.now, f32[25,112,128]{2,1,0:T(8,128)S(1)} %get-tuple-element.26.before.later_in, f32[240,128]{1,0:T(8,128)S(1)} %get-tuple-element.27.own.x_low_own, ...), custom_call_target="tpu_custom_call", output_to_operand_aliasing={{0}: (1, {})} | custom-call | tf_op jit(solution)/shard_map/third_step/pallas_call | solution.py:543
  20.5 1.4 %rims.1 = (f32[25,112,128]{2,1,0:T(8,128)S(1)}, f32[24,96,128]{2,1,0:T(8,128)}) custom-call(f32[25,112,128]{2,1,0:T(8,128)S(1)} %get-tuple-element.29.last_in, f32[240,128]{1,0:T(8,128)S(1)} %get-tuple-element.27.own.x_low_own, f32[240,128]{1,0:T(8,128)S(1)} %get-tuple-element.28.own.x_up_own, ...), custom_call_target="tpu_custom_call", output_to_operand_aliasing={{0}: (0, {})} | custom-call | tf_op jit(solution)/shard_map/rims/pallas_call | solution.py:557
  21.9 0.0 collective-permute-done.5.from_right
  22.0 0.0 collective-permute-done.4.from_left
  22.0 1.7 %corners_last.1 = (f32[25,112,128]{2,1,0:T(8,128)S(1)}, f32[24,96,128]{2,1,0:T(8,128)}) custom-call(f32[25,112,128]{2,1,0:T(8,128)S(1)} %get-tuple-element.30.last_in, f32[24,96,128]{2,1,0:T(8,128)} %get-tuple-element.31.result_in, f32[240,128]{1,0:T(8,128)S(1)} %get-tuple-element.27.own.x_low_own, ...), custom_call_target="tpu_custom_call", output_to_operand_aliasing={{0}: (0, {}), {1}: (1, {})} | custom-call | tf_op jit(solution)/shard_map/corners_last/pallas_call | solution.py:568
  (2 shorter events, 0.0 us)
Async XLA Ops:
  3.5 14.5 %collective-permute-start.2 = (f32[240,128]{1,0:T(8,128)S(1)}, f32[240,128]{1,0:T(8,128)S(1)}, u32[]{:S(2)}, u32[]{:S(2)}) collective-permute-start(f32[240,128]{1,0:T(8,128)S(1)} %get-tuple-element.28.own.x_up_own), channel_id=1, source_target_pairs={{28,0},{0,4},{4,8},{8,12},{12,16},{16,20},{20,24},{24,28},{29,1},{... | collective-permute-start | bytes 368648 | tf_op jit(solution)/shard_map/ppermute | solution.py:463
  6.4 11.6 %collective-permute-start.3 = (f32[240,128]{1,0:T(8,128)S(1)}, f32[240,128]{1,0:T(8,128)S(1)}, u32[]{:S(2)}, u32[]{:S(2)}) collective-permute-start(f32[240,128]{1,0:T(8,128)S(1)} %get-tuple-element.27.own.x_low_own), channel_id=1, source_target_pairs={{4,0},{8,4},{12,8},{16,12},{20,16},{24,20},{28,24},{0,28},{5,1},{9... | collective-permute-start | bytes 368648 | tf_op jit(solution)/shard_map/ppermute | solution.py:463
  11.4 2.1 %collective-permute-start.1 = (f32[24,128]{1,0:T(8,128)S(1)}, f32[24,128]{1,0:T(8,128)S(1)}, u32[]{:S(2)}, u32[]{:S(2)}) collective-permute-start(f32[24,128]{1,0:T(8,128)S(1)} %get-tuple-element.23.y_low_own), channel_id=1, source_target_pairs={{1,0},{2,1},{3,2},{0,3},{5,4},{6,5},{7,6},{4,7},{9,8},{10,9},{11,1... | collective-permute-start | bytes 36872 | tf_op jit(solution)/shard_map/ppermute | solution.py:463
  12.1 3.1 %collective-permute-start = (f32[24,128]{1,0:T(8,128)S(1)}, f32[24,128]{1,0:T(8,128)S(1)}, u32[]{:S(2)}, u32[]{:S(2)}) collective-permute-start(f32[24,128]{1,0:T(8,128)S(1)} %get-tuple-element.24.y_up_own), channel_id=1, source_target_pairs={{3,0},{0,1},{1,2},{2,3},{7,4},{4,5},{5,6},{6,7},{11,8},{8,9},{9,10... | collective-permute-start | bytes 36872 | tf_op jit(solution)/shard_map/ppermute | solution.py:463
  18.0 3.9 %collective-permute-start.5 = (f32[72,128]{1,0:T(8,128)S(1)}, f32[72,128]{1,0:T(8,128)S(1)}, u32[]{:S(2)}, u32[]{:S(2)}) collective-permute-start(f32[72,128]{1,0:T(8,128)S(1)} %corners_up.1.changes), channel_id=1, source_target_pairs={{1,0},{2,1},{3,2},{0,3},{5,4},{6,5},{7,6},{4,7},{9,8},{10,9},{11,1... | collective-permute-start | bytes 110600 | tf_op jit(solution)/shard_map/ppermute | solution.py:463
  18.1 3.8 %collective-permute-start.4 = (f32[72,128]{1,0:T(8,128)S(1)}, f32[72,128]{1,0:T(8,128)S(1)}, u32[]{:S(2)}, u32[]{:S(2)}) collective-permute-start(f32[72,128]{1,0:T(8,128)S(1)} %corners_up.1.changes), channel_id=1, source_target_pairs={{3,0},{0,1},{1,2},{2,3},{7,4},{4,5},{5,6},{6,7},{11,8},{8,9},{9,10... | collective-permute-start | bytes 110600 | tf_op jit(solution)/shard_map/ppermute | solution.py:463

commit v7 on v4

--- a/solution.py
+++ b/solution.py
@@ -12,7 +12,7 @@
 SPAN = 8
 GROUP = 16
 RATE = 0.1
-UNROLL = 4
+PART = 4
 
 
 def row_and_lane(rows, cols):
@@ -47,15 +47,16 @@
         return (parts[0] + parts[1]) + (parts[2] + parts[3])
 
     def at(z):
-        return pl.ds(pl.multiple_of((z + 1) * rows, rows), rows)
+        return pl.ds((z + 1) * rows, rows)
 
     def layer(z, factor):
         following, parts = [None] * 4, [None] * 4
         for s in range(slots):
             v, below, above = src[s, at(z), :], src[s, at(z - 1), :], src[s, at(z + 1), :]
             add(following, s, above * above)
-            x_sum = jnp.where(first_row, 0.0, pltpu.roll(v, 1, 0)) + jnp.where(
-                last_row, 0.0, pltpu.roll(v, rows - 1, 0)
+            base = (z + 1) * rows
+            x_sum = jnp.where(first_row, 0.0, src[s, pl.ds(base - 1, rows), :]) + jnp.where(
+                last_row, 0.0, src[s, pl.ds(base + 1, rows), :]
             )
             y_sum = jnp.where(first_lane, 0.0, pltpu.roll(v, 1, 1)) + jnp.where(
                 last_lane, 0.0, pltpu.roll(v, cols - 1, 1)
@@ -65,38 +66,34 @@
             if squares is not None:
                 add(parts, s, new * new)
         if squares is not None:
-            squares[pl.ds(pl.multiple_of(z * rows, rows), rows), :] = total(parts)
+            squares[pl.ds(z * rows, rows), :] = total(parts)
         return 4.5 - 1.5 * total(following)
-
-    def layers(i, factor):
-        if wait is not None:
-            pl.when(i + 1 < depth // UNROLL)(lambda: wait(i + 1))
-        for j in range(UNROLL):
-            factor = layer(i * UNROLL + j, factor)
-        return factor
 
     first = [None] * 4
     for s in range(slots):
         v = src[s, at(0), :]
         add(first, s, v * v)
-    lax.fori_loop(0, depth // UNROLL, layers, 4.5 - 1.5 * total(first))
-
-
-def gather_columns(ref, linked, c, depth, rows, cols, beside=0):
+    factor = 4.5 - 1.5 * total(first)
+    for z in range(depth):
+        if wait is not None and z % PART == PART - 1 and z < depth - 1:
+            wait(z // PART + 1)
+        factor = layer(z, factor)
+
+
+def gather_columns(ref, low, up, depth, rows, cols, beside=False):
     _, lane = row_and_lane(rows, cols)
-    result, other = jnp.zeros((rows, cols), jnp.float32), jnp.zeros((rows, cols), jnp.float32)
+    shifts = (0, -1, 1, -2) if beside else (0, -1)
+    results = [jnp.zeros((rows, cols), jnp.float32)] * len(shifts)
     for k in range(LINKS):
-        slot = linked[k]
-        near, far = jnp.zeros_like(result), jnp.zeros_like(other)
+        parts = [jnp.zeros((rows, cols), jnp.float32)] * len(shifts)
         for z in range(depth):
+            at = pl.ds((z + 1) * rows, rows)
             place = GROUP * k + z
-            moved = spin(ref[slot, pl.ds((z + 1) * rows, rows), :], place - c)
-            near = jnp.where(lane == place, moved, near)
-            if beside:
-                far = jnp.where(lane == (place + beside) % cols, moved, far)
-        result = result + near
-        other = other + far
-    return result, spin(other, -beside)
+            moved = spin(jnp.where(lane < cols // 2, ref[low[k], at, :], ref[up[k], at, :]), place)
+            for i, shift in enumerate(shifts):
+                parts[i] = jnp.where(lane == (place + shift) % cols, moved, parts[i])
+        results = [result + part for result, part in zip(results, parts)]
+    return [spin(result, -shift) for result, shift in zip(results, shifts)]
 
 
 def x_rows(part, k, depth):
@@ -114,16 +111,16 @@
         pltpu.make_async_copy(grains, grains_in, arrived.at[1]),
         pltpu.make_async_copy(planes, planes_in, arrived.at[2]),
     ]
-    part = UNROLL * rows
+    part = PART * rows
 
     def field_part(i):
-        to = pl.ds(pl.multiple_of(i * part + rows, rows), part)
-        source = field.at[:, pl.ds(pl.multiple_of(i * part, rows), part), :]
+        to = pl.ds(i * part + rows, part)
+        source = field.at[:, pl.ds(i * part, part), :]
         return pltpu.make_async_copy(source, now.at[pl.ds(0, slots), to, :], arrived.at[3 + i])
 
     for copy in copies:
         copy.start()
-    for i in range(depth // UNROLL):
+    for i in range(depth // PART):
         field_part(i).start()
     for ref in (now, stepped):
         ref[slots] = jnp.zeros(((depth + 2) * rows, cols), jnp.float32)
@@ -204,24 +201,28 @@
 def y_kernel(slots, depth, rows, cols, now, stepped, squares, lists, y_low, y_up):
     top = (depth + 1) * rows
     _, lane = row_and_lane(rows, cols)
-    for side, out in ((0, y_low), (1, y_up)):
-        c, inward = (0, 1) if side == 0 else (cols - 1, -1)
-        linked = [lists[(2 + side) * SPAN + k] for k in range(LINKS)]
-        rim, _ = gather_columns(now, linked, c, depth, rows, cols)
-        partial, inner = gather_columns(stepped, linked, c, depth, rows, cols, beside=inward)
-        for k in range(LINKS):
-            for z, at in ((0, 0), (depth - 1, top)):
-                place = GROUP * k + z
-                frozen = spin(now[linked[k], pl.ds(at, rows), :], place - c)
-                inner = inner + jnp.where(lane == place, frozen, 0.0)
-        total = jnp.zeros((rows, cols), jnp.float32)
-        for z in range(depth):
-            place = LINKS * GROUP + z
-            total = jnp.where(lane == place, spin(tile(squares, z, rows), place - c), total)
-        inner = jnp.where(in_last_group(lane), total - group_sum(partial * partial), inner)
-        out[pl.ds(0, rows), :] = rim
-        out[pl.ds(rows, rows), :] = partial
-        out[pl.ds(2 * rows, rows), :] = inner
+    low, up = ([lists[face * SPAN + k] for k in range(LINKS)] for face in (2, 3))
+    rims = gather_columns(now, low, up, depth, rows, cols)
+    *partials, inner_low, inner_up = gather_columns(stepped, low, up, depth, rows, cols, beside=True)
+    frozen = [jnp.zeros((rows, cols), jnp.float32)] * 2
+    totals = [jnp.zeros((rows, cols), jnp.float32)] * 2
+    for k in range(LINKS):
+        for z, at in ((0, 0), (depth - 1, top)):
+            place = GROUP * k + z
+            at = pl.ds(at, rows)
+            moved = spin(jnp.where(lane < cols // 2, now[low[k], at, :], now[up[k], at, :]), place)
+            for side in range(2):
+                frozen[side] = jnp.where(lane == (place - side) % cols, moved, frozen[side])
+    for z in range(depth):
+        place = LINKS * GROUP + z
+        moved = spin(tile(squares, z, rows), place)
+        for side in range(2):
+            totals[side] = jnp.where(lane == place - side, moved, totals[side])
+    for side, out, inner in ((0, y_low, inner_low), (1, y_up, inner_up)):
+        rest = spin(totals[side], side) - group_sum(partials[side] * partials[side])
+        out[pl.ds(0, rows), :] = rims[side]
+        out[pl.ds(rows, rows), :] = partials[side]
+        out[pl.ds(2 * rows, rows), :] = jnp.where(in_last_group(lane), rest, inner + spin(frozen[side], side))
 
 
 def in_last_group(lane):
@@ -442,7 +443,7 @@
             pltpu.SMEM(grain_ids.shape, jnp.int32),
             pltpu.SMEM(channel_maps.shape, jnp.int32),
             pltpu.SMEM((2 * (slots + 1),), jnp.int32),
-            pltpu.SemaphoreType.DMA((3 + depth // UNROLL,)),
+            pltpu.SemaphoreType.DMA((3 + depth // PART,)),
         ],
         compiler_params=params,
         name="first_step",

time: 21.5 us -> 21 us (0.977)
  Pallas kernels: 9.36 us -> 8.79 us
    pallas_call x1, Pallas kernels: 1.26 us -> 0.98 us  [on_device(): pl.pallas_call(functools.partial(y_kernel, *sizes), out_shape=[y_pack, y_...]
  transfers between devices with their start and end apart: 6 -> 6, of which waited for: 3 -> 3; matrix products, arithmetic and copies ran while one was open for 0% -> 0% of each run, Pallas kernels for 22% -> 20%
where the time goes in v7:
time: 21 us; the launch traced here: 20.8 us
  Pallas kernels  8.79 us (42%)
  starting transfers between devices  7.35 us (35%)
  waiting for transfers between devices  4.6 us (22%)
    ppermute x6, starting transfers between devices, shifted(): lax.ppermute(block, axis, [((i - distance) % size, i) for i in range(size)])  7.35 us
    ppermute x6, waiting for transfers between devices, shifted(): lax.ppermute(block, axis, [((i - distance) % size, i) for i in range(size)])  4.6 us
    pallas_call x1, Pallas kernels, on_device(): pl.pallas_call(functools.partial(first_kernel, *sizes), out_shape=[padded...  2.78 us
    pallas_call x1, Pallas kernels, on_device(): pl.pallas_call(functools.partial(last_kernel, *sizes), out_shape=[padded,...  1.81 us
    pallas_call x1, Pallas kernels, on_device(): pl.pallas_call(functools.partial(second_kernel, *sizes), out_shape=[padde...  1.64 us
    pallas_call x1, Pallas kernels, on_device(): pl.pallas_call(functools.partial(third_kernel, *sizes), out_shape=[padded...  1.55 us
    pallas_call x1, Pallas kernels, on_device(): pl.pallas_call(functools.partial(y_kernel, *sizes), out_shape=[y_pack, y_...  0.98 us
  transfers between devices with their start and end apart: 6, of which 3 were waited for; matrix products, arithmetic and copies ran while one was open for 0% of the time, Pallas kernels for 20%

profile of v7, /device:TPU:0, one launch (start us, length us, event | category | flops | bytes accessed | tf_op | source)
XLA Modules:
  0.0 20.8 jit_solution(8025641495599491207)
XLA Ops:
  0.0 2.8 %first_step.1 = (f32[25,112,128]{2,1,0:T(8,128)S(1)}, f32[25,112,128]{2,1,0:T(8,128)S(1)}, f32[96,128]{1,0:T(8,128)S(1)}, f32[240,128]{1,0:T(8,128)S(1)}, f32[240,128]{1,0:T(8,128)S(1)}, /*index=5*/s32[56]{0:T(128)S(1)}) custom-call(f32[24,96,128]{2,1,0:T(8,128)} %bitcast.2, s32[2,8,128]{2,1,0:T(8,128)} %planes.1, s32[1,1,24]{2,1,0:T(1,128)} %grains.1, ...), custom_call_target="tpu_custom_call" | custom-call | tf_op jit(solution)/shard_map/first_step/pallas_call | solution.py:436
  2.8 3.0 %collective-permute-start.2 = (f32[240,128]{1,0:T(8,128)S(1)}, f32[240,128]{1,0:T(8,128)S(1)}, u32[]{:S(2)}, u32[]{:S(2)}) collective-permute-start(f32[240,128]{1,0:T(8,128)S(1)} %get-tuple-element.26.own.x_up_own), channel_id=1, source_target_pairs={{28,0},{0,4},{4,8},{8,12},{12,16},{16,20},{20,24},{24,28},{29,1},{... | collective-permute-start | bytes 368648 | tf_op jit(solution)/shard_map/ppermute | solution.py:416
  5.8 3.1 %collective-permute-start.3 = (f32[240,128]{1,0:T(8,128)S(1)}, f32[240,128]{1,0:T(8,128)S(1)}, u32[]{:S(2)}, u32[]{:S(2)}) collective-permute-start(f32[240,128]{1,0:T(8,128)S(1)} %get-tuple-element.25.own.x_low_own), channel_id=1, source_target_pairs={{4,0},{8,4},{12,8},{16,12},{20,16},{24,20},{28,24},{0,28},{5,1},{9... | collective-permute-start | bytes 368648 | tf_op jit(solution)/shard_map/ppermute | solution.py:416
  8.9 1.0 %y_rims.1 = (f32[24,128]{1,0:T(8,128)S(1)}, f32[24,128]{1,0:T(8,128)S(1)}) custom-call(f32[25,112,128]{2,1,0:T(8,128)S(1)} %get-tuple-element.18.now, f32[25,112,128]{2,1,0:T(8,128)S(1)} %get-tuple-element.17.stepped.stepped_in, f32[96,128]{1,0:T(8,128)S(1)} %get-tuple-element.19.squares, s32[56]{0:T(128)S(1)} %get-tuple-element.20.lists), custom_call_target="tpu_custom_call" | custom-call | flops 5898240 | bytes 2359296 | tf_op jit(solution)/shard_map/y_rims/pallas_call | solution.py:455
  9.9 0.7 %collective-permute-start.1 = (f32[24,128]{1,0:T(8,128)S(1)}, f32[24,128]{1,0:T(8,128)S(1)}, u32[]{:S(2)}, u32[]{:S(2)}) collective-permute-start(f32[24,128]{1,0:T(8,128)S(1)} %get-tuple-element.21.y_low_own), channel_id=1, source_target_pairs={{1,0},{2,1},{3,2},{0,3},{5,4},{6,5},{7,6},{4,7},{9,8},{10,9},{11,1... | collective-permute-start | bytes 36872 | tf_op jit(solution)/shard_map/ppermute | solution.py:416
  10.6 0.0 collective-permute-start
  10.6 1.4 %collective-permute-done.1.y_up = f32[24,128]{1,0:T(8,128)S(1)} collective-permute-done((f32[24,128]{1,0:T(8,128)S(1)}, f32[24,128]{1,0:T(8,128)S(1)}, u32[]{:S(2)}, u32[]{:S(2)}) %collective-permute-start.1) | collective-permute-done | bytes 12320 | tf_op jit(solution)/shard_map/ppermute | solution.py:416
  12.0 1.7 %collective-permute-done.y_low = f32[24,128]{1,0:T(8,128)S(1)} collective-permute-done((f32[24,128]{1,0:T(8,128)S(1)}, f32[24,128]{1,0:T(8,128)S(1)}, u32[]{:S(2)}, u32[]{:S(2)}) %collective-permute-start) | collective-permute-done | bytes 12320 | tf_op jit(solution)/shard_map/ppermute | solution.py:416
  13.7 1.6 %second_step.1 = (f32[25,112,128]{2,1,0:T(8,128)S(1)}, f32[25,112,128]{2,1,0:T(8,128)S(1)}) custom-call(f32[25,112,128]{2,1,0:T(8,128)S(1)} %get-tuple-element.17.stepped.stepped_in, f32[24,128]{1,0:T(8,128)S(1)} %get-tuple-element.21.y_low_own, f32[24,128]{1,0:T(8,128)S(1)} %get-tuple-element.22.y_up_own, ...), custom_call_target="tpu_custom_call", output_to_operand_aliasing={{0}: (0, {})} | custom-call | flops 5898240 | bytes 2359296 | tf_op jit(solution)/shard_map/second_step/pallas_call | solution.py:468
  15.3 0.0 collective-permute-done.2.got.x_low
  15.4 0.0 collective-permute-done.3.got.x_up
  15.4 0.4 %collective-permute-start.5 = (f32[48,128]{1,0:T(8,128)S(1)}, f32[48,128]{1,0:T(8,128)S(1)}, u32[]{:S(2)}, u32[]{:S(2)}) collective-permute-start(f32[48,128]{1,0:T(8,128)S(1)} %corners_up.1.changes), channel_id=1, source_target_pairs={{1,0},{2,1},{3,2},{0,3},{5,4},{6,5},{7,6},{4,7},{9,8},{10,9},{11,1... | collective-permute-start | bytes 73736 | tf_op jit(solution)/shard_map/ppermute | solution.py:416
  15.7 0.2 %collective-permute-start.4 = (f32[48,128]{1,0:T(8,128)S(1)}, f32[48,128]{1,0:T(8,128)S(1)}, u32[]{:S(2)}, u32[]{:S(2)}) collective-permute-start(f32[48,128]{1,0:T(8,128)S(1)} %corners_up.1.changes), channel_id=1, source_target_pairs={{3,0},{0,1},{1,2},{2,3},{7,4},{4,5},{5,6},{6,7},{11,8},{8,9},{9,10... | collective-permute-start | bytes 73736 | tf_op jit(solution)/shard_map/ppermute | solution.py:416
  16.0 1.6 %third_step.1 = (f32[25,112,128]{2,1,0:T(8,128)S(1)}, f32[25,112,128]{2,1,0:T(8,128)S(1)}) custom-call(f32[25,112,128]{2,1,0:T(8,128)S(1)} %get-tuple-element.23.now, f32[25,112,128]{2,1,0:T(8,128)S(1)} %get-tuple-element.24.before.later_in, f32[240,128]{1,0:T(8,128)S(1)} %get-tuple-element.25.own.x_low_own, ...), custom_call_target="tpu_custom_call", output_to_operand_aliasing={{0}: (1, {})} | custom-call | tf_op jit(solution)/shard_map/third_step/pallas_call | solution.py:496
  17.5 0.0 collective-permute-done.5.from_right
  17.5 1.5 %collective-permute-done.4.from_left = f32[48,128]{1,0:T(8,128)S(1)} collective-permute-done((f32[48,128]{1,0:T(8,128)S(1)}, f32[48,128]{1,0:T(8,128)S(1)}, u32[]{:S(2)}, u32[]{:S(2)}) %collective-permute-start.4) | collective-permute-done | bytes 24608 | tf_op jit(solution)/shard_map/ppermute | solution.py:416
  19.0 1.8 %last_rims.1 = (f32[25,112,128]{2,1,0:T(8,128)S(1)}, f32[24,96,128]{2,1,0:T(8,128)}) custom-call(f32[25,112,128]{2,1,0:T(8,128)S(1)} %get-tuple-element.27.last_in, f32[240,128]{1,0:T(8,128)S(1)} %get-tuple-element.25.own.x_low_own, f32[240,128]{1,0:T(8,128)S(1)} %get-tuple-element.26.own.x_up_own, ...), custom_call_target="tpu_custom_call", output_to_operand_aliasing={{0}: (0, {})} | custom-call | tf_op jit(solution)/shard_map/last_rims/pallas_call | solution.py:509
  (2 shorter events, 0.0 us)
Async XLA Ops:
  2.8 12.5 %collective-permute-start.2 = (f32[240,128]{1,0:T(8,128)S(1)}, f32[240,128]{1,0:T(8,128)S(1)}, u32[]{:S(2)}, u32[]{:S(2)}) collective-permute-start(f32[240,128]{1,0:T(8,128)S(1)} %get-tuple-element.26.own.x_up_own), channel_id=1, source_target_pairs={{28,0},{0,4},{4,8},{8,12},{12,16},{16,20},{20,24},{24,28},{29,1},{... | collective-permute-start | bytes 368648 | tf_op jit(solution)/shard_map/ppermute | solution.py:416
  5.8 9.6 %collective-permute-start.3 = (f32[240,128]{1,0:T(8,128)S(1)}, f32[240,128]{1,0:T(8,128)S(1)}, u32[]{:S(2)}, u32[]{:S(2)}) collective-permute-start(f32[240,128]{1,0:T(8,128)S(1)} %get-tuple-element.25.own.x_low_own), channel_id=1, source_target_pairs={{4,0},{8,4},{12,8},{16,12},{20,16},{24,20},{28,24},{0,28},{5,1},{9... | collective-permute-start | bytes 368648 | tf_op jit(solution)/shard_map/ppermute | solution.py:416
  9.9 2.1 %collective-permute-start.1 = (f32[24,128]{1,0:T(8,128)S(1)}, f32[24,128]{1,0:T(8,128)S(1)}, u32[]{:S(2)}, u32[]{:S(2)}) collective-permute-start(f32[24,128]{1,0:T(8,128)S(1)} %get-tuple-element.21.y_low_own), channel_id=1, source_target_pairs={{1,0},{2,1},{3,2},{0,3},{5,4},{6,5},{7,6},{4,7},{9,8},{10,9},{11,1... | collective-permute-start | bytes 36872 | tf_op jit(solution)/shard_map/ppermute | solution.py:416
  10.6 3.1 %collective-permute-start = (f32[24,128]{1,0:T(8,128)S(1)}, f32[24,128]{1,0:T(8,128)S(1)}, u32[]{:S(2)}, u32[]{:S(2)}) collective-permute-start(f32[24,128]{1,0:T(8,128)S(1)} %get-tuple-element.22.y_up_own), channel_id=1, source_target_pairs={{3,0},{0,1},{1,2},{2,3},{7,4},{4,5},{5,6},{6,7},{11,8},{8,9},{9,10... | collective-permute-start | bytes 36872 | tf_op jit(solution)/shard_map/ppermute | solution.py:416
  15.4 2.1 %collective-permute-start.5 = (f32[48,128]{1,0:T(8,128)S(1)}, f32[48,128]{1,0:T(8,128)S(1)}, u32[]{:S(2)}, u32[]{:S(2)}) collective-permute-start(f32[48,128]{1,0:T(8,128)S(1)} %corners_up.1.changes), channel_id=1, source_target_pairs={{1,0},{2,1},{3,2},{0,3},{5,4},{6,5},{7,6},{4,7},{9,8},{10,9},{11,1... | collective-permute-start | bytes 73736 | tf_op jit(solution)/shard_map/ppermute | solution.py:416
  15.7 3.3 %collective-permute-start.4 = (f32[48,128]{1,0:T(8,128)S(1)}, f32[48,128]{1,0:T(8,128)S(1)}, u32[]{:S(2)}, u32[]{:S(2)}) collective-permute-start(f32[48,128]{1,0:T(8,128)S(1)} %corners_up.1.changes), channel_id=1, source_target_pairs={{3,0},{0,1},{1,2},{2,3},{7,4},{4,5},{5,6},{6,7},{11,8},{8,9},{9,10... | collective-permute-start | bytes 73736 | tf_op jit(solution)/shard_map/ppermute | solution.py:416

commit v8 on v7

--- a/solution.py
+++ b/solution.py
@@ -233,7 +233,7 @@
     return ref[pl.ds(i * rows, rows), :]
 
 
-def y_faces(ref, tiles, lists, depth, rows, cols, replace=False, done=None):
+def y_faces(ref, tiles, lists, depth, rows, cols, replace=False):
     _, lane = row_and_lane(rows, cols)
     for k in range(LINKS):
         for side in range(2):
@@ -244,23 +244,6 @@
             for z in range(depth):
                 moved = spin(tiles[side], c - GROUP * k - z)
                 ref[slot, ats[z], :] = jnp.where(lane == c, moved if replace else old[z] + moved, old[z])
-            if done is not None:
-                done(slot)
-
-
-def second_kernel(
-    slots, depth, rows, cols, stepped_in, y_low_own, y_up_own, y_low, y_up, lists, now, later
-):
-    for s in range(slots):
-        for at in (0, (depth + 1) * rows):
-            later[s, pl.ds(at, rows), :] = now[s, pl.ds(at, rows), :]
-    later[slots] = jnp.zeros(((depth + 2) * rows, cols), jnp.float32)
-    pairs = ((y_low_own, y_low), (y_up_own, y_up))
-    own_one = [tile(own, 1, rows) + RATE * tile(got, 0, rows) for own, got in pairs]
-    one = [RATE * (tile(got, 1, rows) + RATE * tile(own, 0, rows)) for own, got in pairs]
-    y_faces(now, own_one, lists, depth, rows, cols, replace=True)
-    step(now, later, slots, depth, rows, cols)
-    y_faces(later, one, lists, depth, rows, cols)
 
 
 def x_rims(own, got, k, depth):
@@ -268,7 +251,8 @@
     return own[one, :] + RATE * got[zero, :], got[one, :] + RATE * own[zero, :]
 
 
-def change_kernel(depth, cols, own, got, before, out):
+def change_kernel(depth, cols, own, got, *refs):
+    out = refs[-1]
     change = jnp.zeros((depth, cols), jnp.float32)
     for k in range(LINKS):
         own_one, _ = x_rims(own, got, k, depth)
@@ -276,11 +260,12 @@
         change = change + (own_one * own_one - partial * partial)
     out[pl.ds(0, depth), :] = change
     out[pl.ds(depth, depth), :] = got[pl.ds(3 * LINKS * depth, depth), :]
+    out[pl.ds(2 * depth, depth), :] = own[pl.ds(3 * LINKS * depth, depth), :]
 
 
 def both_changes_kernel(depth, cols, own, got, before, out):
-    out[pl.ds(0, 2 * depth), :] = before[...]
-    change_kernel(depth, cols, own, got, None, out.at[pl.ds(2 * depth, 2 * depth), :])
+    out[pl.ds(0, 3 * depth), :] = before[...]
+    change_kernel(depth, cols, own, got, out.at[pl.ds(3 * depth, 3 * depth), :])
 
 
 def x_rim_step(padded, face, k, one, factor, outer, depth, cols):
@@ -302,113 +287,112 @@
     return RATE * (one * (factor + one * one) + (outer + (x_sum + z_sum)))
 
 
-def third_kernel(
+def later_kernel(
     slots, depth, rows, cols,
-    now, later_in, x_low_own, x_up_own, x_low, x_up, changes, lists,
-    later, last,
-    x_own_one,
+    stepped_in, x_low_own, x_up_own, x_low, x_up, y_low_own, y_up_own, y_low, y_up, lists, after,
+    now, last,
+    later, x_one,
 ):
-    last[slots] = jnp.zeros(((depth + 2) * rows, cols), jnp.float32)
-    x_own_one[...] = jnp.zeros(x_own_one.shape, jnp.float32)
-    for face, own, got in ((0, x_low_own, x_low), (1, x_up_own, x_up)):
-        r, inner_r = (0, 1) if face == 0 else (rows - 1, rows - 2)
-        rim_rows = pl.ds(rows + r, depth, stride=rows)
-        inner_rows = pl.ds(rows + inner_r, depth, stride=rows)
+    _, lane = row_and_lane(rows, cols)
+    for s in range(slots):
+        for at in (0, (depth + 1) * rows):
+            later[s, pl.ds(at, rows), :] = now[s, pl.ds(at, rows), :]
+    for ref in (later, last):
+        ref[slots] = jnp.zeros(((depth + 2) * rows, cols), jnp.float32)
+    x_one[...] = jnp.zeros(x_one.shape, jnp.float32)
+    linked = [[lists[face * SPAN + k] for k in range(LINKS)] for face in range(2)]
+    rim_rows = [pl.ds(rows + r, depth, stride=rows) for r in (0, rows - 1)]
+    faces = ((0, x_low_own, x_low), (1, x_up_own, x_up))
+
+    x_ones, x_twos = [], []
+    for face, own, got in faces:
         rims = [x_rims(own, got, k, depth) for k in range(LINKS)]
-        for k in range(LINKS):
-            x_own_one[face, pl.ds(SPAN + k, depth, stride=SPAN), :] = rims[k][0]
-
-        change = changes[pl.ds(2 * face * depth, depth), :]
-        scaled = 0.15 * change
-        parts = [change, None, None, None]
-        for first in range(0, slots, 4):
-            rim = [now[first + i, rim_rows, :] for i in range(4)]
-            old = [later[first + i, rim_rows, :] for i in range(4)]
-            for i in range(4):
-                parts[i] = rim[i] * rim[i] if parts[i] is None else parts[i] + rim[i] * rim[i]
-                later[first + i, rim_rows, :] = old[i] - scaled * rim[i]
-        factor = 4.5 - 1.5 * ((parts[0] + parts[1]) + (parts[2] + parts[3]))
-
-        linked = [lists[face * SPAN + k] for k in range(LINKS)]
-        beside = [later[slot, inner_rows, :] for slot in linked]
+        total = got[pl.ds((3 * LINKS + 1) * depth, depth), :]
+        for k, (own_one, one) in enumerate(rims):
+            now[linked[face][k], rim_rows[face], :] = own_one
+            total = total + one * one
+            x_one[face, pl.ds(SPAN + k, depth, stride=SPAN), :] = one
+        factor = 4.5 - 1.5 * total
+        x_ones.append([RATE * one for _, one in rims])
         two = []
-        for k in range(LINKS):
-            outer = own[x_rows(2, k, depth), :] + rims[k][1]
-            two.append(x_rim_step(x_own_one, face, k, rims[k][0], factor, outer, depth, cols))
-        for k in range(LINKS):
-            later[linked[k], rim_rows, :] = two[k]
-            later[linked[k], inner_rows, :] = beside[k] + RATE * RATE * got[x_rows(0, k, depth), :]
-
-    step(later, last, slots, depth, rows, cols)
-
-
-def last_kernel(
-    slots, depth, rows, cols,
-    last_in, x_low_own, x_up_own, x_low, x_up, y_low_own, y_up_own, y_low, y_up, from_left, from_right,
-    lists,
-    last, result,
-    x_one, sent,
-):
-    whole = last.at[pl.ds(0, slots), pl.ds(rows, depth * rows), :]
-
-    def send(slot):
-        pltpu.make_async_copy(last.at[slot, pl.ds(rows, depth * rows), :], result.at[slot], sent).start()
-
-    def send_linked(slot):
-        pl.when(slot < slots)(lambda: send(slot))
-
-    for s in range(slots):
-        pl.when(lists[4 * SPAN + s] == 0)(functools.partial(send, s))
-
-    row, lane = row_and_lane(rows, cols)
-    _, flat_lane = row_and_lane(depth, cols)
-    tall_row, tall_lane = row_and_lane(GROUP, cols)
-    block = LINKS * depth
-    passed_on = (from_left, from_right)
-    x_one[...] = jnp.zeros(x_one.shape, jnp.float32)
-    for face, own, got in ((0, x_low_own, x_low), (1, x_up_own, x_up)):
-        rims = [x_rims(own, got, k, depth) for k in range(LINKS)]
-        total = got[pl.ds(3 * block + depth, depth), :]
-        for k in range(LINKS):
-            total = total + rims[k][1] * rims[k][1]
-            x_one[face, pl.ds(SPAN + k, depth, stride=SPAN), :] = rims[k][1]
-        corners = got[pl.ds(3 * block, depth), :]
-        for side in range(2):
-            place = side * LINKS
-            came_from = (3 - side) * LINKS
-            term = RATE * spin(passed_on[side][pl.ds((2 * face + 1) * depth, depth), :], place - came_from)
-            term = term * (2.0 * corners + term)
-            term = jnp.where((flat_lane >= place) & (flat_lane < place + LINKS), term, 0.0)
-            column = jnp.sum(term, axis=1, keepdims=True)
-            total = total + jnp.where(flat_lane == side * (cols - 1), column, 0.0)
-        factor = 4.5 - 1.5 * total
-        rim_rows = pl.ds(rows + (0 if face == 0 else rows - 1), depth, stride=rows)
-        linked = [lists[face * SPAN + k] for k in range(LINKS)]
-        old = [last[slot, rim_rows, :] for slot in linked]
-        for k in range(LINKS):
-            outer = got[x_rows(2, k, depth), :] + rims[k][0]
-            two = x_rim_step(x_one, face, k, rims[k][1], factor, outer, depth, cols)
-            last[linked[k], rim_rows, :] = old[k] + RATE * two
-        for slot in linked:
-            send_linked(slot)
-
-    twos = []
-    for side, own, got in ((0, y_low_own, y_low), (1, y_up_own, y_up)):
-        c = side * (cols - 1)
+        for k, (own_one, one) in enumerate(rims):
+            outer = got[x_rows(2, k, depth), :] + own_one
+            two.append(RATE * x_rim_step(x_one, face, k, one, factor, outer, depth, cols))
+        x_twos.append(two)
+    y_own_ones, y_ones, y_twos = [], [], []
+    for own, got in ((y_low_own, y_low), (y_up_own, y_up)):
         own_one = tile(own, 1, rows) + RATE * tile(got, 0, rows)
         one = tile(got, 1, rows) + RATE * tile(own, 0, rows)
         inner = tile(got, 2, rows)
-        squares = one * one + jnp.where(in_last_group(lane), inner, 0.0)
+        factor = 4.5 - 1.5 * group_sum(one * one + jnp.where(in_last_group(lane), inner, 0.0))
+        y_own_ones.append(own_one)
+        y_ones.append(RATE * one)
+        y_twos.append(RATE * y_rim_step(one, factor, inner + own_one))
+
+    def add_rims(ref, x_terms, y_terms):
         for face in range(2):
-            change = passed_on[side][pl.ds(2 * face * depth, depth), :]
-            column = jnp.sum(jnp.where(flat_lane == cols - 1 - c, change, 0.0), axis=1, keepdims=True)
-            line = jnp.sum(jnp.where(tall_row == tall_lane, 1.0, 0.0)[:depth] * column, axis=0, keepdims=True)
-            at_row = row == (0 if face == 0 else rows - 1)
-            squares = squares + jnp.where(at_row, jnp.broadcast_to(line, (rows, cols)), 0.0)
-        factor = 4.5 - 1.5 * group_sum(squares)
-        twos.append(RATE * y_rim_step(one, factor, inner + own_one))
-    y_faces(last, twos, lists, depth, rows, cols, done=send_linked)
-    pltpu.make_async_copy(whole, result, sent).wait()
+            old = [ref[slot, rim_rows[face], :] for slot in linked[face]]
+            for k in range(LINKS):
+                ref[linked[face][k], rim_rows[face], :] = old[k] + x_terms[face][k]
+        y_faces(ref, y_terms, lists, depth, rows, cols)
+
+    y_faces(now, y_own_ones, lists, depth, rows, cols, replace=True)
+    step(now, later, slots, depth, rows, cols)
+    add_rims(later, x_ones, y_ones)
+    step(later, last, slots, depth, rows, cols)
+    add_rims(last, x_twos, y_twos)
+
+
+def last_kernel(
+    slots, depth, rows, cols,
+    last_in, x_low_own, x_up_own, x_low, x_up, from_left, from_right, lists,
+    last, result,
+    sent,
+):
+    def send(slot):
+        pltpu.make_async_copy(last.at[slot, pl.ds(rows, depth * rows), :], result.at[slot], sent).start()
+
+    for s in range(slots):
+        pl.when(lists[4 * SPAN + s] == 0)(functools.partial(send, s))
+
+    _, lane = row_and_lane(depth, cols)
+    scale = -1.5 * RATE * RATE
+    passed_on = (from_left, from_right)
+    part = lambda ref, i: ref[pl.ds(i * depth, depth), :]
+    corner_cells = lambda ref: ref[pl.ds(3 * LINKS * depth, depth), :]
+    linked = [[lists[face * SPAN + k] for k in range(LINKS)] for face in range(4)]
+    rims = [pl.ds(rows + r, depth, stride=rows) for r in (0, rows - 1)]
+
+    for face, own, got in ((0, x_low_own, x_low), (1, x_up_own, x_up)):
+        total = jnp.zeros((depth, cols), jnp.float32)
+        for side in range(2):
+            place = side * LINKS
+            term = RATE * spin(part(passed_on[side], 3 * face + 1), place - (3 - side) * LINKS)
+            term = term * (2.0 * corner_cells(got) + term)
+            term = jnp.where((lane >= place) & (lane < place + LINKS), term, 0.0)
+            column = jnp.sum(term, axis=1, keepdims=True)
+            total = total + jnp.where(lane == side * (cols - 1), column, 0.0)
+        total = scale * total
+        old = [last[slot, rims[face], :] for slot in linked[face]]
+        for k in range(LINKS):
+            _, one = x_rims(own, got, k, depth)
+            last[linked[face][k], rims[face], :] = old[k] + total * one
+
+    for side in range(2):
+        c = side * (cols - 1)
+        for face, own in ((0, x_low_own), (1, x_up_own)):
+            place = (1 - side) * LINKS
+            one = part(passed_on[side], 3 * face + 2) + RATE * spin(corner_cells(own), place - (2 + side) * LINKS)
+            change = jnp.where(lane == cols - 1 - c, part(passed_on[side], 3 * face), 0.0)
+            one = scale * one * jnp.sum(change, axis=1, keepdims=True)
+            old = [last[slot, rims[face], :] for slot in linked[2 + side]]
+            for k in range(LINKS):
+                moved = jnp.where(lane == c, spin(one, c - place - k), 0.0)
+                last[linked[2 + side][k], rims[face], :] = old[k] + moved
+    for face in range(4):
+        for slot in linked[face]:
+            pl.when(slot < slots)(functools.partial(send, slot))
+    pltpu.make_async_copy(last.at[pl.ds(0, slots), pl.ds(rows, depth * rows), :], result, sent).wait()
 
 
 def shifted(block, axis, distance):
@@ -465,60 +449,47 @@
     from_right = shifted(y_low, "gy", -1)
     from_left = shifted(y_up, "gy", 1)
 
-    fixed, later = pl.pallas_call(
-        functools.partial(second_kernel, *sizes),
-        out_shape=[padded, padded],
-        in_specs=[vmem] * 5 + [smem],
-        out_specs=[vmem] * 2,
-        input_output_aliases={0: 0},
-        compiler_params=params,
-        cost_estimate=work,
-        name="second_step",
-    )(stepped, y_low, y_up, from_left, from_right, lists)
-
-    changes = later
+    changes = (from_left, from_right)
     for body, own, got, name in (
         (change_kernel, x_low, from_low, "corners_low"),
         (both_changes_kernel, x_up, from_up, "corners_up"),
     ):
-        changes = pl.pallas_call(
-            functools.partial(body, depth, cols),
-            out_shape=shape(((2 if body is change_kernel else 4) * depth, cols), f32),
-            in_specs=[vmem] * 3,
-            out_specs=vmem,
-            compiler_params=params,
-            name=name,
-        )(own, got, changes)
+        changes = [
+            pl.pallas_call(
+                functools.partial(body, depth, cols),
+                out_shape=shape(((3 if body is change_kernel else 6) * depth, cols), f32),
+                in_specs=[vmem] * (2 + len(changes)),
+                out_specs=vmem,
+                compiler_params=params,
+                name=name,
+            )(own, got, *changes)
+        ]
+    changes = changes[0]
 
     changes_from_right = shifted(changes, "gy", -1)
     changes_from_left = shifted(changes, "gy", 1)
 
     _, last = pl.pallas_call(
-        functools.partial(third_kernel, *sizes),
+        functools.partial(later_kernel, *sizes),
         out_shape=[padded, padded],
-        in_specs=[vmem] * 7 + [smem],
+        in_specs=[vmem] * 9 + [smem, vmem],
         out_specs=[vmem] * 2,
-        scratch_shapes=[rims],
-        input_output_aliases={1: 0},
+        scratch_shapes=[padded, rims],
+        input_output_aliases={0: 0},
         compiler_params=params,
-        name="third_step",
-    )(
-        fixed, later, x_low, x_up, from_low, from_up, changes, lists,
-    )
+        name="later_steps",
+    )(stepped, x_low, x_up, from_low, from_up, y_low, y_up, from_left, from_right, lists, changes)
 
     _, result = pl.pallas_call(
         functools.partial(last_kernel, *sizes),
         out_shape=[padded, shape(field.shape, f32)],
-        in_specs=[vmem] * 11 + [smem],
+        in_specs=[vmem] * 7 + [smem],
         out_specs=[vmem, hbm],
-        scratch_shapes=[rims, pltpu.SemaphoreType.DMA],
+        scratch_shapes=[pltpu.SemaphoreType.DMA],
         input_output_aliases={0: 0},
         compiler_params=params,
-        name="last_rims",
-    )(
-        last, x_low, x_up, from_low, from_up,
-        y_low, y_up, from_left, from_right, changes_from_left, changes_from_right, lists,
-    )
+        name="last_corners",
+    )(last, x_low, x_up, from_low, from_up, changes_from_left, changes_from_right, lists)
     return result.reshape(order_params.shape)
 
 

time: 21 us -> 19.8 us (0.943)
  waiting for transfers between devices: 4.6 us -> 1.65 us
  starting transfers between devices: 7.35 us -> 9.64 us
  Pallas kernels: 8.79 us -> 8.15 us
    ppermute x6, waiting for transfers between devices: 4.6 us -> 1.65 us  [shifted(): lax.ppermute(block, axis, [((i - distance) % size, i) for i in range(size)])]
    ppermute x6, starting transfers between devices: 7.35 us -> 9.64 us  [shifted(): lax.ppermute(block, axis, [((i - distance) % size, i) for i in range(size)])]
    pallas_call x4 -> x3, Pallas kernels: 3.22 us -> 2.71 us  [the longest x1 2.67 us: on_device(): pl.pallas_call(functools.partial(later_kernel, *sizes), out_shape=[padded...]
  transfers between devices with their start and end apart: 6 -> 6, of which waited for: 3 -> 2; matrix products, arithmetic and copies ran while one was open for 0% -> 0% of each run, Pallas kernels for 20% -> 19%
where the time goes in v8:
time: 19.8 us; the launch traced here: 19.5 us
  starting transfers between devices  9.64 us (49%)
  Pallas kernels  8.15 us (41%)
  waiting for transfers between devices  1.65 us (8%)
    ppermute x6, starting transfers between devices, shifted(): lax.ppermute(block, axis, [((i - distance) % size, i) for i in range(size)])  9.64 us
    pallas_call x1, Pallas kernels, on_device(): pl.pallas_call(functools.partial(first_kernel, *sizes), out_shape=[padded...  2.74 us
    pallas_call x1, Pallas kernels, on_device(): pl.pallas_call(functools.partial(later_kernel, *sizes), out_shape=[padded...  2.67 us
    pallas_call x1, Pallas kernels, on_device(): pl.pallas_call(functools.partial(last_kernel, *sizes), out_shape=[padded,...  1.72 us
    ppermute x6, waiting for transfers between devices, shifted(): lax.ppermute(block, axis, [((i - distance) % size, i) for i in range(size)])  1.65 us
    pallas_call x1, Pallas kernels, on_device(): pl.pallas_call(functools.partial(y_kernel, *sizes), out_shape=[y_pack, y_...  0.98 us
  transfers between devices with their start and end apart: 6, of which 2 were waited for; matrix products, arithmetic and copies ran while one was open for 0% of the time, Pallas kernels for 19%

profile of v8, /device:TPU:0, one launch (start us, length us, event | category | flops | bytes accessed | tf_op | source)
XLA Modules:
  0.0 19.5 jit_solution(9848972407729337960)
XLA Ops:
  0.0 2.7 %first_step.1 = (f32[25,112,128]{2,1,0:T(8,128)S(1)}, f32[25,112,128]{2,1,0:T(8,128)S(1)}, f32[96,128]{1,0:T(8,128)S(1)}, f32[240,128]{1,0:T(8,128)S(1)}, f32[240,128]{1,0:T(8,128)S(1)}, /*index=5*/s32[56]{0:T(128)S(1)}) custom-call(f32[24,96,128]{2,1,0:T(8,128)} %bitcast.2, s32[2,8,128]{2,1,0:T(8,128)} %planes.1, s32[1,1,24]{2,1,0:T(1,128)} %grains.1, ...), custom_call_target="tpu_custom_call" | custom-call | tf_op jit(solution)/shard_map/first_step/pallas_call | solution.py:420
  2.7 3.0 %collective-permute-start = (f32[240,128]{1,0:T(8,128)S(1)}, f32[240,128]{1,0:T(8,128)S(1)}, u32[]{:S(2)}, u32[]{:S(2)}) collective-permute-start(f32[240,128]{1,0:T(8,128)S(1)} %get-tuple-element.17.own.x_up_own), channel_id=1, source_target_pairs={{28,0},{0,4},{4,8},{8,12},{12,16},{16,20},{20,24},{24,28},{29,1},{... | collective-permute-start | bytes 368648 | tf_op jit(solution)/shard_map/ppermute | solution.py:400
  5.7 3.1 %collective-permute-start.1 = (f32[240,128]{1,0:T(8,128)S(1)}, f32[240,128]{1,0:T(8,128)S(1)}, u32[]{:S(2)}, u32[]{:S(2)}) collective-permute-start(f32[240,128]{1,0:T(8,128)S(1)} %get-tuple-element.16.own.x_low_own), channel_id=1, source_target_pairs={{4,0},{8,4},{12,8},{16,12},{20,16},{24,20},{28,24},{0,28},{5,1},{9... | collective-permute-start | bytes 368648 | tf_op jit(solution)/shard_map/ppermute | solution.py:400
  8.8 1.0 %y_rims.1 = (f32[24,128]{1,0:T(8,128)S(1)}, f32[24,128]{1,0:T(8,128)S(1)}) custom-call(f32[25,112,128]{2,1,0:T(8,128)S(1)} %get-tuple-element.18.now, f32[25,112,128]{2,1,0:T(8,128)S(1)} %get-tuple-element.15.stepped.stepped_in, f32[96,128]{1,0:T(8,128)S(1)} %get-tuple-element.19.squares, s32[56]{0:T(128)S(1)} %get-tuple-element.20.lists), custom_call_target="tpu_custom_call" | custom-call | flops 5898240 | bytes 2359296 | tf_op jit(solution)/shard_map/y_rims/pallas_call | solution.py:439
  9.8 0.0 collective-permute-start.2
  9.8 1.7 %collective-permute-start.3 = (f32[24,128]{1,0:T(8,128)S(1)}, f32[24,128]{1,0:T(8,128)S(1)}, u32[]{:S(2)}, u32[]{:S(2)}) collective-permute-start(f32[24,128]{1,0:T(8,128)S(1)} %get-tuple-element.21.y_low_own), channel_id=1, source_target_pairs={{1,0},{2,1},{3,2},{0,3},{5,4},{6,5},{7,6},{4,7},{9,8},{10,9},{11,1... | collective-permute-start | bytes 36872 | tf_op jit(solution)/shard_map/ppermute | solution.py:400
  11.6 1.4 %collective-permute-done.2.refs_0_.y_low = f32[24,128]{1,0:T(8,128)S(1)} collective-permute-done((f32[24,128]{1,0:T(8,128)S(1)}, f32[24,128]{1,0:T(8,128)S(1)}, u32[]{:S(2)}, u32[]{:S(2)}) %collective-permute-start.2) | collective-permute-done | bytes 12320 | tf_op jit(solution)/shard_map/ppermute | solution.py:400
  13.0 0.0 collective-permute-done.3.refs_1_.y_up
  13.0 0.0 collective-permute-done.got.x_low
  13.0 0.2 %collective-permute-done.1.got.x_up = f32[240,128]{1,0:T(8,128)S(1)} collective-permute-done((f32[240,128]{1,0:T(8,128)S(1)}, f32[240,128]{1,0:T(8,128)S(1)}, u32[]{:S(2)}, u32[]{:S(2)}) %collective-permute-start.1) | collective-permute-done | bytes 122912 | tf_op jit(solution)/shard_map/ppermute | solution.py:400
  13.3 1.6 %collective-permute-start.4 = (f32[72,128]{1,0:T(8,128)S(1)}, f32[72,128]{1,0:T(8,128)S(1)}, u32[]{:S(2)}, u32[]{:S(2)}) collective-permute-start(f32[72,128]{1,0:T(8,128)S(1)} %corners_up.1.after), channel_id=1, source_target_pairs={{3,0},{0,1},{1,2},{2,3},{7,4},{4,5},{5,6},{6,7},{11,8},{8,9},{9,10... | collective-permute-start | bytes 110600 | tf_op jit(solution)/shard_map/ppermute | solution.py:400
  14.8 0.2 %collective-permute-start.5 = (f32[72,128]{1,0:T(8,128)S(1)}, f32[72,128]{1,0:T(8,128)S(1)}, u32[]{:S(2)}, u32[]{:S(2)}) collective-permute-start(f32[72,128]{1,0:T(8,128)S(1)} %corners_up.1.after), channel_id=1, source_target_pairs={{1,0},{2,1},{3,2},{0,3},{5,4},{6,5},{7,6},{4,7},{9,8},{10,9},{11,1... | collective-permute-start | bytes 110600 | tf_op jit(solution)/shard_map/ppermute | solution.py:400
  15.1 2.7 %later_steps.1 = (f32[25,112,128]{2,1,0:T(8,128)S(1)}, f32[25,112,128]{2,1,0:T(8,128)S(1)}) custom-call(f32[25,112,128]{2,1,0:T(8,128)S(1)} %get-tuple-element.15.stepped.stepped_in, f32[240,128]{1,0:T(8,128)S(1)} %get-tuple-element.16.own.x_low_own, f32[240,128]{1,0:T(8,128)S(1)} %get-tuple-element.17.own.x_up_own, ...), custom_call_target="tpu_custom_call", output_to_operand_aliasing={{0}: (0, {})} | custom-call | tf_op jit(solution)/shard_map/later_steps/pallas_call | solution.py:472
  17.7 0.0 collective-permute-done.4.from_left
  17.8 0.0 collective-permute-done.5.from_right
  17.8 1.7 %last_corners.1 = (f32[25,112,128]{2,1,0:T(8,128)S(1)}, f32[24,96,128]{2,1,0:T(8,128)}) custom-call(f32[25,112,128]{2,1,0:T(8,128)S(1)} %get-tuple-element.23.last_in, f32[240,128]{1,0:T(8,128)S(1)} %get-tuple-element.16.own.x_low_own, f32[240,128]{1,0:T(8,128)S(1)} %get-tuple-element.17.own.x_up_own, ...), custom_call_target="tpu_custom_call", output_to_operand_aliasing={{0}: (0, {})} | custom-call | tf_op jit(solution)/shard_map/last_corners/pallas_call | solution.py:483
  (2 shorter events, 0.0 us)
Async XLA Ops:
  2.7 10.2 %collective-permute-start = (f32[240,128]{1,0:T(8,128)S(1)}, f32[240,128]{1,0:T(8,128)S(1)}, u32[]{:S(2)}, u32[]{:S(2)}) collective-permute-start(f32[240,128]{1,0:T(8,128)S(1)} %get-tuple-element.17.own.x_up_own), channel_id=1, source_target_pairs={{28,0},{0,4},{4,8},{8,12},{12,16},{16,20},{20,24},{24,28},{29,1},{... | collective-permute-start | bytes 368648 | tf_op jit(solution)/shard_map/ppermute | solution.py:400
  5.7 7.5 %collective-permute-start.1 = (f32[240,128]{1,0:T(8,128)S(1)}, f32[240,128]{1,0:T(8,128)S(1)}, u32[]{:S(2)}, u32[]{:S(2)}) collective-permute-start(f32[240,128]{1,0:T(8,128)S(1)} %get-tuple-element.16.own.x_low_own), channel_id=1, source_target_pairs={{4,0},{8,4},{12,8},{16,12},{20,16},{24,20},{28,24},{0,28},{5,1},{9... | collective-permute-start | bytes 368648 | tf_op jit(solution)/shard_map/ppermute | solution.py:400
  9.8 3.1 %collective-permute-start.2 = (f32[24,128]{1,0:T(8,128)S(1)}, f32[24,128]{1,0:T(8,128)S(1)}, u32[]{:S(2)}, u32[]{:S(2)}) collective-permute-start(f32[24,128]{1,0:T(8,128)S(1)} %get-tuple-element.22.y_up_own), channel_id=1, source_target_pairs={{3,0},{0,1},{1,2},{2,3},{7,4},{4,5},{5,6},{6,7},{11,8},{8,9},{9,10... | collective-permute-start | bytes 36872 | tf_op jit(solution)/shard_map/ppermute | solution.py:400
  9.8 3.1 %collective-permute-start.3 = (f32[24,128]{1,0:T(8,128)S(1)}, f32[24,128]{1,0:T(8,128)S(1)}, u32[]{:S(2)}, u32[]{:S(2)}) collective-permute-start(f32[24,128]{1,0:T(8,128)S(1)} %get-tuple-element.21.y_low_own), channel_id=1, source_target_pairs={{1,0},{2,1},{3,2},{0,3},{5,4},{6,5},{7,6},{4,7},{9,8},{10,9},{11,1... | collective-permute-start | bytes 36872 | tf_op jit(solution)/shard_map/ppermute | solution.py:400
  13.3 4.5 %collective-permute-start.4 = (f32[72,128]{1,0:T(8,128)S(1)}, f32[72,128]{1,0:T(8,128)S(1)}, u32[]{:S(2)}, u32[]{:S(2)}) collective-permute-start(f32[72,128]{1,0:T(8,128)S(1)} %corners_up.1.after), channel_id=1, source_target_pairs={{3,0},{0,1},{1,2},{2,3},{7,4},{4,5},{5,6},{6,7},{11,8},{8,9},{9,10... | collective-permute-start | bytes 110600 | tf_op jit(solution)/shard_map/ppermute | solution.py:400
  14.8 2.9 %collective-permute-start.5 = (f32[72,128]{1,0:T(8,128)S(1)}, f32[72,128]{1,0:T(8,128)S(1)}, u32[]{:S(2)}, u32[]{:S(2)}) collective-permute-start(f32[72,128]{1,0:T(8,128)S(1)} %corners_up.1.after), channel_id=1, source_target_pairs={{1,0},{2,1},{3,2},{0,3},{5,4},{6,5},{7,6},{4,7},{9,8},{10,9},{11,1... | collective-permute-start | bytes 110600 | tf_op jit(solution)/shard_map/ppermute | solution.py:400

commit v9 on v8

--- a/solution.py
+++ b/solution.py
@@ -349,12 +349,6 @@
     last, result,
     sent,
 ):
-    def send(slot):
-        pltpu.make_async_copy(last.at[slot, pl.ds(rows, depth * rows), :], result.at[slot], sent).start()
-
-    for s in range(slots):
-        pl.when(lists[4 * SPAN + s] == 0)(functools.partial(send, s))
-
     _, lane = row_and_lane(depth, cols)
     scale = -1.5 * RATE * RATE
     passed_on = (from_left, from_right)
@@ -389,10 +383,9 @@
             for k in range(LINKS):
                 moved = jnp.where(lane == c, spin(one, c - place - k), 0.0)
                 last[linked[2 + side][k], rims[face], :] = old[k] + moved
-    for face in range(4):
-        for slot in linked[face]:
-            pl.when(slot < slots)(functools.partial(send, slot))
-    pltpu.make_async_copy(last.at[pl.ds(0, slots), pl.ds(rows, depth * rows), :], result, sent).wait()
+    copy = pltpu.make_async_copy(last.at[pl.ds(0, slots), pl.ds(rows, depth * rows), :], result, sent)
+    copy.start()
+    copy.wait()
 
 
 def shifted(block, axis, distance):

time: 19.8 us -> 20 us (1.010)
  Pallas kernels: 8.15 us -> 8.42 us
    pallas_call x1, Pallas kernels: 1.72 us -> 2 us  [on_device(): pl.pallas_call(functools.partial(last_kernel, *sizes), out_shape=[padded,...]
where the time goes in v9:
time: 20 us; the launch traced here: 19.8 us
  starting transfers between devices  9.64 us (48%)
  Pallas kernels  8.42 us (42%)
  waiting for transfers between devices  1.65 us (8%)
    ppermute x6, starting transfers between devices, shifted(): lax.ppermute(block, axis, [((i - distance) % size, i) for i in range(size)])  9.64 us
    pallas_call x1, Pallas kernels, on_device(): pl.pallas_call(functools.partial(first_kernel, *sizes), out_shape=[padded...  2.74 us
    pallas_call x1, Pallas kernels, on_device(): pl.pallas_call(functools.partial(later_kernel, *sizes), out_shape=[padded...  2.67 us
    pallas_call x1, Pallas kernels, on_device(): pl.pallas_call(functools.partial(last_kernel, *sizes), out_shape=[padded,...  2 us
    ppermute x6, waiting for transfers between devices, shifted(): lax.ppermute(block, axis, [((i - distance) % size, i) for i in range(size)])  1.65 us
    pallas_call x1, Pallas kernels, on_device(): pl.pallas_call(functools.partial(y_kernel, *sizes), out_shape=[y_pack, y_...  0.98 us
  transfers between devices with their start and end apart: 6, of which 2 were waited for; matrix products, arithmetic and copies ran while one was open for 0% of the time, Pallas kernels for 19%

profile of v9, /device:TPU:0, one launch (start us, length us, event | category | flops | bytes accessed | tf_op | source)
XLA Modules:
  0.0 19.8 jit_solution(17826876362481413999)
XLA Ops:
  0.0 2.7 %first_step.1 = (f32[25,112,128]{2,1,0:T(8,128)S(1)}, f32[25,112,128]{2,1,0:T(8,128)S(1)}, f32[96,128]{1,0:T(8,128)S(1)}, f32[240,128]{1,0:T(8,128)S(1)}, f32[240,128]{1,0:T(8,128)S(1)}, /*index=5*/s32[56]{0:T(128)S(1)}) custom-call(f32[24,96,128]{2,1,0:T(8,128)} %bitcast.2, s32[2,8,128]{2,1,0:T(8,128)} %planes.1, s32[1,1,24]{2,1,0:T(1,128)} %grains.1, ...), custom_call_target="tpu_custom_call" | custom-call | tf_op jit(solution)/shard_map/first_step/pallas_call | solution.py:413
  2.7 3.0 %collective-permute-start = (f32[240,128]{1,0:T(8,128)S(1)}, f32[240,128]{1,0:T(8,128)S(1)}, u32[]{:S(2)}, u32[]{:S(2)}) collective-permute-start(f32[240,128]{1,0:T(8,128)S(1)} %get-tuple-element.17.own.x_up_own), channel_id=1, source_target_pairs={{28,0},{0,4},{4,8},{8,12},{12,16},{16,20},{20,24},{24,28},{29,1},{... | collective-permute-start | bytes 368648 | tf_op jit(solution)/shard_map/ppermute | solution.py:393
  5.7 3.1 %collective-permute-start.1 = (f32[240,128]{1,0:T(8,128)S(1)}, f32[240,128]{1,0:T(8,128)S(1)}, u32[]{:S(2)}, u32[]{:S(2)}) collective-permute-start(f32[240,128]{1,0:T(8,128)S(1)} %get-tuple-element.16.own.x_low_own), channel_id=1, source_target_pairs={{4,0},{8,4},{12,8},{16,12},{20,16},{24,20},{28,24},{0,28},{5,1},{9... | collective-permute-start | bytes 368648 | tf_op jit(solution)/shard_map/ppermute | solution.py:393
  8.8 1.0 %y_rims.1 = (f32[24,128]{1,0:T(8,128)S(1)}, f32[24,128]{1,0:T(8,128)S(1)}) custom-call(f32[25,112,128]{2,1,0:T(8,128)S(1)} %get-tuple-element.18.now, f32[25,112,128]{2,1,0:T(8,128)S(1)} %get-tuple-element.15.stepped.stepped_in, f32[96,128]{1,0:T(8,128)S(1)} %get-tuple-element.19.squares, s32[56]{0:T(128)S(1)} %get-tuple-element.20.lists), custom_call_target="tpu_custom_call" | custom-call | flops 5898240 | bytes 2359296 | tf_op jit(solution)/shard_map/y_rims/pallas_call | solution.py:432
  9.8 0.0 collective-permute-start.2
  9.8 1.7 %collective-permute-start.3 = (f32[24,128]{1,0:T(8,128)S(1)}, f32[24,128]{1,0:T(8,128)S(1)}, u32[]{:S(2)}, u32[]{:S(2)}) collective-permute-start(f32[24,128]{1,0:T(8,128)S(1)} %get-tuple-element.21.y_low_own), channel_id=1, source_target_pairs={{1,0},{2,1},{3,2},{0,3},{5,4},{6,5},{7,6},{4,7},{9,8},{10,9},{11,1... | collective-permute-start | bytes 36872 | tf_op jit(solution)/shard_map/ppermute | solution.py:393
  11.6 1.4 %collective-permute-done.2.refs_0_.y_low = f32[24,128]{1,0:T(8,128)S(1)} collective-permute-done((f32[24,128]{1,0:T(8,128)S(1)}, f32[24,128]{1,0:T(8,128)S(1)}, u32[]{:S(2)}, u32[]{:S(2)}) %collective-permute-start.2) | collective-permute-done | bytes 12320 | tf_op jit(solution)/shard_map/ppermute | solution.py:393
  13.0 0.0 collective-permute-done.3.refs_1_.y_up
  13.0 0.0 collective-permute-done.got.x_low
  13.0 0.2 %collective-permute-done.1.got.x_up = f32[240,128]{1,0:T(8,128)S(1)} collective-permute-done((f32[240,128]{1,0:T(8,128)S(1)}, f32[240,128]{1,0:T(8,128)S(1)}, u32[]{:S(2)}, u32[]{:S(2)}) %collective-permute-start.1) | collective-permute-done | bytes 122912 | tf_op jit(solution)/shard_map/ppermute | solution.py:393
  13.3 1.6 %collective-permute-start.4 = (f32[72,128]{1,0:T(8,128)S(1)}, f32[72,128]{1,0:T(8,128)S(1)}, u32[]{:S(2)}, u32[]{:S(2)}) collective-permute-start(f32[72,128]{1,0:T(8,128)S(1)} %corners_up.1.after), channel_id=1, source_target_pairs={{3,0},{0,1},{1,2},{2,3},{7,4},{4,5},{5,6},{6,7},{11,8},{8,9},{9,10... | collective-permute-start | bytes 110600 | tf_op jit(solution)/shard_map/ppermute | solution.py:393
  14.8 0.2 %collective-permute-start.5 = (f32[72,128]{1,0:T(8,128)S(1)}, f32[72,128]{1,0:T(8,128)S(1)}, u32[]{:S(2)}, u32[]{:S(2)}) collective-permute-start(f32[72,128]{1,0:T(8,128)S(1)} %corners_up.1.after), channel_id=1, source_target_pairs={{1,0},{2,1},{3,2},{0,3},{5,4},{6,5},{7,6},{4,7},{9,8},{10,9},{11,1... | collective-permute-start | bytes 110600 | tf_op jit(solution)/shard_map/ppermute | solution.py:393
  15.1 2.7 %later_steps.1 = (f32[25,112,128]{2,1,0:T(8,128)S(1)}, f32[25,112,128]{2,1,0:T(8,128)S(1)}) custom-call(f32[25,112,128]{2,1,0:T(8,128)S(1)} %get-tuple-element.15.stepped.stepped_in, f32[240,128]{1,0:T(8,128)S(1)} %get-tuple-element.16.own.x_low_own, f32[240,128]{1,0:T(8,128)S(1)} %get-tuple-element.17.own.x_up_own, ...), custom_call_target="tpu_custom_call", output_to_operand_aliasing={{0}: (0, {})} | custom-call | tf_op jit(solution)/shard_map/later_steps/pallas_call | solution.py:465
  17.7 0.0 collective-permute-done.4.from_left
  17.8 0.0 collective-permute-done.5.from_right
  17.8 2.0 %last_corners.1 = (f32[25,112,128]{2,1,0:T(8,128)S(1)}, f32[24,96,128]{2,1,0:T(8,128)}) custom-call(f32[25,112,128]{2,1,0:T(8,128)S(1)} %get-tuple-element.23.last_in, f32[240,128]{1,0:T(8,128)S(1)} %get-tuple-element.16.own.x_low_own, f32[240,128]{1,0:T(8,128)S(1)} %get-tuple-element.17.own.x_up_own, ...), custom_call_target="tpu_custom_call", output_to_operand_aliasing={{0}: (0, {})} | custom-call | tf_op jit(solution)/shard_map/last_corners/pallas_call | solution.py:476
  (2 shorter events, 0.0 us)
Async XLA Ops:
  2.7 10.2 %collective-permute-start = (f32[240,128]{1,0:T(8,128)S(1)}, f32[240,128]{1,0:T(8,128)S(1)}, u32[]{:S(2)}, u32[]{:S(2)}) collective-permute-start(f32[240,128]{1,0:T(8,128)S(1)} %get-tuple-element.17.own.x_up_own), channel_id=1, source_target_pairs={{28,0},{0,4},{4,8},{8,12},{12,16},{16,20},{20,24},{24,28},{29,1},{... | collective-permute-start | bytes 368648 | tf_op jit(solution)/shard_map/ppermute | solution.py:393
  5.7 7.5 %collective-permute-start.1 = (f32[240,128]{1,0:T(8,128)S(1)}, f32[240,128]{1,0:T(8,128)S(1)}, u32[]{:S(2)}, u32[]{:S(2)}) collective-permute-start(f32[240,128]{1,0:T(8,128)S(1)} %get-tuple-element.16.own.x_low_own), channel_id=1, source_target_pairs={{4,0},{8,4},{12,8},{16,12},{20,16},{24,20},{28,24},{0,28},{5,1},{9... | collective-permute-start | bytes 368648 | tf_op jit(solution)/shard_map/ppermute | solution.py:393
  9.8 3.1 %collective-permute-start.2 = (f32[24,128]{1,0:T(8,128)S(1)}, f32[24,128]{1,0:T(8,128)S(1)}, u32[]{:S(2)}, u32[]{:S(2)}) collective-permute-start(f32[24,128]{1,0:T(8,128)S(1)} %get-tuple-element.22.y_up_own), channel_id=1, source_target_pairs={{3,0},{0,1},{1,2},{2,3},{7,4},{4,5},{5,6},{6,7},{11,8},{8,9},{9,10... | collective-permute-start | bytes 36872 | tf_op jit(solution)/shard_map/ppermute | solution.py:393
  9.8 3.1 %collective-permute-start.3 = (f32[24,128]{1,0:T(8,128)S(1)}, f32[24,128]{1,0:T(8,128)S(1)}, u32[]{:S(2)}, u32[]{:S(2)}) collective-permute-start(f32[24,128]{1,0:T(8,128)S(1)} %get-tuple-element.21.y_low_own), channel_id=1, source_target_pairs={{1,0},{2,1},{3,2},{0,3},{5,4},{6,5},{7,6},{4,7},{9,8},{10,9},{11,1... | collective-permute-start | bytes 36872 | tf_op jit(solution)/shard_map/ppermute | solution.py:393
  13.3 4.5 %collective-permute-start.4 = (f32[72,128]{1,0:T(8,128)S(1)}, f32[72,128]{1,0:T(8,128)S(1)}, u32[]{:S(2)}, u32[]{:S(2)}) collective-permute-start(f32[72,128]{1,0:T(8,128)S(1)} %corners_up.1.after), channel_id=1, source_target_pairs={{3,0},{0,1},{1,2},{2,3},{7,4},{4,5},{5,6},{6,7},{11,8},{8,9},{9,10... | collective-permute-start | bytes 110600 | tf_op jit(solution)/shard_map/ppermute | solution.py:393
  14.8 2.9 %collective-permute-start.5 = (f32[72,128]{1,0:T(8,128)S(1)}, f32[72,128]{1,0:T(8,128)S(1)}, u32[]{:S(2)}, u32[]{:S(2)}) collective-permute-start(f32[72,128]{1,0:T(8,128)S(1)} %corners_up.1.after), channel_id=1, source_target_pairs={{1,0},{2,1},{3,2},{0,3},{5,4},{6,5},{7,6},{4,7},{9,8},{10,9},{11,1... | collective-permute-start | bytes 110600 | tf_op jit(solution)/shard_map/ppermute | solution.py:393

commit v10 on v8

--- a/solution.py
+++ b/solution.py
@@ -378,6 +378,10 @@
             _, one = x_rims(own, got, k, depth)
             last[linked[face][k], rims[face], :] = old[k] + total * one
 
+    for face in (0, 1):
+        for slot in linked[face]:
+            pl.when(slot < slots)(functools.partial(send, slot))
+
     for side in range(2):
         c = side * (cols - 1)
         for face, own in ((0, x_low_own), (1, x_up_own)):
@@ -389,7 +393,7 @@
             for k in range(LINKS):
                 moved = jnp.where(lane == c, spin(one, c - place - k), 0.0)
                 last[linked[2 + side][k], rims[face], :] = old[k] + moved
-    for face in range(4):
+    for face in (2, 3):
         for slot in linked[face]:
             pl.when(slot < slots)(functools.partial(send, slot))
     pltpu.make_async_copy(last.at[pl.ds(0, slots), pl.ds(rows, depth * rows), :], result, sent).wait()

time: 19.8 us -> 19.8 us (level)
  no operation moved by 1% of the time
where the time goes in v10:
time: 19.8 us; the launch traced here: 19.5 us
  starting transfers between devices  9.64 us (49%)
  Pallas kernels  8.17 us (41%)
  waiting for transfers between devices  1.65 us (8%)
    ppermute x6, starting transfers between devices, shifted(): lax.ppermute(block, axis, [((i - distance) % size, i) for i in range(size)])  9.64 us
    pallas_call x1, Pallas kernels, on_device(): pl.pallas_call(functools.partial(first_kernel, *sizes), out_shape=[padded...  2.74 us
    pallas_call x1, Pallas kernels, on_device(): pl.pallas_call(functools.partial(later_kernel, *sizes), out_shape=[padded...  2.67 us
    pallas_call x1, Pallas kernels, on_device(): pl.pallas_call(functools.partial(last_kernel, *sizes), out_shape=[padded,...  1.74 us
    ppermute x6, waiting for transfers between devices, shifted(): lax.ppermute(block, axis, [((i - distance) % size, i) for i in range(size)])  1.65 us
    pallas_call x1, Pallas kernels, on_device(): pl.pallas_call(functools.partial(y_kernel, *sizes), out_shape=[y_pack, y_...  0.98 us
  transfers between devices with their start and end apart: 6, of which 2 were waited for; matrix products, arithmetic and copies ran while one was open for 0% of the time, Pallas kernels for 19%

profile of v10, /device:TPU:0, one launch (start us, length us, event | category | flops | bytes accessed | tf_op | source)
XLA Modules:
  0.0 19.5 jit_solution(4306421382551379906)
XLA Ops:
  0.0 2.7 %first_step.1 = (f32[25,112,128]{2,1,0:T(8,128)S(1)}, f32[25,112,128]{2,1,0:T(8,128)S(1)}, f32[96,128]{1,0:T(8,128)S(1)}, f32[240,128]{1,0:T(8,128)S(1)}, f32[240,128]{1,0:T(8,128)S(1)}, /*index=5*/s32[56]{0:T(128)S(1)}) custom-call(f32[24,96,128]{2,1,0:T(8,128)} %bitcast.2, s32[2,8,128]{2,1,0:T(8,128)} %planes.1, s32[1,1,24]{2,1,0:T(1,128)} %grains.1, ...), custom_call_target="tpu_custom_call" | custom-call | tf_op jit(solution)/shard_map/first_step/pallas_call | solution.py:424
  2.7 3.0 %collective-permute-start = (f32[240,128]{1,0:T(8,128)S(1)}, f32[240,128]{1,0:T(8,128)S(1)}, u32[]{:S(2)}, u32[]{:S(2)}) collective-permute-start(f32[240,128]{1,0:T(8,128)S(1)} %get-tuple-element.17.own.x_up_own), channel_id=1, source_target_pairs={{28,0},{0,4},{4,8},{8,12},{12,16},{16,20},{20,24},{24,28},{29,1},{... | collective-permute-start | bytes 368648 | tf_op jit(solution)/shard_map/ppermute | solution.py:404
  5.7 3.1 %collective-permute-start.1 = (f32[240,128]{1,0:T(8,128)S(1)}, f32[240,128]{1,0:T(8,128)S(1)}, u32[]{:S(2)}, u32[]{:S(2)}) collective-permute-start(f32[240,128]{1,0:T(8,128)S(1)} %get-tuple-element.16.own.x_low_own), channel_id=1, source_target_pairs={{4,0},{8,4},{12,8},{16,12},{20,16},{24,20},{28,24},{0,28},{5,1},{9... | collective-permute-start | bytes 368648 | tf_op jit(solution)/shard_map/ppermute | solution.py:404
  8.8 1.0 %y_rims.1 = (f32[24,128]{1,0:T(8,128)S(1)}, f32[24,128]{1,0:T(8,128)S(1)}) custom-call(f32[25,112,128]{2,1,0:T(8,128)S(1)} %get-tuple-element.18.now, f32[25,112,128]{2,1,0:T(8,128)S(1)} %get-tuple-element.15.stepped.stepped_in, f32[96,128]{1,0:T(8,128)S(1)} %get-tuple-element.19.squares, s32[56]{0:T(128)S(1)} %get-tuple-element.20.lists), custom_call_target="tpu_custom_call" | custom-call | flops 5898240 | bytes 2359296 | tf_op jit(solution)/shard_map/y_rims/pallas_call | solution.py:443
  9.8 0.0 collective-permute-start.2
  9.8 1.7 %collective-permute-start.3 = (f32[24,128]{1,0:T(8,128)S(1)}, f32[24,128]{1,0:T(8,128)S(1)}, u32[]{:S(2)}, u32[]{:S(2)}) collective-permute-start(f32[24,128]{1,0:T(8,128)S(1)} %get-tuple-element.21.y_low_own), channel_id=1, source_target_pairs={{1,0},{2,1},{3,2},{0,3},{5,4},{6,5},{7,6},{4,7},{9,8},{10,9},{11,1... | collective-permute-start | bytes 36872 | tf_op jit(solution)/shard_map/ppermute | solution.py:404
  11.6 1.4 %collective-permute-done.2.refs_0_.y_low = f32[24,128]{1,0:T(8,128)S(1)} collective-permute-done((f32[24,128]{1,0:T(8,128)S(1)}, f32[24,128]{1,0:T(8,128)S(1)}, u32[]{:S(2)}, u32[]{:S(2)}) %collective-permute-start.2) | collective-permute-done | bytes 12320 | tf_op jit(solution)/shard_map/ppermute | solution.py:404
  13.0 0.0 collective-permute-done.3.refs_1_.y_up
  13.0 0.0 collective-permute-done.got.x_low
  13.0 0.2 %collective-permute-done.1.got.x_up = f32[240,128]{1,0:T(8,128)S(1)} collective-permute-done((f32[240,128]{1,0:T(8,128)S(1)}, f32[240,128]{1,0:T(8,128)S(1)}, u32[]{:S(2)}, u32[]{:S(2)}) %collective-permute-start.1) | collective-permute-done | bytes 122912 | tf_op jit(solution)/shard_map/ppermute | solution.py:404
  13.3 1.6 %collective-permute-start.4 = (f32[72,128]{1,0:T(8,128)S(1)}, f32[72,128]{1,0:T(8,128)S(1)}, u32[]{:S(2)}, u32[]{:S(2)}) collective-permute-start(f32[72,128]{1,0:T(8,128)S(1)} %corners_up.1.after), channel_id=1, source_target_pairs={{3,0},{0,1},{1,2},{2,3},{7,4},{4,5},{5,6},{6,7},{11,8},{8,9},{9,10... | collective-permute-start | bytes 110600 | tf_op jit(solution)/shard_map/ppermute | solution.py:404
  14.8 0.2 %collective-permute-start.5 = (f32[72,128]{1,0:T(8,128)S(1)}, f32[72,128]{1,0:T(8,128)S(1)}, u32[]{:S(2)}, u32[]{:S(2)}) collective-permute-start(f32[72,128]{1,0:T(8,128)S(1)} %corners_up.1.after), channel_id=1, source_target_pairs={{1,0},{2,1},{3,2},{0,3},{5,4},{6,5},{7,6},{4,7},{9,8},{10,9},{11,1... | collective-permute-start | bytes 110600 | tf_op jit(solution)/shard_map/ppermute | solution.py:404
  15.1 2.7 %later_steps.1 = (f32[25,112,128]{2,1,0:T(8,128)S(1)}, f32[25,112,128]{2,1,0:T(8,128)S(1)}) custom-call(f32[25,112,128]{2,1,0:T(8,128)S(1)} %get-tuple-element.15.stepped.stepped_in, f32[240,128]{1,0:T(8,128)S(1)} %get-tuple-element.16.own.x_low_own, f32[240,128]{1,0:T(8,128)S(1)} %get-tuple-element.17.own.x_up_own, ...), custom_call_target="tpu_custom_call", output_to_operand_aliasing={{0}: (0, {})} | custom-call | tf_op jit(solution)/shard_map/later_steps/pallas_call | solution.py:476
  17.7 0.0 collective-permute-done.4.from_left
  17.8 0.0 collective-permute-done.5.from_right
  17.8 1.7 %last_corners.1 = (f32[25,112,128]{2,1,0:T(8,128)S(1)}, f32[24,96,128]{2,1,0:T(8,128)}) custom-call(f32[25,112,128]{2,1,0:T(8,128)S(1)} %get-tuple-element.23.last_in, f32[240,128]{1,0:T(8,128)S(1)} %get-tuple-element.16.own.x_low_own, f32[240,128]{1,0:T(8,128)S(1)} %get-tuple-element.17.own.x_up_own, ...), custom_call_target="tpu_custom_call", output_to_operand_aliasing={{0}: (0, {})} | custom-call | tf_op jit(solution)/shard_map/last_corners/pallas_call | solution.py:487
  (2 shorter events, 0.0 us)
Async XLA Ops:
  2.7 10.2 %collective-permute-start = (f32[240,128]{1,0:T(8,128)S(1)}, f32[240,128]{1,0:T(8,128)S(1)}, u32[]{:S(2)}, u32[]{:S(2)}) collective-permute-start(f32[240,128]{1,0:T(8,128)S(1)} %get-tuple-element.17.own.x_up_own), channel_id=1, source_target_pairs={{28,0},{0,4},{4,8},{8,12},{12,16},{16,20},{20,24},{24,28},{29,1},{... | collective-permute-start | bytes 368648 | tf_op jit(solution)/shard_map/ppermute | solution.py:404
  5.7 7.5 %collective-permute-start.1 = (f32[240,128]{1,0:T(8,128)S(1)}, f32[240,128]{1,0:T(8,128)S(1)}, u32[]{:S(2)}, u32[]{:S(2)}) collective-permute-start(f32[240,128]{1,0:T(8,128)S(1)} %get-tuple-element.16.own.x_low_own), channel_id=1, source_target_pairs={{4,0},{8,4},{12,8},{16,12},{20,16},{24,20},{28,24},{0,28},{5,1},{9... | collective-permute-start | bytes 368648 | tf_op jit(solution)/shard_map/ppermute | solution.py:404
  9.8 3.1 %collective-permute-start.2 = (f32[24,128]{1,0:T(8,128)S(1)}, f32[24,128]{1,0:T(8,128)S(1)}, u32[]{:S(2)}, u32[]{:S(2)}) collective-permute-start(f32[24,128]{1,0:T(8,128)S(1)} %get-tuple-element.22.y_up_own), channel_id=1, source_target_pairs={{3,0},{0,1},{1,2},{2,3},{7,4},{4,5},{5,6},{6,7},{11,8},{8,9},{9,10... | collective-permute-start | bytes 36872 | tf_op jit(solution)/shard_map/ppermute | solution.py:404
  9.8 3.1 %collective-permute-start.3 = (f32[24,128]{1,0:T(8,128)S(1)}, f32[24,128]{1,0:T(8,128)S(1)}, u32[]{:S(2)}, u32[]{:S(2)}) collective-permute-start(f32[24,128]{1,0:T(8,128)S(1)} %get-tuple-element.21.y_low_own), channel_id=1, source_target_pairs={{1,0},{2,1},{3,2},{0,3},{5,4},{6,5},{7,6},{4,7},{9,8},{10,9},{11,1... | collective-permute-start | bytes 36872 | tf_op jit(solution)/shard_map/ppermute | solution.py:404
  13.3 4.5 %collective-permute-start.4 = (f32[72,128]{1,0:T(8,128)S(1)}, f32[72,128]{1,0:T(8,128)S(1)}, u32[]{:S(2)}, u32[]{:S(2)}) collective-permute-start(f32[72,128]{1,0:T(8,128)S(1)} %corners_up.1.after), channel_id=1, source_target_pairs={{3,0},{0,1},{1,2},{2,3},{7,4},{4,5},{5,6},{6,7},{11,8},{8,9},{9,10... | collective-permute-start | bytes 110600 | tf_op jit(solution)/shard_map/ppermute | solution.py:404
  14.8 2.9 %collective-permute-start.5 = (f32[72,128]{1,0:T(8,128)S(1)}, f32[72,128]{1,0:T(8,128)S(1)}, u32[]{:S(2)}, u32[]{:S(2)}) collective-permute-start(f32[72,128]{1,0:T(8,128)S(1)} %corners_up.1.after), channel_id=1, source_target_pairs={{1,0},{2,1},{3,2},{0,3},{5,4},{6,5},{7,6},{4,7},{9,8},{10,9},{11,1... | collective-permute-start | bytes 110600 | tf_op jit(solution)/shard_map/ppermute | solution.py:404
